TPU v7x, 512 devices: a whole 4x4x16 slice. The times are simulated.
512 devices in a mesh: section: 8 (over x, y_hi), seq: 64 (over z, y_lo, core).
Axes of the slice: x: 4, y: 4 (y_hi: 2, y_lo: 2; y = y_hi * 2 + y_lo), z: 16, core: 2. Of those that a mesh axis runs over, the one named last changes fastest.
Arguments:
- codes: int32 [8, 2, 112, 8192], P('section', None, None, 'seq'), may hold values from -240 to 240
- exponents: int32 [8, 2, 112], P('section'), may hold values from -12 to -7
- sample_ids: int32 [8, 2], replicated, may hold values from 0 to 2, as said below
- buffer_in: bfloat16 [8, 3, 112, 8192], P('section', None, None, 'seq'), may hold values from -16 to 16
- buffer_out: bfloat16 [8, 3, 112, 8192], P('section', None, None, 'seq'), may hold values from -6 to 6
- norm_gain: bfloat16 [8, 8192], P('section', 'seq'), may hold values from 0.25 to 1.75
- w_query: bfloat16 [8, 8192, 8192], P('section', None, 'seq'), may hold values from -0.0625 to 0.0625
- w_keyval: bfloat16 [8, 8192, 2048], P('section', None, 'seq'), may hold values from -0.0625 to 0.0625
- w_output: bfloat16 [8, 8192, 8192], P('section', None, 'seq'), may hold values from -0.5 to 0.5
Outputs:
- next_input: bfloat16 [8, 2, 112, 8192], P('section', None, None, 'seq')
- buffer_in_new: bfloat16 [8, 3, 112, 8192], P('section', None, None, 'seq')
- buffer_out_new: bfloat16 [8, 3, 112, 8192], P('section', None, None, 'seq')
Inputs may be any that keep to these rules, and one draw needn't show every extreme that they name: `sample_ids`: each row names 2 different slots.
All inputs are finite; a program needn't handle non-finite values.
Results may differ from a plain program's by a relative error of at most 0.015.
Values may be sent and summed in bfloat16 or wider, within the bound.
No kernel may reach another device: no remote copies, remote signals or barrier semaphores. Data moves between devices by JAX's collectives and lax.ppermute only.
A program may use at most 64 MiB of HBM per device.

v0:
```python
import math

import jax
import jax.numpy as jnp
from jax import lax
from jax.sharding import PartitionSpec as P

KV_HEADS = 8


rope_base = 500000.0
norm_eps = 1e-05


def shifted(x, axis, by):
    size = lax.axis_size(axis)
    pairs = [(i, i + by) for i in range(size) if 0 <= i + by < size]
    return lax.ppermute(x, axis, pairs)


def rotate(values, positions):
    half_width = values.shape[-1] // 2
    freq_steps = jnp.arange(half_width, dtype=jnp.float32)
    frequency = jnp.exp(freq_steps * (-2.0 * math.log(rope_base) / values.shape[-1]))
    rotation = positions[..., None] * frequency
    cos_part = jnp.cos(rotation)
    sin_part = jnp.sin(rotation)
    first_half = values[..., :half_width]
    second_half = values[..., half_width:]
    return jnp.concatenate(
        [
            first_half * cos_part - second_half * sin_part,
            second_half * cos_part + first_half * sin_part,
        ],
        axis=-1,
    )


def per_device(
    codes, exponents, sample_ids, buffer_in, buffer_out, norm_gain, w_query, w_keyval, w_output
):
    section_index = lax.axis_index("section")
    head_index = lax.axis_index("seq")
    head_count = lax.axis_size("seq")
    slot_ids = lax.dynamic_index_in_dim(sample_ids, section_index, 0, keepdims=False)
    sender_ids = lax.dynamic_index_in_dim(
        sample_ids, jnp.maximum(section_index - 1, 0), 0, keepdims=False
    )
    stored_in = buffer_in[0]
    scales = jnp.exp2(exponents[0].astype(jnp.float32))
    stored = jnp.take(stored_in, slot_ids, axis=0).astype(jnp.float32)
    inputs = (stored + codes[0].astype(jnp.float32) * scales[..., None]).astype(jnp.bfloat16)
    stored_in = stored_in.at[slot_ids].set(inputs)
    seq_total, seq_length, local_width = inputs.shape
    row_count = seq_total * seq_length
    full_width = local_width * head_count
    flat_inputs = inputs.reshape(row_count, local_width)
    query_weight = w_query[0]
    keyval_weight = w_keyval[0]
    head_width = query_weight.shape[1]
    widened = flat_inputs.astype(jnp.float32)
    square_sum = lax.psum(jnp.sum(widened * widened, axis=1), "seq")
    inverse = lax.rsqrt(square_sum / full_width + norm_eps)
    normed = (widened * inverse[:, None] * norm_gain[0].astype(jnp.float32)).astype(jnp.bfloat16)
    piece = lax.all_gather(normed, "seq", axis=1, tiled=True)
    query_sum = jnp.dot(piece, query_weight, preferred_element_type=jnp.float32)
    keyval_sum = jnp.dot(piece, keyval_weight, preferred_element_type=jnp.float32)
    positions = (jnp.arange(row_count) % seq_length).astype(jnp.float32)
    queries = rotate(query_sum, positions).astype(jnp.bfloat16)
    keyval = lax.all_gather(keyval_sum.astype(jnp.bfloat16), "seq", axis=1, tiled=True)
    kv_width = keyval.shape[1] // 2
    kv_group = head_index // (head_count // KV_HEADS)
    key_rows = lax.dynamic_slice_in_dim(keyval, kv_group * head_width, head_width, 1)
    key_rows = rotate(key_rows.astype(jnp.float32), positions).astype(jnp.bfloat16)
    value_rows = lax.dynamic_slice_in_dim(keyval, kv_width + kv_group * head_width, head_width, 1)
    query_blocks = queries.reshape(seq_total, seq_length, head_width)
    key_blocks = key_rows.reshape(seq_total, seq_length, head_width)
    value_blocks = value_rows.reshape(seq_total, seq_length, head_width)
    scores = jnp.einsum(
        "sqd,skd->sqk", query_blocks, key_blocks, preferred_element_type=jnp.float32
    ) / math.sqrt(head_width)
    causal = jnp.arange(seq_length)[:, None] >= jnp.arange(seq_length)[None, :]
    scores = jnp.where(causal[None], scores, -1e30)
    row_peak = jnp.max(scores, axis=-1, keepdims=True)
    raised = jnp.exp(scores - row_peak)
    weights = (raised / jnp.sum(raised, axis=-1, keepdims=True)).astype(jnp.bfloat16)
    context = jnp.einsum("sqk,skd->sqd", weights, value_blocks, preferred_element_type=jnp.float32)
    context = context.astype(jnp.bfloat16).reshape(row_count, head_width)
    output_weight = w_output[0]
    mixed_rows = jnp.dot(
        lax.all_gather(context, "seq", axis=1, tiled=True),
        output_weight,
        preferred_element_type=jnp.float32,
    )
    updated = flat_inputs.astype(jnp.float32) + mixed_rows
    stored_out = (
        jnp.take(buffer_out[0], slot_ids, axis=0)
        .astype(jnp.float32)
        .reshape(row_count, local_width)
    )
    message = (updated - stored_out).astype(jnp.bfloat16)
    refreshed = (
        (stored_out + message.astype(jnp.float32))
        .astype(jnp.bfloat16)
        .reshape(seq_total, seq_length, local_width)
    )
    new_out = buffer_out[0].at[slot_ids].set(refreshed)
    arrived = shifted(message, "section", 1)
    arrived = arrived.reshape(seq_total, seq_length, local_width)
    following = (
        jnp.take(stored_in, sender_ids, axis=0).astype(jnp.float32) + arrived.astype(jnp.float32)
    ).astype(jnp.bfloat16)
    stored_in = stored_in.at[sender_ids].set(following)
    return (following[None], stored_in[None], new_out[None])


def solution(mesh):
    return jax.shard_map(
        per_device,
        mesh=mesh,
        in_specs=(
            P("section", None, None, "seq"),
            P("section", None, None),
            P(),
            P("section", None, None, "seq"),
            P("section", None, None, "seq"),
            P("section", "seq"),
            P("section", None, "seq"),
            P("section", None, "seq"),
            P("section", None, "seq"),
        ),
        out_specs=(
            P("section", None, None, "seq"),
            P("section", None, None, "seq"),
            P("section", None, None, "seq"),
        ),
        check_vma=False,
    )
```

profile of v0, /device:TPU:6, one launch (start us, length us, event | category | flops | bytes accessed | tf_op | source)
XLA Modules:
  0.0 468.0 jit_solution(7466414931775466283)
XLA Ops:
  7.2 0.0 copy-start
  7.2 0.0 all-gather.3.cloned.1.call-start
  7.2 1.0 copy.24
  8.3 0.9 copy.25
  9.1 1.0 dynamic-slice_reduce_fusion
  10.1 0.7 bitcast_convert_fusion
  10.8 0.7 exponential_bitcast_fusion
  11.5 0.6 gather_fusion
  12.1 1.1 multiply_reduce_fusion
  13.1 0.1 reduce_sum.21
  13.2 114.6 %psum.7 = f32[224]{0:T(256)S(1)} all-reduce(f32[224]{0:T(256)S(1)} %reduce_sum.21), channel_id=1, replica_groups=mesh['section'=8,'seq'=64] {'seq'}, use_global_device_ids=true, to_apply=%region_2.4 | all-reduce | flops 224 | bytes 1792 | tf_op jit(solution)/shard_map/psum | solution.py:62
  127.8 0.7 fusion.37
  128.6 0.0 all-gather.3.cloned.1.call-update
  128.6 0.0 all-gather.5.cloned.1.call-start
  128.7 122.3 %all-gather.3.cloned.1.call-done = bf16[224,8192]{1,0:T(8,128)(2,1)} async-done(((bf16[224,128]{1,0:T(8,128)(2,1)}), bf16[224,8192]{1,0:T(8,128)(2,1)}) %all-gather.3.cloned.1.call-update) | async-done | bytes 3670032 | tf_op jit(solution)/shard_map/all_gather | solution.py:65
  251.0 3.4 convolution_convert_fusion.1
  254.4 64.0 %all_gather.10 = bf16[224,2048]{0,1:T(8,128)(2,1)S(1)} all-gather(bf16[224,32]{0,1:T(8,128)(2,1)S(1)} %convolution_convert_fusion.1), channel_id=1, replica_groups=mesh['section'=8,'seq'=64] {'seq'}, dimensions={1}, use_global_device_ids=true | all-gather | bytes 931840 | tf_op jit(solution)/shard_map/all_gather | solution.py:70
  318.4 0.1 copy.18
  318.5 3.9 fusion.3
  322.4 0.5 fusion.32
  322.9 0.3 fusion.61
  323.2 0.3 fusion.13
  323.5 0.1 copy.15
  323.6 0.9 convolution_convert_fusion
  324.5 0.0 all-gather.5.cloned.1.call-update
  324.5 0.6 scatter_fusion
  325.2 0.6 gather_fusion.2
  325.8 0.1 broadcast_select_fusion
  325.8 122.4 %all-gather.5.cloned.1.call-done = bf16[224,8192]{1,0:T(8,128)(2,1)} async-done(((bf16[224,128]{1,0:T(8,128)(2,1)}), bf16[224,8192]{1,0:T(8,128)(2,1)}) %all-gather.5.cloned.1.call-update) | async-done | bytes 3670032 | tf_op jit(solution)/shard_map/all_gather | solution.py:91
  448.2 0.0 copy-done
  448.2 3.1 fusion.26
  451.3 4.4 collective-permute-start
  455.8 0.6 gather_fusion.1
  456.3 0.6 scatter_fusion.2
  457.0 0.0 copy-start.2
  457.0 2.8 collective-permute-done
  459.8 0.1 fusion.35
  459.9 0.0 copy-start.3
  459.9 0.6 scatter_fusion.1
  460.6 0.0 copy-start.1
  460.6 0.0 copy-done.2
  460.6 0.0 copy-done.3
  460.6 0.6 copy-done.1
  (12 shorter events, 0.1 us)
Async XLA Ops:
  7.2 441.0 %copy-start = (bf16[1,8192,128]{2,1,0:T(8,128)(2,1)S(1)}, bf16[1,8192,128]{2,1,0:T(8,128)(2,1)}, u32[]{:S(2)}) copy-start(bf16[1,8192,128]{2,1,0:T(8,128)(2,1)} %param.19) | copy-start | bytes 6291460
  7.2 243.8 %all-gather.3.cloned.1.call-start = ((), (), s32[]{:S(2)}) async-start(), calls=%async_computation | async-start | bytes 3727360 | tf_op jit(solution)/shard_map/all_gather | solution.py:65
  128.6 319.6 %all-gather.5.cloned.1.call-start = ((), (), s32[]{:S(2)}) async-start(), calls=%async_computation.1 | async-start | bytes 3727360 | tf_op jit(solution)/shard_map/all_gather | solution.py:91
  451.3 8.5 %collective-permute-start = (bf16[224,128]{1,0:T(8,128)(2,1)S(1)}, bf16[224,128]{1,0:T(8,128)(2,1)S(1)}, u32[]{:S(2)}, u32[]{:S(2)}) collective-permute-start(bf16[224,128]{1,0:T(8,128)(2,1)S(1)} %get-tuple-element.17), channel_id=1, source_target_pairs={{0,64},{64,128},{128,192},{192,256},{256,320},{320,384},{384,448},... | collective-permute-start | bytes 172040 | tf_op jit(solution)/shard_map/ppermute | solution.py:18
  457.0 3.6 copy-start.2
  459.9 0.7 copy-start.3
  460.6 0.6 copy-start.1
Sparse Core Ops, SparseCore 0:
  128.7 122.2 all-gather.2
  324.6 123.4 all-gather.4
where the time goes:
time: 468 us
  waiting for transfers between devices  247 us (53%)
  blocking collectives  179 us (38%)
  between operations  14.3 us (3%)
  matrix products  11.8 us (3%)
  local copies, waits for them, and re-layouts  7.38 us (2%)
    all_gather x1, waiting for transfers between devices, per_device(): lax.all_gather(context, 'seq', axis=1, tiled=True)  122 us
    all_gather x1, waiting for transfers between devices, per_device(): piece = lax.all_gather(normed, 'seq', axis=1, tiled=True)  122 us
    psum x1, blocking collectives, per_device(): square_sum = lax.psum(jnp.sum(widened * widened, axis=1), 'seq')  115 us
    all_gather x1, blocking collectives, per_device(): lax.all_gather(keyval_sum.astype(jnp.bfloat16), 'seq', axis=1, tiled=True)  64 us
  transfers between devices with their start and end apart: 3, of which 3 were waited for; matrix products, arithmetic and copies ran while one was open for 1% of the time, Pallas kernels for 0%

commit v1 on v0

v1 whole, which is shorter than its diff:
```python
import functools
import math

import jax
import jax.numpy as jnp
import numpy as np
from jax import lax
from jax.experimental import pallas as pl
from jax.experimental.pallas import tpu as pltpu
from jax.sharding import Mesh
from jax.sharding import PartitionSpec as P

SEQS, LEN, SLOTS, HEAD, KV_HEADS = 2, 112, 3, 128, 8
ROWS = SEQS * LEN
PAY = ROWS + 16
ZN, YN, CN = 16, 2, 2
PIECES = 4
LANES = ("z", "y", "core")
rope_base = 500000.0
norm_eps = 1e-05

VMEM = pl.BlockSpec(memory_space=pltpu.VMEM)
SMEM = pl.BlockSpec(memory_space=pltpu.SMEM)
PARAMS = pltpu.CompilerParams(vmem_limit_bytes=40 * 1024 * 1024)
NT = (((1,), (1,)), ((), ()))


def rope_tables():
    half = HEAD // 2
    frequency = np.exp(np.arange(half) * (-2.0 * math.log(rope_base) / HEAD))
    positions = np.arange(ROWS) % LEN
    angle = positions[:, None] * frequency[None, :]
    return np.cos(angle).astype(np.float32), np.sin(angle).astype(np.float32)


def call(kernel, outs, n_in, flops, bytes_accessed, smem=(), scratch=()):
    return pl.pallas_call(
        kernel,
        out_shape=outs,
        in_specs=[SMEM if i in smem else VMEM for i in range(n_in)],
        out_specs=jax.tree.map(lambda _: VMEM, outs),
        scratch_shapes=list(scratch),
        compiler_params=PARAMS,
        cost_estimate=pl.CostEstimate(
            flops=flops, bytes_accessed=bytes_accessed, transcendentals=0
        ),
    )


def shape(dims, dtype=jnp.bfloat16):
    return jax.ShapeDtypeStruct(dims, dtype)


def prepare(
    ids, codes, exponents, buffer_in, gain, query, keyval, output,
    packed, packed_out, pay, inputs_out,
    codes_v, exponents_v, stored_v, gain_v, keyval_v, half_v, keyval_half_v, sems, half_sems,
):
    section = lax.axis_index("section")
    far = lax.axis_index("y") ^ 1
    copies = [
        pltpu.make_async_copy(exponents, exponents_v, sems.at[0]),
        pltpu.make_async_copy(gain, gain_v, sems.at[1]),
        pltpu.make_async_copy(codes, codes_v, sems.at[2]),
        pltpu.make_async_copy(buffer_in.at[0, ids[0, section]], stored_v.at[0], sems.at[3]),
        pltpu.make_async_copy(buffer_in.at[0, ids[1, section]], stored_v.at[1], sems.at[4]),
        pltpu.make_async_copy(keyval, keyval_v, sems.at[5]),
    ]
    for item in copies:
        item.start()

    step = ZN // PIECES
    loads, stores = [], []
    for i in range(2 * PIECES):
        source, target = (query, packed) if i < PIECES else (output, packed_out)
        part = pl.ds(i % PIECES * step, step)
        loads.append(
            pltpu.make_async_copy(source.at[part, far], half_v.at[i], half_sems.at[0, i])
        )
        stores.append(
            pltpu.make_async_copy(half_v.at[i], target.at[part], half_sems.at[1, i])
        )
        loads[-1].start()
    for item in copies[:5]:
        item.wait()
    eye = lax.broadcasted_iota(jnp.int32, (LEN, LEN), 0) == lax.broadcasted_iota(
        jnp.int32, (LEN, LEN), 1
    )
    gains = gain_v[...].astype(jnp.float32)
    sums = []
    for s in range(SEQS):
        steps = jnp.exp2(exponents_v[0, s : s + 1, :].astype(jnp.float32))
        diagonal = jnp.where(eye, steps, 0.0).astype(jnp.bfloat16)
        scales = jnp.dot(
            diagonal, jnp.ones((LEN, HEAD), jnp.bfloat16), preferred_element_type=jnp.float32
        )
        stored = stored_v[s].astype(jnp.float32)
        inputs = (stored + codes_v[0, s].astype(jnp.float32) * scales).astype(jnp.bfloat16)
        inputs_out[s] = inputs
        widened = inputs.astype(jnp.float32)
        pay[s * LEN : (s + 1) * LEN, :] = (widened * gains).astype(jnp.bfloat16)
        squares = widened * widened
        high = squares.astype(jnp.bfloat16)
        low = (squares - high.astype(jnp.float32)).astype(jnp.bfloat16)
        ones = jnp.ones((16, HEAD), jnp.bfloat16)
        total = lax.dot_general(ones, high, NT, preferred_element_type=jnp.float32)
        total += lax.dot_general(ones, low, NT, preferred_element_type=jnp.float32)
        sums.append(jnp.concatenate([total, jnp.zeros((16, HEAD - LEN), jnp.float32)], axis=1))
    row = lax.broadcasted_iota(jnp.int32, (16, HEAD), 0)
    value = jnp.where(row % 2 == 0, sums[0], sums[1])
    first = value.astype(jnp.bfloat16).astype(jnp.float32)
    second = value - first
    tail = jnp.where(row < 2, first, jnp.where(row < 4, second, 0.0))
    pay[ROWS:PAY, :] = tail.astype(jnp.bfloat16)

    copies[5].wait()
    kv_width = keyval.shape[1]
    per_row = CN * HEAD // kv_width
    for z in range(ZN):
        for core in range(CN):
            i = z * CN + core
            start = (i % per_row) * kv_width
            keyval_half_v[i // per_row, start : start + kv_width, :] = keyval_v[
                0, :, head_rows(z, far, core)
            ]
    last = pltpu.make_async_copy(
        keyval_half_v, packed.at[pl.ds(ZN, keyval_half_v.shape[0])], sems.at[6]
    )
    last.start()
    for load, store in zip(loads, stores):
        load.wait()
        store.start()
    last.wait()
    for store in stores:
        store.wait()


def head_rows(z, y, core):
    head = z * (YN * CN) + y * CN + core
    return pl.ds(pl.multiple_of(head * HEAD, HEAD), HEAD)


def half_rows(z, core):
    return pl.ds(pl.multiple_of((z * CN + core) * HEAD, HEAD), HEAD)


def keyval_kernel(here, there, weight, received, out, sums_out):
    y, core = lax.axis_index("y"), lax.axis_index("core")
    kv_width = weight.shape[1]
    sums = jnp.sum(here[:, ROWS:PAY, :].astype(jnp.float32), axis=0)
    sums += jnp.sum(there[:, ROWS:PAY, :].astype(jnp.float32), axis=0)
    sums = jnp.concatenate(
        [sums[s : s + 1, :LEN] + sums[SEQS + s : SEQS + s + 1, :LEN] for s in range(SEQS)], axis=1
    )
    high = sums.astype(jnp.bfloat16).astype(jnp.float32)
    row = lax.broadcasted_iota(jnp.int32, (PAY - ROWS, ROWS), 0)
    tail = jnp.where(row == 0, high, jnp.where(row == 1, sums - high, 0.0))
    sums_out[...] = tail.astype(jnp.bfloat16)
    acc = jnp.zeros((2 * kv_width, ROWS), jnp.float32)
    for z in range(ZN):
        block = jnp.concatenate([here[z, :ROWS, :], there[z, :ROWS, :]], axis=1)
        parts = []
        for side in (core, core ^ 1):
            start = ZN * CN * HEAD + (z * CN + side) * kv_width
            mine = weight[0, :, head_rows(z, y, side)]
            other = received[pl.ds(pl.multiple_of(start, kv_width), kv_width), :]
            parts.append(jnp.concatenate([mine, other], axis=0))
        part = jnp.concatenate(parts, axis=1)
        acc += lax.dot_general(part, block, NT, preferred_element_type=jnp.float32)
    out[...] = acc.astype(jnp.bfloat16)


def both_partials(here, there, weight, received):
    y, core = lax.axis_index("y"), lax.axis_index("core")
    acc = jnp.zeros((ROWS, 2 * HEAD), jnp.float32)
    for z in range(ZN):
        block = jnp.concatenate([here[z, :ROWS, :], there[z, :ROWS, :]], axis=1)
        parts = []
        for side in (core, core ^ 1):
            mine = weight[0, head_rows(z, y, side), :]
            other = received[half_rows(z, side), :]
            parts.append(jnp.concatenate([mine, other], axis=1))
        part = jnp.concatenate(parts, axis=0)
        acc += jnp.dot(block, part, preferred_element_type=jnp.float32)
    return acc


def query_kernel(here, there, weight, received, mine_out, other_out):
    acc = both_partials(here, there, weight, received)
    mine_out[...] = acc[:, :HEAD]
    other_out[...] = acc[:, HEAD:].astype(jnp.bfloat16)


def sum_kernel(near, far, cos_t, sin_t, out, factors_out):
    z_odd, y, core = lax.axis_index("z") % 2, lax.axis_index("y"), lax.axis_index("core")
    width = (near.shape[0] - (PAY - ROWS)) // 4
    tail = near[4 * width :, :].astype(jnp.float32) + far[4 * width :, :].astype(jnp.float32)
    square_sum = tail[0:1, :] + tail[1:2, :]
    inverse = lax.rsqrt(square_sum / (ZN * YN * CN * HEAD) + norm_eps)
    factors = jnp.broadcast_to(inverse, (width, ROWS))
    factors_out[...] = jnp.broadcast_to(inverse, (HEAD, ROWS)).T

    def piece(kind, which):
        plane = z_odd ^ kind
        a = near[pl.ds(pl.multiple_of((plane * 2 + (which ^ y)) * width, width), width), :]
        b = far[pl.ds(pl.multiple_of((plane * 2 + 1 - (which ^ y)) * width, width), width), :]
        return ((a.astype(jnp.float32) + b.astype(jnp.float32)) * factors).astype(jnp.bfloat16)

    first, second = piece(0, 0).astype(jnp.float32), piece(0, 1).astype(jnp.float32)
    rows = pl.ds(pl.multiple_of(core * width, width), width)
    c, s = cos_t[rows, :], sin_t[rows, :]
    out[0] = (first * c - second * s).astype(jnp.bfloat16)
    out[1] = (second * c + first * s).astype(jnp.bfloat16)
    out[2] = piece(1, 0)
    out[3] = piece(1, 1)


def rope_kernel(mine, other, factors, cos, sin, out):
    acc = (mine[...] + other[...].astype(jnp.float32)) * factors[...]
    first, second = acc[:, : HEAD // 2], acc[:, HEAD // 2 :]
    c, s = cos[...], sin[...]
    out[...] = jnp.concatenate(
        [first * c - second * s, second * c + first * s], axis=1
    ).astype(jnp.bfloat16)


def attention_kernel(query, own, sibling, out):
    core = lax.axis_index("core")
    keys_values = []
    for kind in range(2):
        parts = []
        for which in range(2):
            a, b = own[2 * kind + which], sibling[2 * kind + which]
            parts += [jnp.where(core == 0, a, b), jnp.where(core == 0, b, a)]
        keys_values.append(jnp.concatenate(parts, axis=0))
    keys, values = keys_values
    scores = jnp.dot(query[...], keys, preferred_element_type=jnp.float32) / math.sqrt(HEAD)
    row = lax.broadcasted_iota(jnp.int32, (ROWS, ROWS), 0)
    column = lax.broadcasted_iota(jnp.int32, (ROWS, ROWS), 1)
    allowed = (column <= row) & ((row < LEN) | (column >= LEN))
    scores = jnp.where(allowed, scores, -1e30)
    peak = jnp.max(scores, axis=-1, keepdims=True)
    raised = jnp.exp(scores - peak)
    weights = (raised / jnp.sum(raised, axis=-1, keepdims=True)).astype(jnp.bfloat16)
    context = lax.dot_general(weights, values, NT, preferred_element_type=jnp.float32)
    out[...] = context.astype(jnp.bfloat16)


def output_kernel(here, there, weight, received, mine_out, other_out):
    acc = both_partials(here, there, weight, received)
    mine_out[...] = acc[:, :HEAD]
    other_out[...] = acc[:, HEAD:].astype(jnp.bfloat16)


def message_kernel(ids, mine, other, inputs, buffer_out, message_out):
    section = lax.axis_index("section")
    for s in range(SEQS):
        rows = slice(s * LEN, (s + 1) * LEN)
        stored = buffer_out[0, ids[s, section]].astype(jnp.float32)
        mixed = mine[rows, :] + other[rows, :].astype(jnp.float32)
        message_out[s] = (inputs[s].astype(jnp.float32) + mixed - stored).astype(jnp.bfloat16)


def refresh_kernel(ids, message, buffer_out, new_out):
    section = lax.axis_index("section")
    new_out[...] = buffer_out[...]
    for s in range(SEQS):
        slot = ids[s, section]
        stored = buffer_out[0, slot].astype(jnp.float32)
        new_out[0, slot] = (stored + message[s].astype(jnp.float32)).astype(jnp.bfloat16)


def finish_kernel(ids, buffer_in, inputs, arrived, following_out, stored_out):
    section = lax.axis_index("section")
    before = jnp.maximum(section - 1, 0)
    stored_out[...] = buffer_in[...]
    for s in range(SEQS):
        stored_out[0, ids[s, section]] = inputs[s]
    results = []
    for s in range(SEQS):
        current = stored_out[0, ids[s, before]].astype(jnp.float32)
        results.append((current + arrived[s].astype(jnp.float32)).astype(jnp.bfloat16))
    for s in range(SEQS):
        following_out[0, s] = results[s]
        stored_out[0, ids[s, before]] = results[s]


def lane(z, y, core):
    return (z % ZN) * (YN * CN) + y * CN + core


def permute(x, target):
    pairs = [
        (lane(z, y, c), lane(*target(z, y, c)))
        for z in range(ZN)
        for y in range(YN)
        for c in range(CN)
    ]
    return lax.ppermute(x, LANES, pairs)


def swap_core(x):
    return permute(x, lambda z, y, c: (z, y, c ^ 1))


def swap_y(x):
    return permute(x, lambda z, y, c: (z, y ^ 1, c))


def after(x, earlier):
    return lax.optimization_barrier((x, earlier))[0]


def gather_z(x):
    return lax.all_gather(x, "z", axis=0)


def per_device(
    codes, exponents, sample_ids, buffer_in, buffer_out, norm_gain, w_query, w_keyval, w_output
):
    cos, sin = rope_tables()
    sample_ids = sample_ids.T
    kv_width = w_keyval.shape[2]
    half = ZN * CN * HEAD
    w_keyval = jnp.swapaxes(w_keyval, 1, 2)
    partial_flops = 2 * ROWS * half * 256
    wide = shape((ROWS, HEAD), jnp.float32)

    by_half = (ZN, YN, CN * HEAD, HEAD)
    any_spec = pl.BlockSpec(memory_space=pl.ANY)
    bf16, int32 = jnp.bfloat16, jnp.int32
    packed, packed_out, pay, inputs = pl.pallas_call(
        prepare,
        out_shape=(
            shape((ZN + ZN * kv_width // HEAD, CN * HEAD, HEAD)),
            shape((ZN, CN * HEAD, HEAD)),
            shape((PAY, HEAD)),
            shape((SEQS, LEN, HEAD)),
        ),
        in_specs=[SMEM] + [any_spec] * 7,
        out_specs=(any_spec, any_spec, VMEM, VMEM),
        scratch_shapes=[
            pltpu.VMEM(codes.shape, int32),
            pltpu.VMEM(exponents.shape, int32),
            pltpu.VMEM((SEQS, LEN, HEAD), bf16),
            pltpu.VMEM(norm_gain.shape, bf16),
            pltpu.VMEM(w_keyval.shape, bf16),
            pltpu.VMEM((2 * PIECES, ZN // PIECES, CN * HEAD, HEAD), bf16),
            pltpu.VMEM((ZN * kv_width // HEAD, CN * HEAD, HEAD), bf16),
            pltpu.SemaphoreType.DMA((7,)),
            pltpu.SemaphoreType.DMA((2, 2 * PIECES)),
        ],
        cost_estimate=pl.CostEstimate(flops=10**7, bytes_accessed=4 * 10**6, transcendentals=0),
    )(
        sample_ids, codes, exponents, buffer_in, norm_gain,
        w_query.reshape(by_half), w_keyval, w_output.reshape(by_half),
    )
    received = swap_y(packed).reshape(-1, HEAD)
    received_out = swap_y(packed_out).reshape(half, HEAD)
    here = gather_z(pay)
    there = swap_core(here)

    keyval, sums = call(
        keyval_kernel,
        (shape((2 * kv_width, ROWS)), shape((PAY - ROWS, ROWS))),
        4,
        partial_flops,
        5 * 10**6,
    )(here, there, w_keyval, received)
    even = permute(keyval, lambda z, y, c: (2 * z if z < 8 else 2 * (z - 8) + 1, y, c))
    odd = permute(keyval, lambda z, y, c: (2 * z + 1 if z < 8 else 2 * (z - 8), y, c))
    mine, other = call(
        query_kernel, (wide, shape((ROWS, HEAD))), 4, partial_flops, 6 * 10**6
    )(here, there, w_query, after(received, keyval))
    other = swap_y(other)
    near = after(jnp.concatenate([even, odd, sums]), mine)
    far = swap_y(near)
    own, factors = call(
        sum_kernel, (shape((4, kv_width, ROWS)), wide), 4, 10**6, 10**6
    )(after(near, received_out), far, cos.T.copy(), sin.T.copy())
    sibling = swap_core(own)
    queries = call(rope_kernel, shape((ROWS, HEAD)), 5, 10**6, 10**6)(
        mine, other, factors, cos, sin
    )
    context = call(attention_kernel, shape((ROWS, HEAD)), 3, 4 * ROWS * ROWS * HEAD, 10**6)(
        queries, own, sibling
    )

    here = gather_z(context)
    there = swap_core(here)
    mine, other = call(
        output_kernel, (wide, shape((ROWS, HEAD))), 4, partial_flops, 6 * 10**6
    )(here, there, w_output, received_out)
    other = swap_y(other)
    message = call(
        message_kernel, shape((SEQS, LEN, HEAD)), 5, 10**6, 10**6, smem=(0,)
    )(sample_ids, mine, other, inputs, buffer_out)

    sections = lax.axis_size("section")
    arrived = lax.ppermute(message, "section", [(i, i + 1) for i in range(sections - 1)])
    following, new_in = call(
        finish_kernel,
        (shape((1, SEQS, LEN, HEAD)), shape(buffer_in.shape)),
        4,
        10**6,
        10**6,
        smem=(0,),
    )(sample_ids, buffer_in, inputs, arrived)
    new_out = call(refresh_kernel, shape(buffer_out.shape), 3, 10**6, 10**6, smem=(0,))(
        sample_ids, message, buffer_out
    )
    return following, new_in, new_out


def solution(mesh):
    sections = mesh.shape["section"]
    fine = Mesh(mesh.devices.reshape(sections, ZN, YN, CN), ("section",) + LANES)
    return jax.shard_map(
        per_device,
        mesh=fine,
        in_specs=(
            P("section", None, None, LANES),
            P("section", None, None),
            P(),
            P("section", None, None, LANES),
            P("section", None, None, LANES),
            P("section", LANES),
            P("section", None, LANES),
            P("section", None, LANES),
            P("section", None, LANES),
        ),
        out_specs=(
            P("section", None, None, LANES),
            P("section", None, None, LANES),
            P("section", None, None, LANES),
        ),
        check_vma=False,
    )
```

time: 468 us -> 140 us (0.30)
  waiting for transfers between devices: 247 us -> 26.8 us
  blocking collectives: 179 us -> 73.6 us
  starting transfers between devices: 4.48 us -> 27.6 us
  between operations: 14.3 us -> 0.88 us
  matrix products: 11.8 us -> 0 us
  Pallas kernels: 0 us -> 10.8 us
  local copies, waits for them, and re-layouts: 7.38 us -> 0.06 us
    all_gather x2 -> x0, waiting for transfers between devices: 245 us -> none  [the longest x1 122 us: per_device(): lax.all_gather(context, 'seq', axis=1, tiled=True)]
    psum x1 -> x0, blocking collectives: 115 us -> none  [per_device(): square_sum = lax.psum(jnp.sum(widened * widened, axis=1), 'seq')]
    ppermute x1 -> x11, waiting for transfers between devices: 2.85 us -> 26.8 us  [the longest x10 24.4 us: permute(): return lax.ppermute(x, LANES, pairs)]
    ppermute x1 -> x11, starting transfers between devices: 4.4 us -> 27.6 us  [the longest x10 22.8 us: permute(): return lax.ppermute(x, LANES, pairs)]
    dot_general x5 -> x0, matrix products: 11.5 us -> none  [the longest x1 3.86 us: per_device(): query_sum = jnp.dot(piece, query_weight, preferred_element_type=jnp.float32)]
    pallas_call x0 -> x10, Pallas kernels: none -> 10.8 us  [the longest x1 4.95 us: per_device(): pl.pallas_call(prepare, out_shape=(shape((ZN + ZN * kv_width // HEAD, CN...]
    all_gather x1 -> x2, blocking collectives: 64 us -> 73.6 us  [gather_z(): return lax.all_gather(x, 'z', axis=0)]
  transfers between devices with their start and end apart: 3 -> 11, of which waited for: 3 -> 8; matrix products, arithmetic and copies ran while one was open for 1% -> 0% of each run, Pallas kernels for 0% -> 2%
where the time goes in v1:
time: 140 us
  blocking collectives  73.6 us (53%)
  starting transfers between devices  27.6 us (20%)
  waiting for transfers between devices  26.8 us (19%)
  Pallas kernels  10.8 us (8%)
    all_gather x2, blocking collectives, gather_z(): return lax.all_gather(x, 'z', axis=0)  73.6 us
    ppermute x10, waiting for transfers between devices, permute(): return lax.ppermute(x, LANES, pairs)  24.4 us
    ppermute x10, starting transfers between devices, permute(): return lax.ppermute(x, LANES, pairs)  22.8 us
    pallas_call x1, Pallas kernels, per_device(): pl.pallas_call(prepare, out_shape=(shape((ZN + ZN * kv_width // HEAD, CN...  4.95 us
    ppermute x1, starting transfers between devices, per_device(): lax.ppermute(message, 'section', [(i, i + 1) for i in range(sections - 1)])  4.81 us
  transfers between devices with their start and end apart: 11, of which 8 were waited for; matrix products, arithmetic and copies ran while one was open for 0% of the time, Pallas kernels for 2%

profile of v1, /device:TPU:6, one launch (start us, length us, event | category | flops | bytes accessed | tf_op | source)
XLA Modules:
  0.0 139.7 jit_solution(8753302344668596901)
XLA Ops:
  0.6 0.0 copy-start.2
  0.6 5.0 %shard_map.148 = (bf16[20,256,128]{2,1,0:T(8,128)(2,1)}, bf16[16,256,128]{2,1,0:T(8,128)(2,1)}, bf16[240,128]{1,0:T(8,128)(2,1)}, bf16[2,112,128]{2,1,0:T(8,128)(2,1)}) custom-call(s32[2,8]{1,0:T(2,128)} %bitcast.20, s32[1,2,112,128]{3,2,1,0:T(8,128)} %codes.1, s32[1,2,112]{2,1,0:T(2,128)} %exponents.1, bf16[1,3,112,128]{3,2,1,0:T(8,128)(2,1)} %buffer_in.3, ...), custom_call_target="tpu_custom_call" | custom-call | flops 10000000 | bytes 4000000 | tf_op jit(solution)/shard_map/pallas_call | solution.py:332
  5.6 3.5 %collective-permute-start.1 = (bf16[20,256,128]{2,1,0:T(8,128)(2,1)}, bf16[20,256,128]{2,1,0:T(8,128)(2,1)S(1)}, u32[]{:S(2)}, u32[]{:S(2)}) collective-permute-start(bf16[20,256,128]{2,1,0:T(8,128)(2,1)} %get-tuple-element.22), channel_id=1, source_target_pairs={{0,2},{1,3},{2,0},{3,1},{4,6},{5,7},{6,4},{7,5},{8,10},{9,11},{10,... | collective-permute-start | bytes 3932168 | tf_op jit(solution)/shard_map/ppermute | solution.py:299
  9.1 42.1 %all-gather = bf16[3840,128]{1,0:T(8,128)(2,1)S(1)} all-gather(bf16[240,128]{1,0:T(8,128)(2,1)} %get-tuple-element.21), channel_id=2, replica_groups=mesh['section'=8,'z'=16,'y'=2,'core'=2] {'z'}, dimensions={0}, use_global_device_ids=true | all-gather | bytes 1044480 | tf_op jit(solution)/shard_map/all_gather | solution.py:315
  51.2 2.0 %collective-permute-start = (bf16[16,240,128]{2,1,0:T(8,128)(2,1)S(1)}, bf16[16,240,128]{2,1,0:T(8,128)(2,1)S(1)}, u32[]{:S(2)}, u32[]{:S(2)}) collective-permute-start(bf16[16,240,128]{2,1,0:T(8,128)(2,1)S(1)} %bitcast.8), channel_id=1, source_target_pairs={{0,1},{1,0},{2,3},{3,2},{4,5},{5,4},{6,7},{7,6},{8,9},{9,8},{10,11... | collective-permute-start | bytes 2949128 | tf_op jit(solution)/shard_map/ppermute | solution.py:299
  53.3 2.3 %collective-permute-start.5 = (bf16[16,256,128]{2,1,0:T(8,128)(2,1)}, bf16[16,256,128]{2,1,0:T(8,128)(2,1)S(1)}, u32[]{:S(2)}, u32[]{:S(2)}) collective-permute-start(bf16[16,256,128]{2,1,0:T(8,128)(2,1)} %get-tuple-element.29), channel_id=1, source_target_pairs={{0,2},{1,3},{2,0},{3,1},{4,6},{5,7},{6,4},{7,5},{8,10},{9,11},{10,... | collective-permute-start | bytes 3145736 | tf_op jit(solution)/shard_map/ppermute | solution.py:299
  55.6 0.2 collective-permute-done.there
  55.8 0.0 collective-permute-done.1
  55.8 0.0 copy-done.2
  55.8 0.7 shard_map.149
  56.5 0.0 copy-start.8
  56.5 0.0 copy-start.9
  56.5 0.0 copy-start.6
  56.6 0.0 copy-start.7
  56.6 2.1 %collective-permute-start.4 = (bf16[64,224]{1,0:T(8,128)(2,1)S(1)}, bf16[64,224]{1,0:T(8,128)(2,1)S(1)}, u32[]{:S(2)}, u32[]{:S(2)}) collective-permute-start(bf16[64,224]{1,0:T(8,128)(2,1)S(1)} %get-tuple-element.23), channel_id=1, source_target_pairs={{0,4},{1,5},{2,6},{3,7},{4,12},{5,13},{6,14},{7,15},{8,20},{9,21},... | collective-permute-start | bytes 86024 | tf_op jit(solution)/shard_map/ppermute | solution.py:299
  58.6 0.7 collective-permute-start.3
  59.3 0.0 copy-done.1
  59.3 0.7 shard_map.150
  60.0 0.0 copy-start
  60.0 12.2 %collective-permute-done.4 = bf16[64,224]{1,0:T(8,128)(2,1)S(1)} collective-permute-done((bf16[64,224]{1,0:T(8,128)(2,1)S(1)}, bf16[64,224]{1,0:T(8,128)(2,1)S(1)}, u32[]{:S(2)}, u32[]{:S(2)}) %collective-permute-start.4) | collective-permute-done | bytes 28704 | tf_op jit(solution)/shard_map/ppermute | solution.py:299
  72.2 0.0 collective-permute-done.3
  72.2 3.4 %collective-permute-start.6 = (bf16[144,224]{1,0:T(8,128)(2,1)S(1)}, bf16[144,224]{1,0:T(8,128)(2,1)S(1)}, u32[]{:S(2)}, u32[]{:S(2)}) collective-permute-start(bf16[144,224]{1,0:T(8,128)(2,1)S(1)} %pad_maximum_fusion.near), channel_id=1, source_target_pairs={{0,2},{1,3},{2,0},{3,1},{4,6},{5,7},{6,4},{7,5},{8,10},{9,11},{10,... | collective-permute-start | bytes 193544 | tf_op jit(solution)/shard_map/ppermute | solution.py:299
  75.6 2.4 %collective-permute-start.2 = (bf16[224,128]{1,0:T(8,128)(2,1)S(1)}, bf16[224,128]{1,0:T(8,128)(2,1)S(1)}, u32[]{:S(2)}, u32[]{:S(2)}) collective-permute-start(bf16[224,128]{1,0:T(8,128)(2,1)S(1)} %get-tuple-element.26), channel_id=1, source_target_pairs={{0,2},{1,3},{2,0},{3,1},{4,6},{5,7},{6,4},{7,5},{8,10},{9,11},{10,... | collective-permute-start | bytes 172040 | tf_op jit(solution)/shard_map/ppermute | solution.py:299
  78.1 3.3 %collective-permute-done.5 = bf16[16,256,128]{2,1,0:T(8,128)(2,1)S(1)} collective-permute-done((bf16[16,256,128]{2,1,0:T(8,128)(2,1)}, bf16[16,256,128]{2,1,0:T(8,128)(2,1)S(1)}, u32[]{:S(2)}, u32[]{:S(2)}) %collective-permute-start.5) | collective-permute-done | bytes 1048608 | tf_op jit(solution)/shard_map/ppermute | solution.py:299
  81.4 1.6 %collective-permute-done.6.far = bf16[144,224]{1,0:T(8,128)(2,1)S(1)} collective-permute-done((bf16[144,224]{1,0:T(8,128)(2,1)S(1)}, bf16[144,224]{1,0:T(8,128)(2,1)S(1)}, u32[]{:S(2)}, u32[]{:S(2)}) %collective-permute-start.6) | collective-permute-done | bytes 64544 | tf_op jit(solution)/shard_map/ppermute | solution.py:299
  82.9 0.0 copy-done.8
  82.9 0.0 copy-done.9
  82.9 0.1 shard_map.151
  83.1 1.9 %collective-permute-start.7 = (bf16[4,32,224]{2,1,0:T(8,128)(2,1)S(1)}, bf16[4,32,224]{2,1,0:T(8,128)(2,1)S(1)}, u32[]{:S(2)}, u32[]{:S(2)}) collective-permute-start(bf16[4,32,224]{2,1,0:T(8,128)(2,1)S(1)} %get-tuple-element.32.own), channel_id=1, source_target_pairs={{0,1},{1,0},{2,3},{3,2},{4,5},{5,4},{6,7},{7,6},{8,9},{9,8},{10,11... | collective-permute-start | bytes 172040 | tf_op jit(solution)/shard_map/ppermute | solution.py:299
  85.0 0.0 collective-permute-done.2.other
  85.0 0.0 copy-done.6
  85.0 0.2 shard_map.152.query
  85.2 1.0 collective-permute-done.7.sibling
  86.2 0.5 shard_map.153
  86.7 31.4 %all-gather.1 = bf16[3584,128]{1,0:T(8,128)(2,1)S(1)} all-gather(bf16[224,128]{1,0:T(8,128)(2,1)S(1)} %shard_map.153), channel_id=3, replica_groups=mesh['section'=8,'z'=16,'y'=2,'core'=2] {'z'}, dimensions={0}, use_global_device_ids=true | all-gather | bytes 974848 | tf_op jit(solution)/shard_map/all_gather | solution.py:315
  118.1 2.1 %collective-permute-start.8 = (bf16[16,224,128]{2,1,0:T(8,128)(2,1)S(1)}, bf16[16,224,128]{2,1,0:T(8,128)(2,1)S(1)}, u32[]{:S(2)}, u32[]{:S(2)}) collective-permute-start(bf16[16,224,128]{2,1,0:T(8,128)(2,1)S(1)} %bitcast.15), channel_id=1, source_target_pairs={{0,1},{1,0},{2,3},{3,2},{4,5},{5,4},{6,7},{7,6},{8,9},{9,8},{10,11... | collective-permute-start | bytes 2752520 | tf_op jit(solution)/shard_map/ppermute | solution.py:299
  120.2 2.4 %collective-permute-done.8.there = bf16[16,224,128]{2,1,0:T(8,128)(2,1)S(1)} collective-permute-done((bf16[16,224,128]{2,1,0:T(8,128)(2,1)S(1)}, bf16[16,224,128]{2,1,0:T(8,128)(2,1)S(1)}, u32[]{:S(2)}, u32[]{:S(2)}) %collective-permute-start.8) | collective-permute-done | bytes 917536 | tf_op jit(solution)/shard_map/ppermute | solution.py:299
  122.6 0.0 copy-done
  122.6 0.7 shard_map.154
  123.3 2.3 %collective-permute-start.9 = (bf16[224,128]{1,0:T(8,128)(2,1)S(1)}, bf16[224,128]{1,0:T(8,128)(2,1)S(1)}, u32[]{:S(2)}, u32[]{:S(2)}) collective-permute-start(bf16[224,128]{1,0:T(8,128)(2,1)S(1)} %get-tuple-element.34), channel_id=1, source_target_pairs={{0,2},{1,3},{2,0},{3,1},{4,6},{5,7},{6,4},{7,5},{8,10},{9,11},{10,... | collective-permute-start | bytes 172040 | tf_op jit(solution)/shard_map/ppermute | solution.py:299
  125.7 3.7 %collective-permute-done.9.other = bf16[224,128]{1,0:T(8,128)(2,1)S(1)} collective-permute-done((bf16[224,128]{1,0:T(8,128)(2,1)S(1)}, bf16[224,128]{1,0:T(8,128)(2,1)S(1)}, u32[]{:S(2)}, u32[]{:S(2)}) %collective-permute-start.9) | collective-permute-done | bytes 57376 | tf_op jit(solution)/shard_map/ppermute | solution.py:299
  129.4 0.0 copy-done.3
  129.4 0.6 shard_map.155.message
  130.0 4.8 %collective-permute-start.10 = (bf16[2,112,128]{2,1,0:T(8,128)(2,1)S(1)}, bf16[2,112,128]{2,1,0:T(8,128)(2,1)S(1)}, u32[]{:S(2)}, u32[]{:S(2)}) collective-permute-start(bf16[2,112,128]{2,1,0:T(8,128)(2,1)S(1)} %shard_map.155.message), channel_id=1, source_target_pairs={{0,64},{64,128},{128,192},{192,256},{256,320},{320,384},{384,448},... | collective-permute-start | bytes 172040 | tf_op jit(solution)/shard_map/ppermute | solution.py:400
  134.8 1.2 shard_map.157
  136.0 2.4 %collective-permute-done.10.arrived = bf16[2,112,128]{2,1,0:T(8,128)(2,1)S(1)} collective-permute-done((bf16[2,112,128]{2,1,0:T(8,128)(2,1)S(1)}, bf16[2,112,128]{2,1,0:T(8,128)(2,1)S(1)}, u32[]{:S(2)}, u32[]{:S(2)}) %collective-permute-start.10) | collective-permute-done | bytes 57376 | tf_op jit(solution)/shard_map/ppermute | solution.py:400
  138.4 0.0 copy-done.4
  138.4 1.2 shard_map.156
  (9 shorter events, 0.0 us)
Async XLA Ops:
  0.6 55.2 %copy-start.2 = (bf16[1,8192,32]{1,2,0:T(8,128)(2,1)S(1)}, bf16[1,8192,32]{1,2,0:T(8,128)(2,1)}, u32[]{:S(2)}) copy-start(bf16[1,8192,32]{1,2,0:T(8,128)(2,1)} %param.20) | copy-start | bytes 1572868
  5.6 50.2 %collective-permute-start.1 = (bf16[20,256,128]{2,1,0:T(8,128)(2,1)}, bf16[20,256,128]{2,1,0:T(8,128)(2,1)S(1)}, u32[]{:S(2)}, u32[]{:S(2)}) collective-permute-start(bf16[20,256,128]{2,1,0:T(8,128)(2,1)} %get-tuple-element.22), channel_id=1, source_target_pairs={{0,2},{1,3},{2,0},{3,1},{4,6},{5,7},{6,4},{7,5},{8,10},{9,11},{10,... | collective-permute-start | bytes 3932168 | tf_op jit(solution)/shard_map/ppermute | solution.py:299
  51.2 8.1 %copy-start.1 = (bf16[1,8192,128]{2,1,0:T(8,128)(2,1)S(1)}, bf16[1,8192,128]{2,1,0:T(8,128)(2,1)}, u32[]{:S(2)}) copy-start(bf16[1,8192,128]{2,1,0:T(8,128)(2,1)} %weight.2) | copy-start | bytes 6291460
  51.2 4.6 %collective-permute-start = (bf16[16,240,128]{2,1,0:T(8,128)(2,1)S(1)}, bf16[16,240,128]{2,1,0:T(8,128)(2,1)S(1)}, u32[]{:S(2)}, u32[]{:S(2)}) collective-permute-start(bf16[16,240,128]{2,1,0:T(8,128)(2,1)S(1)} %bitcast.8), channel_id=1, source_target_pairs={{0,1},{1,0},{2,3},{3,2},{4,5},{5,4},{6,7},{7,6},{8,9},{9,8},{10,11... | collective-permute-start | bytes 2949128 | tf_op jit(solution)/shard_map/ppermute | solution.py:299
  53.3 28.1 %collective-permute-start.5 = (bf16[16,256,128]{2,1,0:T(8,128)(2,1)}, bf16[16,256,128]{2,1,0:T(8,128)(2,1)S(1)}, u32[]{:S(2)}, u32[]{:S(2)}) collective-permute-start(bf16[16,256,128]{2,1,0:T(8,128)(2,1)} %get-tuple-element.29), channel_id=1, source_target_pairs={{0,2},{1,3},{2,0},{3,1},{4,6},{5,7},{6,4},{7,5},{8,10},{9,11},{10,... | collective-permute-start | bytes 3145736 | tf_op jit(solution)/shard_map/ppermute | solution.py:299
  56.5 26.4 %copy-start.8 = (f32[64,224]{1,0:T(8,128)S(1)}, f32[64,224]{1,0:T(8,128)}, u32[]{:S(2)}) copy-start(f32[64,224]{1,0:T(8,128)} %constant.9.clone.sin_t) | copy-start | bytes 172036
  56.5 26.4 %copy-start.9 = (f32[64,224]{1,0:T(8,128)S(1)}, f32[64,224]{1,0:T(8,128)}, u32[]{:S(2)}) copy-start(f32[64,224]{1,0:T(8,128)} %constant.8.clone.cos_t) | copy-start | bytes 172036
  56.5 28.5 %copy-start.6 = (f32[224,64]{1,0:T(8,128)S(1)}, f32[224,64]{1,0:T(8,128)}, u32[]{:S(2)}) copy-start(f32[224,64]{1,0:T(8,128)} %constant.11.clone.sin) | copy-start | bytes 172036
  56.6 28.4 %copy-start.7 = (f32[224,64]{1,0:T(8,128)S(1)}, f32[224,64]{1,0:T(8,128)}, u32[]{:S(2)}) copy-start(f32[224,64]{1,0:T(8,128)} %constant.10.clone.cos) | copy-start | bytes 172036
  56.6 15.6 %collective-permute-start.4 = (bf16[64,224]{1,0:T(8,128)(2,1)S(1)}, bf16[64,224]{1,0:T(8,128)(2,1)S(1)}, u32[]{:S(2)}, u32[]{:S(2)}) collective-permute-start(bf16[64,224]{1,0:T(8,128)(2,1)S(1)} %get-tuple-element.23), channel_id=1, source_target_pairs={{0,4},{1,5},{2,6},{3,7},{4,12},{5,13},{6,14},{7,15},{8,20},{9,21},... | collective-permute-start | bytes 86024 | tf_op jit(solution)/shard_map/ppermute | solution.py:299
  58.6 13.6 %collective-permute-start.3 = (bf16[64,224]{1,0:T(8,128)(2,1)S(1)}, bf16[64,224]{1,0:T(8,128)(2,1)S(1)}, u32[]{:S(2)}, u32[]{:S(2)}) collective-permute-start(bf16[64,224]{1,0:T(8,128)(2,1)S(1)} %get-tuple-element.23), channel_id=1, source_target_pairs={{0,0},{1,1},{2,2},{3,3},{4,8},{5,9},{6,10},{7,11},{8,16},{9,17},{1... | collective-permute-start | bytes 86024 | tf_op jit(solution)/shard_map/ppermute | solution.py:299
  60.0 62.6 %copy-start = (bf16[1,8192,128]{2,1,0:T(8,128)(2,1)S(1)}, bf16[1,8192,128]{2,1,0:T(8,128)(2,1)}, u32[]{:S(2)}) copy-start(bf16[1,8192,128]{2,1,0:T(8,128)(2,1)} %weight.3) | copy-start | bytes 6291460
  72.2 10.7 %collective-permute-start.6 = (bf16[144,224]{1,0:T(8,128)(2,1)S(1)}, bf16[144,224]{1,0:T(8,128)(2,1)S(1)}, u32[]{:S(2)}, u32[]{:S(2)}) collective-permute-start(bf16[144,224]{1,0:T(8,128)(2,1)S(1)} %pad_maximum_fusion.near), channel_id=1, source_target_pairs={{0,2},{1,3},{2,0},{3,1},{4,6},{5,7},{6,4},{7,5},{8,10},{9,11},{10,... | collective-permute-start | bytes 193544 | tf_op jit(solution)/shard_map/ppermute | solution.py:299
  75.6 9.3 %collective-permute-start.2 = (bf16[224,128]{1,0:T(8,128)(2,1)S(1)}, bf16[224,128]{1,0:T(8,128)(2,1)S(1)}, u32[]{:S(2)}, u32[]{:S(2)}) collective-permute-start(bf16[224,128]{1,0:T(8,128)(2,1)S(1)} %get-tuple-element.26), channel_id=1, source_target_pairs={{0,2},{1,3},{2,0},{3,1},{4,6},{5,7},{6,4},{7,5},{8,10},{9,11},{10,... | collective-permute-start | bytes 172040 | tf_op jit(solution)/shard_map/ppermute | solution.py:299
  83.1 3.1 %collective-permute-start.7 = (bf16[4,32,224]{2,1,0:T(8,128)(2,1)S(1)}, bf16[4,32,224]{2,1,0:T(8,128)(2,1)S(1)}, u32[]{:S(2)}, u32[]{:S(2)}) collective-permute-start(bf16[4,32,224]{2,1,0:T(8,128)(2,1)S(1)} %get-tuple-element.32.own), channel_id=1, source_target_pairs={{0,1},{1,0},{2,3},{3,2},{4,5},{5,4},{6,7},{7,6},{8,9},{9,8},{10,11... | collective-permute-start | bytes 172040 | tf_op jit(solution)/shard_map/ppermute | solution.py:299
  118.1 11.3 %copy-start.3 = (bf16[1,3,112,128]{3,2,1,0:T(8,128)(2,1)S(1)}, bf16[1,3,112,128]{3,2,1,0:T(8,128)(2,1)}, u32[]{:S(2)}) copy-start(bf16[1,3,112,128]{3,2,1,0:T(8,128)(2,1)} %buffer_out.3) | copy-start | bytes 258052
  118.1 11.3 %copy-start.5 = (bf16[2,112,128]{2,1,0:T(8,128)(2,1)S(1)}, bf16[2,112,128]{2,1,0:T(8,128)(2,1)}, u32[]{:S(2)}) copy-start(bf16[2,112,128]{2,1,0:T(8,128)(2,1)} %get-tuple-element.20.inputs) | copy-start | bytes 172036
  118.1 11.3 %copy-start.10 = (s32[8,2]{0,1:T(2,128)S(1)}, s32[8,2]{0,1:T(2,128)}, u32[]{:S(2)}) copy-start(s32[8,2]{0,1:T(2,128)} %param.15) | copy-start | bytes 196
  118.1 20.3 %copy-start.4 = (bf16[1,3,112,128]{3,2,1,0:T(8,128)(2,1)S(1)}, bf16[1,3,112,128]{3,2,1,0:T(8,128)(2,1)}, u32[]{:S(2)}) copy-start(bf16[1,3,112,128]{3,2,1,0:T(8,128)(2,1)} %buffer_in.3) | copy-start | bytes 258052
  118.1 4.5 %collective-permute-start.8 = (bf16[16,224,128]{2,1,0:T(8,128)(2,1)S(1)}, bf16[16,224,128]{2,1,0:T(8,128)(2,1)S(1)}, u32[]{:S(2)}, u32[]{:S(2)}) collective-permute-start(bf16[16,224,128]{2,1,0:T(8,128)(2,1)S(1)} %bitcast.15), channel_id=1, source_target_pairs={{0,1},{1,0},{2,3},{3,2},{4,5},{5,4},{6,7},{7,6},{8,9},{9,8},{10,11... | collective-permute-start | bytes 2752520 | tf_op jit(solution)/shard_map/ppermute | solution.py:299
  123.3 6.1 %collective-permute-start.9 = (bf16[224,128]{1,0:T(8,128)(2,1)S(1)}, bf16[224,128]{1,0:T(8,128)(2,1)S(1)}, u32[]{:S(2)}, u32[]{:S(2)}) collective-permute-start(bf16[224,128]{1,0:T(8,128)(2,1)S(1)} %get-tuple-element.34), channel_id=1, source_target_pairs={{0,2},{1,3},{2,0},{3,1},{4,6},{5,7},{6,4},{7,5},{8,10},{9,11},{10,... | collective-permute-start | bytes 172040 | tf_op jit(solution)/shard_map/ppermute | solution.py:299
  130.0 8.5 %collective-permute-start.10 = (bf16[2,112,128]{2,1,0:T(8,128)(2,1)S(1)}, bf16[2,112,128]{2,1,0:T(8,128)(2,1)S(1)}, u32[]{:S(2)}, u32[]{:S(2)}) collective-permute-start(bf16[2,112,128]{2,1,0:T(8,128)(2,1)S(1)} %shard_map.155.message), channel_id=1, source_target_pairs={{0,64},{64,128},{128,192},{192,256},{256,320},{320,384},{384,448},... | collective-permute-start | bytes 172040 | tf_op jit(solution)/shard_map/ppermute | solution.py:400

commit v2 on v1

--- a/solution.py
+++ b/solution.py
@@ -52,8 +52,8 @@
 
 
 def prepare(
-    ids, codes, exponents, buffer_in, gain, query, keyval, output,
-    packed, packed_out, pay, inputs_out,
+    ids, codes, exponents, buffer_in, gain, query, keyval,
+    packed, pay, inputs_out,
     codes_v, exponents_v, stored_v, gain_v, keyval_v, half_v, keyval_half_v, sems, half_sems,
 ):
     section = lax.axis_index("section")
@@ -71,14 +71,13 @@
 
     step = ZN // PIECES
     loads, stores = [], []
-    for i in range(2 * PIECES):
-        source, target = (query, packed) if i < PIECES else (output, packed_out)
-        part = pl.ds(i % PIECES * step, step)
+    for i in range(PIECES):
+        part = pl.ds(i * step, step)
         loads.append(
-            pltpu.make_async_copy(source.at[part, far], half_v.at[i], half_sems.at[0, i])
+            pltpu.make_async_copy(query.at[part, far], half_v.at[i], half_sems.at[0, i])
         )
         stores.append(
-            pltpu.make_async_copy(half_v.at[i], target.at[part], half_sems.at[1, i])
+            pltpu.make_async_copy(half_v.at[i], packed.at[part], half_sems.at[1, i])
         )
         loads[-1].start()
     for item in copies[:5]:
@@ -246,6 +245,12 @@
     out[...] = context.astype(jnp.bfloat16)
 
 
+def pack_kernel(weight, out):
+    far = lax.axis_index("y") ^ 1
+    for z in range(ZN):
+        out[z] = weight[z, far]
+
+
 def output_kernel(here, there, weight, received, mine_out, other_out):
     acc = both_partials(here, there, weight, received)
     mine_out[...] = acc[:, :HEAD]
@@ -299,12 +304,8 @@
     return lax.ppermute(x, LANES, pairs)
 
 
-def swap_core(x):
-    return permute(x, lambda z, y, c: (z, y, c ^ 1))
-
-
-def swap_y(x):
-    return permute(x, lambda z, y, c: (z, y ^ 1, c))
+def swap(x, flip_y, flip_core):
+    return permute(x, lambda z, y, c: (z, y ^ flip_y, c ^ flip_core))
 
 
 def after(x, earlier):
@@ -326,39 +327,40 @@
     partial_flops = 2 * ROWS * half * 256
     wide = shape((ROWS, HEAD), jnp.float32)
 
-    by_half = (ZN, YN, CN * HEAD, HEAD)
     any_spec = pl.BlockSpec(memory_space=pl.ANY)
     bf16, int32 = jnp.bfloat16, jnp.int32
-    packed, packed_out, pay, inputs = pl.pallas_call(
+    packed, pay, inputs = pl.pallas_call(
         prepare,
         out_shape=(
             shape((ZN + ZN * kv_width // HEAD, CN * HEAD, HEAD)),
-            shape((ZN, CN * HEAD, HEAD)),
             shape((PAY, HEAD)),
             shape((SEQS, LEN, HEAD)),
         ),
-        in_specs=[SMEM] + [any_spec] * 7,
-        out_specs=(any_spec, any_spec, VMEM, VMEM),
+        in_specs=[SMEM] + [any_spec] * 6,
+        out_specs=(any_spec, VMEM, VMEM),
         scratch_shapes=[
             pltpu.VMEM(codes.shape, int32),
             pltpu.VMEM(exponents.shape, int32),
             pltpu.VMEM((SEQS, LEN, HEAD), bf16),
             pltpu.VMEM(norm_gain.shape, bf16),
             pltpu.VMEM(w_keyval.shape, bf16),
-            pltpu.VMEM((2 * PIECES, ZN // PIECES, CN * HEAD, HEAD), bf16),
+            pltpu.VMEM((PIECES, ZN // PIECES, CN * HEAD, HEAD), bf16),
             pltpu.VMEM((ZN * kv_width // HEAD, CN * HEAD, HEAD), bf16),
             pltpu.SemaphoreType.DMA((7,)),
-            pltpu.SemaphoreType.DMA((2, 2 * PIECES)),
+            pltpu.SemaphoreType.DMA((2, PIECES)),
         ],
         cost_estimate=pl.CostEstimate(flops=10**7, bytes_accessed=4 * 10**6, transcendentals=0),
     )(
         sample_ids, codes, exponents, buffer_in, norm_gain,
-        w_query.reshape(by_half), w_keyval, w_output.reshape(by_half),
-    )
-    received = swap_y(packed).reshape(-1, HEAD)
-    received_out = swap_y(packed_out).reshape(half, HEAD)
+        w_query.reshape(ZN, YN, CN * HEAD, HEAD), w_keyval,
+    )
+    received = swap(packed, 1, 0).reshape(-1, HEAD)
     here = gather_z(pay)
-    there = swap_core(here)
+    there = swap(here, 0, 1)
+    packed_out = call(pack_kernel, shape((ZN, CN * HEAD, HEAD)), 1, 10**6, 2 * 10**6)(
+        w_output.reshape(ZN, YN, CN * HEAD, HEAD)
+    )
+    received_out = swap(packed_out, 1, 0).reshape(half, HEAD)
 
     keyval, sums = call(
         keyval_kernel,
@@ -372,13 +374,13 @@
     mine, other = call(
         query_kernel, (wide, shape((ROWS, HEAD))), 4, partial_flops, 6 * 10**6
     )(here, there, w_query, after(received, keyval))
-    other = swap_y(other)
+    other = swap(other, 1, 0)
     near = after(jnp.concatenate([even, odd, sums]), mine)
-    far = swap_y(near)
+    far = swap(near, 1, 0)
     own, factors = call(
         sum_kernel, (shape((4, kv_width, ROWS)), wide), 4, 10**6, 10**6
     )(after(near, received_out), far, cos.T.copy(), sin.T.copy())
-    sibling = swap_core(own)
+    sibling = swap(own, 0, 1)
     queries = call(rope_kernel, shape((ROWS, HEAD)), 5, 10**6, 10**6)(
         mine, other, factors, cos, sin
     )
@@ -387,11 +389,11 @@
     )
 
     here = gather_z(context)
-    there = swap_core(here)
+    there = swap(here, 0, 1)
     mine, other = call(
         output_kernel, (wide, shape((ROWS, HEAD))), 4, partial_flops, 6 * 10**6
     )(here, there, w_output, received_out)
-    other = swap_y(other)
+    other = swap(other, 1, 0)
     message = call(
         message_kernel, shape((SEQS, LEN, HEAD)), 5, 10**6, 10**6, smem=(0,)
     )(sample_ids, mine, other, inputs, buffer_out)

time: 140 us -> 139 us (level)
  transfers between devices with their start and end apart: 11 -> 11, of which waited for: 8 -> 7; matrix products, arithmetic and copies ran while one was open for 0% -> 0% of each run, Pallas kernels for 2% -> 2%
where the time goes in v2:
time: 139 us
  blocking collectives  73.7 us (53%)
  starting transfers between devices  27.6 us (20%)
  waiting for transfers between devices  26.6 us (19%)
  Pallas kernels  10.2 us (7%)
    all_gather x2, blocking collectives, gather_z(): return lax.all_gather(x, 'z', axis=0)  73.7 us
    ppermute x10, waiting for transfers between devices, permute(): return lax.ppermute(x, LANES, pairs)  24.1 us
    ppermute x10, starting transfers between devices, permute(): return lax.ppermute(x, LANES, pairs)  22.8 us
    ppermute x1, starting transfers between devices, per_device(): lax.ppermute(message, 'section', [(i, i + 1) for i in range(sections - 1)])  4.81 us
    pallas_call x1, Pallas kernels, per_device(): pl.pallas_call(prepare, out_shape=(shape((ZN + ZN * kv_width // HEAD, CN...  4.26 us
  transfers between devices with their start and end apart: 11, of which 7 were waited for; matrix products, arithmetic and copies ran while one was open for 0% of the time, Pallas kernels for 2%

profile of v2, /device:TPU:6, one launch (start us, length us, event | category | flops | bytes accessed | tf_op | source)
XLA Modules:
  0.0 139.0 jit_solution(9611473684604765316)
XLA Ops:
  0.6 0.0 copy-start
  0.6 4.3 %shard_map.148 = (bf16[20,256,128]{2,1,0:T(8,128)(2,1)}, bf16[240,128]{1,0:T(8,128)(2,1)}, bf16[2,112,128]{2,1,0:T(8,128)(2,1)}) custom-call(s32[2,8]{1,0:T(2,128)} %bitcast.20, s32[1,2,112,128]{3,2,1,0:T(8,128)} %codes.1, s32[1,2,112]{2,1,0:T(2,128)} %exponents.1, bf16[1,3,112,128]{3,2,1,0:T(8,128)(2,1)} %buffer_in.3, bf16[1,128]{1,0:T(2,128)(2,1)} %gain.1, ...), custom_call_target="tpu_custom_call" | custom-call | flops 10000000 | bytes 4000000 | tf_op jit(solution)/shard_map/pallas_call | solution.py:332
  4.9 3.5 %collective-permute-start.1 = (bf16[20,256,128]{2,1,0:T(8,128)(2,1)}, bf16[20,256,128]{2,1,0:T(8,128)(2,1)S(1)}, u32[]{:S(2)}, u32[]{:S(2)}) collective-permute-start(bf16[20,256,128]{2,1,0:T(8,128)(2,1)} %get-tuple-element.21), channel_id=1, source_target_pairs={{0,2},{1,3},{2,0},{3,1},{4,6},{5,7},{6,4},{7,5},{8,10},{9,11},{10,... | collective-permute-start | bytes 3932168 | tf_op jit(solution)/shard_map/ppermute | solution.py:304
  8.4 0.0 copy-start.2
  8.4 42.3 %all-gather = bf16[3840,128]{1,0:T(8,128)(2,1)S(1)} all-gather(bf16[240,128]{1,0:T(8,128)(2,1)} %get-tuple-element.20), channel_id=2, replica_groups=mesh['section'=8,'z'=16,'y'=2,'core'=2] {'z'}, dimensions={0}, use_global_device_ids=true | all-gather | bytes 1044480 | tf_op jit(solution)/shard_map/all_gather | solution.py:316
  50.7 1.9 %collective-permute-start = (bf16[16,240,128]{2,1,0:T(8,128)(2,1)S(1)}, bf16[16,240,128]{2,1,0:T(8,128)(2,1)S(1)}, u32[]{:S(2)}, u32[]{:S(2)}) collective-permute-start(bf16[16,240,128]{2,1,0:T(8,128)(2,1)S(1)} %bitcast.8), channel_id=1, source_target_pairs={{0,1},{1,0},{2,3},{3,2},{4,5},{5,4},{6,7},{7,6},{8,9},{9,8},{10,11... | collective-permute-start | bytes 2949128 | tf_op jit(solution)/shard_map/ppermute | solution.py:304
  52.6 0.1 shard_map.151
  52.7 0.0 copy-start.1
  52.7 2.5 %collective-permute-start.5 = (bf16[16,256,128]{2,1,0:T(8,128)(2,1)S(1)}, bf16[16,256,128]{2,1,0:T(8,128)(2,1)S(1)}, u32[]{:S(2)}, u32[]{:S(2)}) collective-permute-start(bf16[16,256,128]{2,1,0:T(8,128)(2,1)S(1)} %shard_map.151), channel_id=1, source_target_pairs={{0,2},{1,3},{2,0},{3,1},{4,6},{5,7},{6,4},{7,5},{8,10},{9,11},{10,... | collective-permute-start | bytes 3145736 | tf_op jit(solution)/shard_map/ppermute | solution.py:304
  55.2 0.0 collective-permute-done.there
  55.2 0.0 collective-permute-done.1
  55.2 0.7 shard_map.149
  55.9 0.0 copy-start.8
  55.9 0.0 copy-start.9
  56.0 0.0 copy-start.6
  56.0 0.0 copy-start.7
  56.0 2.1 %collective-permute-start.4 = (bf16[64,224]{1,0:T(8,128)(2,1)S(1)}, bf16[64,224]{1,0:T(8,128)(2,1)S(1)}, u32[]{:S(2)}, u32[]{:S(2)}) collective-permute-start(bf16[64,224]{1,0:T(8,128)(2,1)S(1)} %get-tuple-element.22), channel_id=1, source_target_pairs={{0,4},{1,5},{2,6},{3,7},{4,12},{5,13},{6,14},{7,15},{8,20},{9,21},... | collective-permute-start | bytes 86024 | tf_op jit(solution)/shard_map/ppermute | solution.py:304
  58.0 0.7 collective-permute-start.3
  58.7 0.0 copy-done.1
  58.7 0.7 shard_map.150
  59.4 12.2 %collective-permute-done.4 = bf16[64,224]{1,0:T(8,128)(2,1)S(1)} collective-permute-done((bf16[64,224]{1,0:T(8,128)(2,1)S(1)}, bf16[64,224]{1,0:T(8,128)(2,1)S(1)}, u32[]{:S(2)}, u32[]{:S(2)}) %collective-permute-start.4) | collective-permute-done | bytes 28704 | tf_op jit(solution)/shard_map/ppermute | solution.py:304
  71.6 0.0 collective-permute-done.3
  71.7 3.5 %collective-permute-start.6 = (bf16[144,224]{1,0:T(8,128)(2,1)S(1)}, bf16[144,224]{1,0:T(8,128)(2,1)S(1)}, u32[]{:S(2)}, u32[]{:S(2)}) collective-permute-start(bf16[144,224]{1,0:T(8,128)(2,1)S(1)} %pad_maximum_fusion.near), channel_id=1, source_target_pairs={{0,2},{1,3},{2,0},{3,1},{4,6},{5,7},{6,4},{7,5},{8,10},{9,11},{10,... | collective-permute-start | bytes 193544 | tf_op jit(solution)/shard_map/ppermute | solution.py:304
  75.2 2.3 %collective-permute-start.2 = (bf16[224,128]{1,0:T(8,128)(2,1)S(1)}, bf16[224,128]{1,0:T(8,128)(2,1)S(1)}, u32[]{:S(2)}, u32[]{:S(2)}) collective-permute-start(bf16[224,128]{1,0:T(8,128)(2,1)S(1)} %get-tuple-element.25), channel_id=1, source_target_pairs={{0,2},{1,3},{2,0},{3,1},{4,6},{5,7},{6,4},{7,5},{8,10},{9,11},{10,... | collective-permute-start | bytes 172040 | tf_op jit(solution)/shard_map/ppermute | solution.py:304
  77.5 3.2 %collective-permute-done.5 = bf16[16,256,128]{2,1,0:T(8,128)(2,1)S(1)} collective-permute-done((bf16[16,256,128]{2,1,0:T(8,128)(2,1)S(1)}, bf16[16,256,128]{2,1,0:T(8,128)(2,1)S(1)}, u32[]{:S(2)}, u32[]{:S(2)}) %collective-permute-start.5) | collective-permute-done | bytes 1048608 | tf_op jit(solution)/shard_map/ppermute | solution.py:304
  80.7 1.6 %collective-permute-done.6.far = bf16[144,224]{1,0:T(8,128)(2,1)S(1)} collective-permute-done((bf16[144,224]{1,0:T(8,128)(2,1)S(1)}, bf16[144,224]{1,0:T(8,128)(2,1)S(1)}, u32[]{:S(2)}, u32[]{:S(2)}) %collective-permute-start.6) | collective-permute-done | bytes 64544 | tf_op jit(solution)/shard_map/ppermute | solution.py:304
  82.3 0.1 shard_map.152
  82.4 1.9 %collective-permute-start.7 = (bf16[4,32,224]{2,1,0:T(8,128)(2,1)S(1)}, bf16[4,32,224]{2,1,0:T(8,128)(2,1)S(1)}, u32[]{:S(2)}, u32[]{:S(2)}) collective-permute-start(bf16[4,32,224]{2,1,0:T(8,128)(2,1)S(1)} %get-tuple-element.30.own), channel_id=1, source_target_pairs={{0,1},{1,0},{2,3},{3,2},{4,5},{5,4},{6,7},{7,6},{8,9},{9,8},{10,11... | collective-permute-start | bytes 172040 | tf_op jit(solution)/shard_map/ppermute | solution.py:304
  84.3 0.0 collective-permute-done.2.other
  84.3 0.0 copy-done.6
  84.4 0.0 copy-done.7
  84.4 0.2 shard_map.153.query
  84.6 1.0 collective-permute-done.7.sibling
  85.6 0.5 shard_map.154
  86.0 31.4 %all-gather.1 = bf16[3584,128]{1,0:T(8,128)(2,1)S(1)} all-gather(bf16[224,128]{1,0:T(8,128)(2,1)S(1)} %shard_map.154), channel_id=3, replica_groups=mesh['section'=8,'z'=16,'y'=2,'core'=2] {'z'}, dimensions={0}, use_global_device_ids=true | all-gather | bytes 974848 | tf_op jit(solution)/shard_map/all_gather | solution.py:316
  117.5 2.1 %collective-permute-start.8 = (bf16[16,224,128]{2,1,0:T(8,128)(2,1)S(1)}, bf16[16,224,128]{2,1,0:T(8,128)(2,1)S(1)}, u32[]{:S(2)}, u32[]{:S(2)}) collective-permute-start(bf16[16,224,128]{2,1,0:T(8,128)(2,1)S(1)} %bitcast.15), channel_id=1, source_target_pairs={{0,1},{1,0},{2,3},{3,2},{4,5},{5,4},{6,7},{7,6},{8,9},{9,8},{10,11... | collective-permute-start | bytes 2752520 | tf_op jit(solution)/shard_map/ppermute | solution.py:304
  119.5 2.4 %collective-permute-done.8.there = bf16[16,224,128]{2,1,0:T(8,128)(2,1)S(1)} collective-permute-done((bf16[16,224,128]{2,1,0:T(8,128)(2,1)S(1)}, bf16[16,224,128]{2,1,0:T(8,128)(2,1)S(1)}, u32[]{:S(2)}, u32[]{:S(2)}) %collective-permute-start.8) | collective-permute-done | bytes 917536 | tf_op jit(solution)/shard_map/ppermute | solution.py:304
  122.0 0.6 shard_map.155
  122.6 2.4 %collective-permute-start.9 = (bf16[224,128]{1,0:T(8,128)(2,1)S(1)}, bf16[224,128]{1,0:T(8,128)(2,1)S(1)}, u32[]{:S(2)}, u32[]{:S(2)}) collective-permute-start(bf16[224,128]{1,0:T(8,128)(2,1)S(1)} %get-tuple-element.32), channel_id=1, source_target_pairs={{0,2},{1,3},{2,0},{3,1},{4,6},{5,7},{6,4},{7,5},{8,10},{9,11},{10,... | collective-permute-start | bytes 172040 | tf_op jit(solution)/shard_map/ppermute | solution.py:304
  125.0 3.7 %collective-permute-done.9.other = bf16[224,128]{1,0:T(8,128)(2,1)S(1)} collective-permute-done((bf16[224,128]{1,0:T(8,128)(2,1)S(1)}, bf16[224,128]{1,0:T(8,128)(2,1)S(1)}, u32[]{:S(2)}, u32[]{:S(2)}) %collective-permute-start.9) | collective-permute-done | bytes 57376 | tf_op jit(solution)/shard_map/ppermute | solution.py:304
  128.7 0.0 copy-done.3
  128.7 0.0 copy-done.10
  128.7 0.6 shard_map.156.message
  129.3 4.8 %collective-permute-start.10 = (bf16[2,112,128]{2,1,0:T(8,128)(2,1)S(1)}, bf16[2,112,128]{2,1,0:T(8,128)(2,1)S(1)}, u32[]{:S(2)}, u32[]{:S(2)}) collective-permute-start(bf16[2,112,128]{2,1,0:T(8,128)(2,1)S(1)} %shard_map.156.message), channel_id=1, source_target_pairs={{0,64},{64,128},{128,192},{192,256},{256,320},{320,384},{384,448},... | collective-permute-start | bytes 172040 | tf_op jit(solution)/shard_map/ppermute | solution.py:402
  134.1 1.2 shard_map.158
  135.3 2.4 %collective-permute-done.10.arrived = bf16[2,112,128]{2,1,0:T(8,128)(2,1)S(1)} collective-permute-done((bf16[2,112,128]{2,1,0:T(8,128)(2,1)S(1)}, bf16[2,112,128]{2,1,0:T(8,128)(2,1)S(1)}, u32[]{:S(2)}, u32[]{:S(2)}) %collective-permute-start.10) | collective-permute-done | bytes 57376 | tf_op jit(solution)/shard_map/ppermute | solution.py:402
  137.8 0.0 copy-done.4
  137.8 1.2 shard_map.157
  (10 shorter events, 0.0 us)
Async XLA Ops:
  0.6 52.0 %copy-start = (bf16[1,8192,128]{2,1,0:T(8,128)(2,1)S(1)}, bf16[1,8192,128]{2,1,0:T(8,128)(2,1)}, u32[]{:S(2)}) copy-start(bf16[1,8192,128]{2,1,0:T(8,128)(2,1)} %weight.3) | copy-start | bytes 6291460
  4.9 50.3 %collective-permute-start.1 = (bf16[20,256,128]{2,1,0:T(8,128)(2,1)}, bf16[20,256,128]{2,1,0:T(8,128)(2,1)S(1)}, u32[]{:S(2)}, u32[]{:S(2)}) collective-permute-start(bf16[20,256,128]{2,1,0:T(8,128)(2,1)} %get-tuple-element.21), channel_id=1, source_target_pairs={{0,2},{1,3},{2,0},{3,1},{4,6},{5,7},{6,4},{7,5},{8,10},{9,11},{10,... | collective-permute-start | bytes 3932168 | tf_op jit(solution)/shard_map/ppermute | solution.py:304
  8.4 46.8 %copy-start.2 = (bf16[1,8192,32]{1,2,0:T(8,128)(2,1)S(1)}, bf16[1,8192,32]{1,2,0:T(8,128)(2,1)}, u32[]{:S(2)}) copy-start(bf16[1,8192,32]{1,2,0:T(8,128)(2,1)} %param.20) | copy-start | bytes 1572868
  50.7 4.5 %collective-permute-start = (bf16[16,240,128]{2,1,0:T(8,128)(2,1)S(1)}, bf16[16,240,128]{2,1,0:T(8,128)(2,1)S(1)}, u32[]{:S(2)}, u32[]{:S(2)}) collective-permute-start(bf16[16,240,128]{2,1,0:T(8,128)(2,1)S(1)} %bitcast.8), channel_id=1, source_target_pairs={{0,1},{1,0},{2,3},{3,2},{4,5},{5,4},{6,7},{7,6},{8,9},{9,8},{10,11... | collective-permute-start | bytes 2949128 | tf_op jit(solution)/shard_map/ppermute | solution.py:304
  52.7 6.0 %copy-start.1 = (bf16[1,8192,128]{2,1,0:T(8,128)(2,1)S(1)}, bf16[1,8192,128]{2,1,0:T(8,128)(2,1)}, u32[]{:S(2)}) copy-start(bf16[1,8192,128]{2,1,0:T(8,128)(2,1)} %weight.2) | copy-start | bytes 6291460
  52.7 28.0 %collective-permute-start.5 = (bf16[16,256,128]{2,1,0:T(8,128)(2,1)S(1)}, bf16[16,256,128]{2,1,0:T(8,128)(2,1)S(1)}, u32[]{:S(2)}, u32[]{:S(2)}) collective-permute-start(bf16[16,256,128]{2,1,0:T(8,128)(2,1)S(1)} %shard_map.151), channel_id=1, source_target_pairs={{0,2},{1,3},{2,0},{3,1},{4,6},{5,7},{6,4},{7,5},{8,10},{9,11},{10,... | collective-permute-start | bytes 3145736 | tf_op jit(solution)/shard_map/ppermute | solution.py:304
  55.9 26.4 %copy-start.8 = (f32[64,224]{1,0:T(8,128)S(1)}, f32[64,224]{1,0:T(8,128)}, u32[]{:S(2)}) copy-start(f32[64,224]{1,0:T(8,128)} %constant.8.clone.cos_t) | copy-start | bytes 172036
  55.9 26.3 %copy-start.9 = (f32[64,224]{1,0:T(8,128)S(1)}, f32[64,224]{1,0:T(8,128)}, u32[]{:S(2)}) copy-start(f32[64,224]{1,0:T(8,128)} %constant.9.clone.sin_t) | copy-start | bytes 172036
  56.0 28.4 %copy-start.6 = (f32[224,64]{1,0:T(8,128)S(1)}, f32[224,64]{1,0:T(8,128)}, u32[]{:S(2)}) copy-start(f32[224,64]{1,0:T(8,128)} %constant.10.clone.cos) | copy-start | bytes 172036
  56.0 28.4 %copy-start.7 = (f32[224,64]{1,0:T(8,128)S(1)}, f32[224,64]{1,0:T(8,128)}, u32[]{:S(2)}) copy-start(f32[224,64]{1,0:T(8,128)} %constant.11.clone.sin) | copy-start | bytes 172036
  56.0 15.7 %collective-permute-start.4 = (bf16[64,224]{1,0:T(8,128)(2,1)S(1)}, bf16[64,224]{1,0:T(8,128)(2,1)S(1)}, u32[]{:S(2)}, u32[]{:S(2)}) collective-permute-start(bf16[64,224]{1,0:T(8,128)(2,1)S(1)} %get-tuple-element.22), channel_id=1, source_target_pairs={{0,4},{1,5},{2,6},{3,7},{4,12},{5,13},{6,14},{7,15},{8,20},{9,21},... | collective-permute-start | bytes 86024 | tf_op jit(solution)/shard_map/ppermute | solution.py:304
  58.0 13.6 %collective-permute-start.3 = (bf16[64,224]{1,0:T(8,128)(2,1)S(1)}, bf16[64,224]{1,0:T(8,128)(2,1)S(1)}, u32[]{:S(2)}, u32[]{:S(2)}) collective-permute-start(bf16[64,224]{1,0:T(8,128)(2,1)S(1)} %get-tuple-element.22), channel_id=1, source_target_pairs={{0,0},{1,1},{2,2},{3,3},{4,8},{5,9},{6,10},{7,11},{8,16},{9,17},{1... | collective-permute-start | bytes 86024 | tf_op jit(solution)/shard_map/ppermute | solution.py:304
  71.7 10.6 %collective-permute-start.6 = (bf16[144,224]{1,0:T(8,128)(2,1)S(1)}, bf16[144,224]{1,0:T(8,128)(2,1)S(1)}, u32[]{:S(2)}, u32[]{:S(2)}) collective-permute-start(bf16[144,224]{1,0:T(8,128)(2,1)S(1)} %pad_maximum_fusion.near), channel_id=1, source_target_pairs={{0,2},{1,3},{2,0},{3,1},{4,6},{5,7},{6,4},{7,5},{8,10},{9,11},{10,... | collective-permute-start | bytes 193544 | tf_op jit(solution)/shard_map/ppermute | solution.py:304
  75.2 9.1 %collective-permute-start.2 = (bf16[224,128]{1,0:T(8,128)(2,1)S(1)}, bf16[224,128]{1,0:T(8,128)(2,1)S(1)}, u32[]{:S(2)}, u32[]{:S(2)}) collective-permute-start(bf16[224,128]{1,0:T(8,128)(2,1)S(1)} %get-tuple-element.25), channel_id=1, source_target_pairs={{0,2},{1,3},{2,0},{3,1},{4,6},{5,7},{6,4},{7,5},{8,10},{9,11},{10,... | collective-permute-start | bytes 172040 | tf_op jit(solution)/shard_map/ppermute | solution.py:304
  82.4 3.1 %collective-permute-start.7 = (bf16[4,32,224]{2,1,0:T(8,128)(2,1)S(1)}, bf16[4,32,224]{2,1,0:T(8,128)(2,1)S(1)}, u32[]{:S(2)}, u32[]{:S(2)}) collective-permute-start(bf16[4,32,224]{2,1,0:T(8,128)(2,1)S(1)} %get-tuple-element.30.own), channel_id=1, source_target_pairs={{0,1},{1,0},{2,3},{3,2},{4,5},{5,4},{6,7},{7,6},{8,9},{9,8},{10,11... | collective-permute-start | bytes 172040 | tf_op jit(solution)/shard_map/ppermute | solution.py:304
  117.5 11.2 %copy-start.3 = (bf16[1,3,112,128]{3,2,1,0:T(8,128)(2,1)S(1)}, bf16[1,3,112,128]{3,2,1,0:T(8,128)(2,1)}, u32[]{:S(2)}) copy-start(bf16[1,3,112,128]{3,2,1,0:T(8,128)(2,1)} %buffer_out.3) | copy-start | bytes 258052
  117.5 11.2 %copy-start.5 = (bf16[2,112,128]{2,1,0:T(8,128)(2,1)S(1)}, bf16[2,112,128]{2,1,0:T(8,128)(2,1)}, u32[]{:S(2)}) copy-start(bf16[2,112,128]{2,1,0:T(8,128)(2,1)} %get-tuple-element.19.inputs) | copy-start | bytes 172036
  117.5 11.2 %copy-start.10 = (s32[8,2]{0,1:T(2,128)S(1)}, s32[8,2]{0,1:T(2,128)}, u32[]{:S(2)}) copy-start(s32[8,2]{0,1:T(2,128)} %param.15) | copy-start | bytes 196
  117.5 20.3 %copy-start.4 = (bf16[1,3,112,128]{3,2,1,0:T(8,128)(2,1)S(1)}, bf16[1,3,112,128]{3,2,1,0:T(8,128)(2,1)}, u32[]{:S(2)}) copy-start(bf16[1,3,112,128]{3,2,1,0:T(8,128)(2,1)} %buffer_in.3) | copy-start | bytes 258052
  117.5 4.5 %collective-permute-start.8 = (bf16[16,224,128]{2,1,0:T(8,128)(2,1)S(1)}, bf16[16,224,128]{2,1,0:T(8,128)(2,1)S(1)}, u32[]{:S(2)}, u32[]{:S(2)}) collective-permute-start(bf16[16,224,128]{2,1,0:T(8,128)(2,1)S(1)} %bitcast.15), channel_id=1, source_target_pairs={{0,1},{1,0},{2,3},{3,2},{4,5},{5,4},{6,7},{7,6},{8,9},{9,8},{10,11... | collective-permute-start | bytes 2752520 | tf_op jit(solution)/shard_map/ppermute | solution.py:304
  122.6 6.1 %collective-permute-start.9 = (bf16[224,128]{1,0:T(8,128)(2,1)S(1)}, bf16[224,128]{1,0:T(8,128)(2,1)S(1)}, u32[]{:S(2)}, u32[]{:S(2)}) collective-permute-start(bf16[224,128]{1,0:T(8,128)(2,1)S(1)} %get-tuple-element.32), channel_id=1, source_target_pairs={{0,2},{1,3},{2,0},{3,1},{4,6},{5,7},{6,4},{7,5},{8,10},{9,11},{10,... | collective-permute-start | bytes 172040 | tf_op jit(solution)/shard_map/ppermute | solution.py:304
  129.3 8.5 %collective-permute-start.10 = (bf16[2,112,128]{2,1,0:T(8,128)(2,1)S(1)}, bf16[2,112,128]{2,1,0:T(8,128)(2,1)S(1)}, u32[]{:S(2)}, u32[]{:S(2)}) collective-permute-start(bf16[2,112,128]{2,1,0:T(8,128)(2,1)S(1)} %shard_map.156.message), channel_id=1, source_target_pairs={{0,64},{64,128},{128,192},{192,256},{256,320},{320,384},{384,448},... | collective-permute-start | bytes 172040 | tf_op jit(solution)/shard_map/ppermute | solution.py:402

commit v3 on v2

--- a/solution.py
+++ b/solution.py
@@ -15,6 +15,7 @@
 PAY = ROWS + 16
 ZN, YN, CN = 16, 2, 2
 PIECES = 4
+EARLY = 3
 LANES = ("z", "y", "core")
 rope_base = 500000.0
 norm_eps = 1e-05
@@ -52,9 +53,10 @@
 
 
 def prepare(
-    ids, codes, exponents, buffer_in, gain, query, keyval,
-    packed, pay, inputs_out,
-    codes_v, exponents_v, stored_v, gain_v, keyval_v, half_v, keyval_half_v, sems, half_sems,
+    ids, codes, exponents, buffer_in, gain, query, keyval, output,
+    packed, pay_out, inputs_out,
+    codes_v, exponents_v, stored_v, gain_v, keyval_v, half_v, keyval_half_v, early_v, pay, inputs_v,
+    sems, half_sems,
 ):
     section = lax.axis_index("section")
     far = lax.axis_index("y") ^ 1
@@ -70,15 +72,16 @@
         item.start()
 
     step = ZN // PIECES
+    moves = [
+        (query.at[pl.ds(i * step, step), far], half_v.at[i], packed.at[pl.ds(i * step, step)])
+        for i in range(PIECES)
+    ]
+    tail = ZN + keyval_half_v.shape[0]
+    moves.append((output.at[pl.ds(0, EARLY), far], early_v, packed.at[pl.ds(tail, EARLY)]))
     loads, stores = [], []
-    for i in range(PIECES):
-        part = pl.ds(i * step, step)
-        loads.append(
-            pltpu.make_async_copy(query.at[part, far], half_v.at[i], half_sems.at[0, i])
-        )
-        stores.append(
-            pltpu.make_async_copy(half_v.at[i], packed.at[part], half_sems.at[1, i])
-        )
+    for i, (source, between, target) in enumerate(moves):
+        loads.append(pltpu.make_async_copy(source, between, half_sems.at[0, i]))
+        stores.append(pltpu.make_async_copy(between, target, half_sems.at[1, i]))
         loads[-1].start()
     for item in copies[:5]:
         item.wait()
@@ -95,7 +98,7 @@
         )
         stored = stored_v[s].astype(jnp.float32)
         inputs = (stored + codes_v[0, s].astype(jnp.float32) * scales).astype(jnp.bfloat16)
-        inputs_out[s] = inputs
+        inputs_v[s] = inputs
         widened = inputs.astype(jnp.float32)
         pay[s * LEN : (s + 1) * LEN, :] = (widened * gains).astype(jnp.bfloat16)
         squares = widened * widened
@@ -111,6 +114,10 @@
     second = value - first
     tail = jnp.where(row < 2, first, jnp.where(row < 4, second, 0.0))
     pay[ROWS:PAY, :] = tail.astype(jnp.bfloat16)
+    stores.append(pltpu.make_async_copy(pay, pay_out, sems.at[7]))
+    stores[-1].start()
+    stores.append(pltpu.make_async_copy(inputs_v, inputs_out, sems.at[8]))
+    stores[-1].start()
 
     copies[5].wait()
     kv_width = keyval.shape[1]
@@ -169,7 +176,7 @@
     out[...] = acc.astype(jnp.bfloat16)
 
 
-def both_partials(here, there, weight, received):
+def both_partials(here, there, weight, received_rows):
     y, core = lax.axis_index("y"), lax.axis_index("core")
     acc = jnp.zeros((ROWS, 2 * HEAD), jnp.float32)
     for z in range(ZN):
@@ -177,7 +184,7 @@
         parts = []
         for side in (core, core ^ 1):
             mine = weight[0, head_rows(z, y, side), :]
-            other = received[half_rows(z, side), :]
+            other = received_rows(z, side)
             parts.append(jnp.concatenate([mine, other], axis=1))
         part = jnp.concatenate(parts, axis=0)
         acc += jnp.dot(block, part, preferred_element_type=jnp.float32)
@@ -185,7 +192,7 @@
 
 
 def query_kernel(here, there, weight, received, mine_out, other_out):
-    acc = both_partials(here, there, weight, received)
+    acc = both_partials(here, there, weight, lambda z, side: received[half_rows(z, side), :])
     mine_out[...] = acc[:, :HEAD]
     other_out[...] = acc[:, HEAD:].astype(jnp.bfloat16)
 
@@ -247,12 +254,17 @@
 
 def pack_kernel(weight, out):
     far = lax.axis_index("y") ^ 1
-    for z in range(ZN):
-        out[z] = weight[z, far]
-
-
-def output_kernel(here, there, weight, received, mine_out, other_out):
-    acc = both_partials(here, there, weight, received)
+    for z in range(EARLY, ZN):
+        out[z - EARLY] = weight[z, far]
+
+
+def output_kernel(here, there, weight, early, received, mine_out, other_out):
+    def received_rows(z, side):
+        if z < EARLY:
+            return early[half_rows(z, side), :]
+        return received[half_rows(z - EARLY, side), :]
+
+    acc = both_partials(here, there, weight, received_rows)
     mine_out[...] = acc[:, :HEAD]
     other_out[...] = acc[:, HEAD:].astype(jnp.bfloat16)
 
@@ -327,17 +339,18 @@
     partial_flops = 2 * ROWS * half * 256
     wide = shape((ROWS, HEAD), jnp.float32)
 
+    by_half = (ZN, YN, CN * HEAD, HEAD)
     any_spec = pl.BlockSpec(memory_space=pl.ANY)
     bf16, int32 = jnp.bfloat16, jnp.int32
     packed, pay, inputs = pl.pallas_call(
         prepare,
         out_shape=(
-            shape((ZN + ZN * kv_width // HEAD, CN * HEAD, HEAD)),
+            shape((ZN + ZN * kv_width // HEAD + EARLY, CN * HEAD, HEAD)),
             shape((PAY, HEAD)),
             shape((SEQS, LEN, HEAD)),
         ),
-        in_specs=[SMEM] + [any_spec] * 6,
-        out_specs=(any_spec, VMEM, VMEM),
+        in_specs=[SMEM] + [any_spec] * 7,
+        out_specs=(any_spec,) * 3,
         scratch_shapes=[
             pltpu.VMEM(codes.shape, int32),
             pltpu.VMEM(exponents.shape, int32),
@@ -346,21 +359,24 @@
             pltpu.VMEM(w_keyval.shape, bf16),
             pltpu.VMEM((PIECES, ZN // PIECES, CN * HEAD, HEAD), bf16),
             pltpu.VMEM((ZN * kv_width // HEAD, CN * HEAD, HEAD), bf16),
-            pltpu.SemaphoreType.DMA((7,)),
-            pltpu.SemaphoreType.DMA((2, PIECES)),
+            pltpu.VMEM((EARLY, CN * HEAD, HEAD), bf16),
+            pltpu.VMEM((PAY, HEAD), bf16),
+            pltpu.VMEM((SEQS, LEN, HEAD), bf16),
+            pltpu.SemaphoreType.DMA((9,)),
+            pltpu.SemaphoreType.DMA((2, PIECES + 1)),
         ],
         cost_estimate=pl.CostEstimate(flops=10**7, bytes_accessed=4 * 10**6, transcendentals=0),
     )(
         sample_ids, codes, exponents, buffer_in, norm_gain,
-        w_query.reshape(ZN, YN, CN * HEAD, HEAD), w_keyval,
+        w_query.reshape(by_half), w_keyval, w_output.reshape(by_half),
     )
     received = swap(packed, 1, 0).reshape(-1, HEAD)
     here = gather_z(pay)
     there = swap(here, 0, 1)
-    packed_out = call(pack_kernel, shape((ZN, CN * HEAD, HEAD)), 1, 10**6, 2 * 10**6)(
-        w_output.reshape(ZN, YN, CN * HEAD, HEAD)
-    )
-    received_out = swap(packed_out, 1, 0).reshape(half, HEAD)
+    packed_out = call(pack_kernel, shape((ZN - EARLY, CN * HEAD, HEAD)), 1, 10**6, 2 * 10**6)(
+        w_output.reshape(by_half)
+    )
+    received_out = swap(packed_out, 1, 0).reshape(-1, HEAD)
 
     keyval, sums = call(
         keyval_kernel,
@@ -391,8 +407,8 @@
     here = gather_z(context)
     there = swap(here, 0, 1)
     mine, other = call(
-        output_kernel, (wide, shape((ROWS, HEAD))), 4, partial_flops, 6 * 10**6
-    )(here, there, w_output, received_out)
+        output_kernel, (wide, shape((ROWS, HEAD))), 5, partial_flops, 6 * 10**6
+    )(here, there, w_output, received[-EARLY * CN * HEAD :], received_out)
     other = swap(other, 1, 0)
     message = call(
         message_kernel, shape((SEQS, LEN, HEAD)), 5, 10**6, 10**6, smem=(0,)

time: 139 us -> 137 us (0.986)
  waiting for transfers between devices: 26.6 us -> 20.8 us
  blocking collectives: 73.7 us -> 75.5 us
  starting transfers between devices: 27.6 us -> 29.3 us
    ppermute x10, waiting for transfers between devices: 24.1 us -> 18.8 us  [permute(): return lax.ppermute(x, LANES, pairs)]
    all_gather x2, blocking collectives: 73.7 us -> 75.5 us  [gather_z(): return lax.all_gather(x, 'z', axis=0)]
  transfers between devices with their start and end apart: 11 -> 11, of which waited for: 7 -> 6; matrix products, arithmetic and copies ran while one was open for 0% -> 0% of each run, Pallas kernels for 2% -> 2%
where the time goes in v3:
time: 137 us; the launch traced here: 136 us
  blocking collectives  75.5 us (55%)
  starting transfers between devices  29.3 us (21%)
  waiting for transfers between devices  20.8 us (15%)
  Pallas kernels  9.64 us (7%)
    all_gather x2, blocking collectives, gather_z(): return lax.all_gather(x, 'z', axis=0)  75.5 us
    ppermute x10, starting transfers between devices, permute(): return lax.ppermute(x, LANES, pairs)  24 us
    ppermute x10, waiting for transfers between devices, permute(): return lax.ppermute(x, LANES, pairs)  18.8 us
    ppermute x1, starting transfers between devices, per_device(): lax.ppermute(message, 'section', [(i, i + 1) for i in range(sections - 1)])  5.33 us
    pallas_call x1, Pallas kernels, per_device(): pl.pallas_call(prepare, out_shape=(shape((ZN + ZN * kv_width // HEAD + EA...  3.71 us
  transfers between devices with their start and end apart: 11, of which 6 were waited for; matrix products, arithmetic and copies ran while one was open for 0% of the time, Pallas kernels for 2%

profile of v3, /device:TPU:6, one launch (start us, length us, event | category | flops | bytes accessed | tf_op | source)
XLA Modules:
  0.0 136.2 jit_solution(12629738158333541267)
XLA Ops:
  0.6 0.0 copy-start
  0.6 3.7 %shard_map.148 = (bf16[23,256,128]{2,1,0:T(8,128)(2,1)}, bf16[240,128]{1,0:T(8,128)(2,1)}, bf16[2,112,128]{2,1,0:T(8,128)(2,1)}) custom-call(s32[2,8]{1,0:T(2,128)} %bitcast.23, s32[1,2,112,128]{3,2,1,0:T(8,128)} %codes.1, s32[1,2,112]{2,1,0:T(2,128)} %exponents.1, bf16[1,3,112,128]{3,2,1,0:T(8,128)(2,1)} %buffer_in.3, bf16[1,128]{1,0:T(2,128)(2,1)} %gain.1, ...), custom_call_target="tpu_custom_call" | custom-call | flops 10000000 | bytes 4000000 | tf_op jit(solution)/shard_map/pallas_call | solution.py:345
  4.4 0.0 copy-start.2
  4.4 3.6 %collective-permute-start.1 = (bf16[23,256,128]{2,1,0:T(8,128)(2,1)}, bf16[23,256,128]{2,1,0:T(8,128)(2,1)S(1)}, u32[]{:S(2)}, u32[]{:S(2)}) collective-permute-start(bf16[23,256,128]{2,1,0:T(8,128)(2,1)} %get-tuple-element.21), channel_id=1, source_target_pairs={{0,2},{1,3},{2,0},{3,1},{4,6},{5,7},{6,4},{7,5},{8,10},{9,11},{10,... | collective-permute-start | bytes 4521992 | tf_op jit(solution)/shard_map/ppermute | solution.py:316
  8.0 42.2 %all-gather = bf16[3840,128]{1,0:T(8,128)(2,1)S(1)} all-gather(bf16[240,128]{1,0:T(8,128)(2,1)} %get-tuple-element.20), channel_id=2, replica_groups=mesh['section'=8,'z'=16,'y'=2,'core'=2] {'z'}, dimensions={0}, use_global_device_ids=true | all-gather | bytes 1044480 | tf_op jit(solution)/shard_map/all_gather | solution.py:328
  50.2 1.9 %collective-permute-start = (bf16[16,240,128]{2,1,0:T(8,128)(2,1)S(1)}, bf16[16,240,128]{2,1,0:T(8,128)(2,1)S(1)}, u32[]{:S(2)}, u32[]{:S(2)}) collective-permute-start(bf16[16,240,128]{2,1,0:T(8,128)(2,1)S(1)} %bitcast.11), channel_id=1, source_target_pairs={{0,1},{1,0},{2,3},{3,2},{4,5},{5,4},{6,7},{7,6},{8,9},{9,8},{10,11... | collective-permute-start | bytes 2949128 | tf_op jit(solution)/shard_map/ppermute | solution.py:316
  52.1 0.0 copy-done
  52.1 0.1 shard_map.151
  52.2 0.0 copy-start.1
  52.2 2.5 %collective-permute-start.5 = (bf16[13,256,128]{2,1,0:T(8,128)(2,1)S(1)}, bf16[13,256,128]{2,1,0:T(8,128)(2,1)S(1)}, u32[]{:S(2)}, u32[]{:S(2)}) collective-permute-start(bf16[13,256,128]{2,1,0:T(8,128)(2,1)S(1)} %shard_map.151), channel_id=1, source_target_pairs={{0,2},{1,3},{2,0},{3,1},{4,6},{5,7},{6,4},{7,5},{8,10},{9,11},{10,... | collective-permute-start | bytes 2555912 | tf_op jit(solution)/shard_map/ppermute | solution.py:316
  54.7 0.0 collective-permute-done.there
  54.7 0.0 collective-permute-done.1
  54.7 0.0 copy-done.2
  54.7 0.7 shard_map.149
  55.4 0.0 copy-start.8
  55.4 0.0 copy-start.9
  55.4 0.0 copy-start.6
  55.4 0.0 copy-start.7
  55.4 2.1 %collective-permute-start.4 = (bf16[64,224]{1,0:T(8,128)(2,1)S(1)}, bf16[64,224]{1,0:T(8,128)(2,1)S(1)}, u32[]{:S(2)}, u32[]{:S(2)}) collective-permute-start(bf16[64,224]{1,0:T(8,128)(2,1)S(1)} %get-tuple-element.22), channel_id=1, source_target_pairs={{0,4},{1,5},{2,6},{3,7},{4,12},{5,13},{6,14},{7,15},{8,20},{9,21},... | collective-permute-start | bytes 86024 | tf_op jit(solution)/shard_map/ppermute | solution.py:316
  57.5 0.7 collective-permute-start.3
  58.2 0.7 shard_map.150
  58.8 12.2 %collective-permute-done.4 = bf16[64,224]{1,0:T(8,128)(2,1)S(1)} collective-permute-done((bf16[64,224]{1,0:T(8,128)(2,1)S(1)}, bf16[64,224]{1,0:T(8,128)(2,1)S(1)}, u32[]{:S(2)}, u32[]{:S(2)}) %collective-permute-start.4) | collective-permute-done | bytes 28704 | tf_op jit(solution)/shard_map/ppermute | solution.py:316
  71.1 0.0 collective-permute-done.3
  71.1 3.5 %collective-permute-start.6 = (bf16[144,224]{1,0:T(8,128)(2,1)S(1)}, bf16[144,224]{1,0:T(8,128)(2,1)S(1)}, u32[]{:S(2)}, u32[]{:S(2)}) collective-permute-start(bf16[144,224]{1,0:T(8,128)(2,1)S(1)} %pad_maximum_fusion.near), channel_id=1, source_target_pairs={{0,2},{1,3},{2,0},{3,1},{4,6},{5,7},{6,4},{7,5},{8,10},{9,11},{10,... | collective-permute-start | bytes 193544 | tf_op jit(solution)/shard_map/ppermute | solution.py:316
  74.6 2.3 %collective-permute-start.2 = (bf16[224,128]{1,0:T(8,128)(2,1)S(1)}, bf16[224,128]{1,0:T(8,128)(2,1)S(1)}, u32[]{:S(2)}, u32[]{:S(2)}) collective-permute-start(bf16[224,128]{1,0:T(8,128)(2,1)S(1)} %get-tuple-element.25), channel_id=1, source_target_pairs={{0,2},{1,3},{2,0},{3,1},{4,6},{5,7},{6,4},{7,5},{8,10},{9,11},{10,... | collective-permute-start | bytes 172040 | tf_op jit(solution)/shard_map/ppermute | solution.py:316
  77.0 0.0 collective-permute-done.5
  77.0 0.4 collective-permute-done.6.far
  77.4 0.1 shard_map.152
  77.5 1.9 %collective-permute-start.7 = (bf16[4,32,224]{2,1,0:T(8,128)(2,1)S(1)}, bf16[4,32,224]{2,1,0:T(8,128)(2,1)S(1)}, u32[]{:S(2)}, u32[]{:S(2)}) collective-permute-start(bf16[4,32,224]{2,1,0:T(8,128)(2,1)S(1)} %get-tuple-element.30.own), channel_id=1, source_target_pairs={{0,1},{1,0},{2,3},{3,2},{4,5},{5,4},{6,7},{7,6},{8,9},{9,8},{10,11... | collective-permute-start | bytes 172040 | tf_op jit(solution)/shard_map/ppermute | solution.py:316
  79.4 1.3 collective-permute-done.2.other
  80.7 0.0 copy-done.6
  80.7 0.2 shard_map.153.query
  80.9 0.0 collective-permute-done.7.sibling
  81.0 0.5 shard_map.154
  81.5 33.3 %all-gather.1 = bf16[3584,128]{1,0:T(8,128)(2,1)S(1)} all-gather(bf16[224,128]{1,0:T(8,128)(2,1)S(1)} %shard_map.154), channel_id=3, replica_groups=mesh['section'=8,'z'=16,'y'=2,'core'=2] {'z'}, dimensions={0}, use_global_device_ids=true | all-gather | bytes 974848 | tf_op jit(solution)/shard_map/all_gather | solution.py:328
  114.8 1.9 %collective-permute-start.8 = (bf16[16,224,128]{2,1,0:T(8,128)(2,1)S(1)}, bf16[16,224,128]{2,1,0:T(8,128)(2,1)S(1)}, u32[]{:S(2)}, u32[]{:S(2)}) collective-permute-start(bf16[16,224,128]{2,1,0:T(8,128)(2,1)S(1)} %bitcast.17), channel_id=1, source_target_pairs={{0,1},{1,0},{2,3},{3,2},{4,5},{5,4},{6,7},{7,6},{8,9},{9,8},{10,11... | collective-permute-start | bytes 2752520 | tf_op jit(solution)/shard_map/ppermute | solution.py:316
  116.7 2.4 %collective-permute-done.8.there = bf16[16,224,128]{2,1,0:T(8,128)(2,1)S(1)} collective-permute-done((bf16[16,224,128]{2,1,0:T(8,128)(2,1)S(1)}, bf16[16,224,128]{2,1,0:T(8,128)(2,1)S(1)}, u32[]{:S(2)}, u32[]{:S(2)}) %collective-permute-start.8) | collective-permute-done | bytes 917536 | tf_op jit(solution)/shard_map/ppermute | solution.py:316
  119.1 0.7 shard_map.155
  119.8 3.6 %collective-permute-start.9 = (bf16[224,128]{1,0:T(8,128)(2,1)S(1)}, bf16[224,128]{1,0:T(8,128)(2,1)S(1)}, u32[]{:S(2)}, u32[]{:S(2)}) collective-permute-start(bf16[224,128]{1,0:T(8,128)(2,1)S(1)} %get-tuple-element.32), channel_id=1, source_target_pairs={{0,2},{1,3},{2,0},{3,1},{4,6},{5,7},{6,4},{7,5},{8,10},{9,11},{10,... | collective-permute-start | bytes 172040 | tf_op jit(solution)/shard_map/ppermute | solution.py:316
  123.4 2.5 %collective-permute-done.9.other = bf16[224,128]{1,0:T(8,128)(2,1)S(1)} collective-permute-done((bf16[224,128]{1,0:T(8,128)(2,1)S(1)}, bf16[224,128]{1,0:T(8,128)(2,1)S(1)}, u32[]{:S(2)}, u32[]{:S(2)}) %collective-permute-start.9) | collective-permute-done | bytes 57376 | tf_op jit(solution)/shard_map/ppermute | solution.py:316
  125.9 0.0 copy-done.3
  125.9 0.0 copy-done.10
  125.9 0.6 shard_map.156.message
  126.5 5.3 %collective-permute-start.10 = (bf16[2,112,128]{2,1,0:T(8,128)(2,1)S(1)}, bf16[2,112,128]{2,1,0:T(8,128)(2,1)S(1)}, u32[]{:S(2)}, u32[]{:S(2)}) collective-permute-start(bf16[2,112,128]{2,1,0:T(8,128)(2,1)S(1)} %shard_map.156.message), channel_id=1, source_target_pairs={{0,64},{64,128},{128,192},{192,256},{256,320},{320,384},{384,448},... | collective-permute-start | bytes 172040 | tf_op jit(solution)/shard_map/ppermute | solution.py:418
  131.8 1.2 shard_map.158
  133.0 1.9 %collective-permute-done.10.arrived = bf16[2,112,128]{2,1,0:T(8,128)(2,1)S(1)} collective-permute-done((bf16[2,112,128]{2,1,0:T(8,128)(2,1)S(1)}, bf16[2,112,128]{2,1,0:T(8,128)(2,1)S(1)}, u32[]{:S(2)}, u32[]{:S(2)}) %collective-permute-start.10) | collective-permute-done | bytes 57376 | tf_op jit(solution)/shard_map/ppermute | solution.py:418
  134.9 0.0 copy-done.4
  134.9 1.2 shard_map.157
  (11 shorter events, 0.0 us)
Async XLA Ops:
  0.6 51.4 %copy-start = (bf16[1,8192,128]{2,1,0:T(8,128)(2,1)S(1)}, bf16[1,8192,128]{2,1,0:T(8,128)(2,1)}, u32[]{:S(2)}) copy-start(bf16[1,8192,128]{2,1,0:T(8,128)(2,1)} %weight.3) | copy-start | bytes 6291460
  4.4 50.3 %copy-start.2 = (bf16[1,8192,32]{1,2,0:T(8,128)(2,1)S(1)}, bf16[1,8192,32]{1,2,0:T(8,128)(2,1)}, u32[]{:S(2)}) copy-start(bf16[1,8192,32]{1,2,0:T(8,128)(2,1)} %param.20) | copy-start | bytes 1572868
  4.4 50.3 %collective-permute-start.1 = (bf16[23,256,128]{2,1,0:T(8,128)(2,1)}, bf16[23,256,128]{2,1,0:T(8,128)(2,1)S(1)}, u32[]{:S(2)}, u32[]{:S(2)}) collective-permute-start(bf16[23,256,128]{2,1,0:T(8,128)(2,1)} %get-tuple-element.21), channel_id=1, source_target_pairs={{0,2},{1,3},{2,0},{3,1},{4,6},{5,7},{6,4},{7,5},{8,10},{9,11},{10,... | collective-permute-start | bytes 4521992 | tf_op jit(solution)/shard_map/ppermute | solution.py:316
  50.2 4.5 %collective-permute-start = (bf16[16,240,128]{2,1,0:T(8,128)(2,1)S(1)}, bf16[16,240,128]{2,1,0:T(8,128)(2,1)S(1)}, u32[]{:S(2)}, u32[]{:S(2)}) collective-permute-start(bf16[16,240,128]{2,1,0:T(8,128)(2,1)S(1)} %bitcast.11), channel_id=1, source_target_pairs={{0,1},{1,0},{2,3},{3,2},{4,5},{5,4},{6,7},{7,6},{8,9},{9,8},{10,11... | collective-permute-start | bytes 2949128 | tf_op jit(solution)/shard_map/ppermute | solution.py:316
  52.2 6.0 %copy-start.1 = (bf16[1,8192,128]{2,1,0:T(8,128)(2,1)S(1)}, bf16[1,8192,128]{2,1,0:T(8,128)(2,1)}, u32[]{:S(2)}) copy-start(bf16[1,8192,128]{2,1,0:T(8,128)(2,1)} %weight.2) | copy-start | bytes 6291460
  52.2 24.8 %collective-permute-start.5 = (bf16[13,256,128]{2,1,0:T(8,128)(2,1)S(1)}, bf16[13,256,128]{2,1,0:T(8,128)(2,1)S(1)}, u32[]{:S(2)}, u32[]{:S(2)}) collective-permute-start(bf16[13,256,128]{2,1,0:T(8,128)(2,1)S(1)} %shard_map.151), channel_id=1, source_target_pairs={{0,2},{1,3},{2,0},{3,1},{4,6},{5,7},{6,4},{7,5},{8,10},{9,11},{10,... | collective-permute-start | bytes 2555912 | tf_op jit(solution)/shard_map/ppermute | solution.py:316
  55.4 22.0 %copy-start.8 = (f32[64,224]{1,0:T(8,128)S(1)}, f32[64,224]{1,0:T(8,128)}, u32[]{:S(2)}) copy-start(f32[64,224]{1,0:T(8,128)} %constant.8.clone.cos_t) | copy-start | bytes 172036
  55.4 22.0 %copy-start.9 = (f32[64,224]{1,0:T(8,128)S(1)}, f32[64,224]{1,0:T(8,128)}, u32[]{:S(2)}) copy-start(f32[64,224]{1,0:T(8,128)} %constant.9.clone.sin_t) | copy-start | bytes 172036
  55.4 25.3 %copy-start.6 = (f32[224,64]{1,0:T(8,128)S(1)}, f32[224,64]{1,0:T(8,128)}, u32[]{:S(2)}) copy-start(f32[224,64]{1,0:T(8,128)} %constant.10.clone.cos) | copy-start | bytes 172036
  55.4 25.3 %copy-start.7 = (f32[224,64]{1,0:T(8,128)S(1)}, f32[224,64]{1,0:T(8,128)}, u32[]{:S(2)}) copy-start(f32[224,64]{1,0:T(8,128)} %constant.11.clone.sin) | copy-start | bytes 172036
  55.4 15.7 %collective-permute-start.4 = (bf16[64,224]{1,0:T(8,128)(2,1)S(1)}, bf16[64,224]{1,0:T(8,128)(2,1)S(1)}, u32[]{:S(2)}, u32[]{:S(2)}) collective-permute-start(bf16[64,224]{1,0:T(8,128)(2,1)S(1)} %get-tuple-element.22), channel_id=1, source_target_pairs={{0,4},{1,5},{2,6},{3,7},{4,12},{5,13},{6,14},{7,15},{8,20},{9,21},... | collective-permute-start | bytes 86024 | tf_op jit(solution)/shard_map/ppermute | solution.py:316
  57.5 13.6 %collective-permute-start.3 = (bf16[64,224]{1,0:T(8,128)(2,1)S(1)}, bf16[64,224]{1,0:T(8,128)(2,1)S(1)}, u32[]{:S(2)}, u32[]{:S(2)}) collective-permute-start(bf16[64,224]{1,0:T(8,128)(2,1)S(1)} %get-tuple-element.22), channel_id=1, source_target_pairs={{0,0},{1,1},{2,2},{3,3},{4,8},{5,9},{6,10},{7,11},{8,16},{9,17},{1... | collective-permute-start | bytes 86024 | tf_op jit(solution)/shard_map/ppermute | solution.py:316
  71.1 6.2 %collective-permute-start.6 = (bf16[144,224]{1,0:T(8,128)(2,1)S(1)}, bf16[144,224]{1,0:T(8,128)(2,1)S(1)}, u32[]{:S(2)}, u32[]{:S(2)}) collective-permute-start(bf16[144,224]{1,0:T(8,128)(2,1)S(1)} %pad_maximum_fusion.near), channel_id=1, source_target_pairs={{0,2},{1,3},{2,0},{3,1},{4,6},{5,7},{6,4},{7,5},{8,10},{9,11},{10,... | collective-permute-start | bytes 193544 | tf_op jit(solution)/shard_map/ppermute | solution.py:316
  74.6 6.1 %collective-permute-start.2 = (bf16[224,128]{1,0:T(8,128)(2,1)S(1)}, bf16[224,128]{1,0:T(8,128)(2,1)S(1)}, u32[]{:S(2)}, u32[]{:S(2)}) collective-permute-start(bf16[224,128]{1,0:T(8,128)(2,1)S(1)} %get-tuple-element.25), channel_id=1, source_target_pairs={{0,2},{1,3},{2,0},{3,1},{4,6},{5,7},{6,4},{7,5},{8,10},{9,11},{10,... | collective-permute-start | bytes 172040 | tf_op jit(solution)/shard_map/ppermute | solution.py:316
  77.5 3.5 %collective-permute-start.7 = (bf16[4,32,224]{2,1,0:T(8,128)(2,1)S(1)}, bf16[4,32,224]{2,1,0:T(8,128)(2,1)S(1)}, u32[]{:S(2)}, u32[]{:S(2)}) collective-permute-start(bf16[4,32,224]{2,1,0:T(8,128)(2,1)S(1)} %get-tuple-element.30.own), channel_id=1, source_target_pairs={{0,1},{1,0},{2,3},{3,2},{4,5},{5,4},{6,7},{7,6},{8,9},{9,8},{10,11... | collective-permute-start | bytes 172040 | tf_op jit(solution)/shard_map/ppermute | solution.py:316
  114.8 4.4 %collective-permute-start.8 = (bf16[16,224,128]{2,1,0:T(8,128)(2,1)S(1)}, bf16[16,224,128]{2,1,0:T(8,128)(2,1)S(1)}, u32[]{:S(2)}, u32[]{:S(2)}) collective-permute-start(bf16[16,224,128]{2,1,0:T(8,128)(2,1)S(1)} %bitcast.17), channel_id=1, source_target_pairs={{0,1},{1,0},{2,3},{3,2},{4,5},{5,4},{6,7},{7,6},{8,9},{9,8},{10,11... | collective-permute-start | bytes 2752520 | tf_op jit(solution)/shard_map/ppermute | solution.py:316
  119.1 6.8 %copy-start.3 = (bf16[1,3,112,128]{3,2,1,0:T(8,128)(2,1)S(1)}, bf16[1,3,112,128]{3,2,1,0:T(8,128)(2,1)}, u32[]{:S(2)}) copy-start(bf16[1,3,112,128]{3,2,1,0:T(8,128)(2,1)} %buffer_out.3) | copy-start | bytes 258052
  119.1 6.8 %copy-start.5 = (bf16[2,112,128]{2,1,0:T(8,128)(2,1)S(1)}, bf16[2,112,128]{2,1,0:T(8,128)(2,1)}, u32[]{:S(2)}) copy-start(bf16[2,112,128]{2,1,0:T(8,128)(2,1)} %get-tuple-element.19.inputs) | copy-start | bytes 172036
  119.1 6.8 %copy-start.10 = (s32[8,2]{0,1:T(2,128)S(1)}, s32[8,2]{0,1:T(2,128)}, u32[]{:S(2)}) copy-start(s32[8,2]{0,1:T(2,128)} %param.15) | copy-start | bytes 196
  119.1 15.8 %copy-start.4 = (bf16[1,3,112,128]{3,2,1,0:T(8,128)(2,1)S(1)}, bf16[1,3,112,128]{3,2,1,0:T(8,128)(2,1)}, u32[]{:S(2)}) copy-start(bf16[1,3,112,128]{3,2,1,0:T(8,128)(2,1)} %buffer_in.3) | copy-start | bytes 258052
  119.8 6.1 %collective-permute-start.9 = (bf16[224,128]{1,0:T(8,128)(2,1)S(1)}, bf16[224,128]{1,0:T(8,128)(2,1)S(1)}, u32[]{:S(2)}, u32[]{:S(2)}) collective-permute-start(bf16[224,128]{1,0:T(8,128)(2,1)S(1)} %get-tuple-element.32), channel_id=1, source_target_pairs={{0,2},{1,3},{2,0},{3,1},{4,6},{5,7},{6,4},{7,5},{8,10},{9,11},{10,... | collective-permute-start | bytes 172040 | tf_op jit(solution)/shard_map/ppermute | solution.py:316
  126.5 8.5 %collective-permute-start.10 = (bf16[2,112,128]{2,1,0:T(8,128)(2,1)S(1)}, bf16[2,112,128]{2,1,0:T(8,128)(2,1)S(1)}, u32[]{:S(2)}, u32[]{:S(2)}) collective-permute-start(bf16[2,112,128]{2,1,0:T(8,128)(2,1)S(1)} %shard_map.156.message), channel_id=1, source_target_pairs={{0,64},{64,128},{128,192},{192,256},{256,320},{320,384},{384,448},... | collective-permute-start | bytes 172040 | tf_op jit(solution)/shard_map/ppermute | solution.py:418

commit v4 on v2

--- a/solution.py
+++ b/solution.py
@@ -53,8 +53,9 @@
 
 def prepare(
     ids, codes, exponents, buffer_in, gain, query, keyval,
-    packed, pay, inputs_out,
-    codes_v, exponents_v, stored_v, gain_v, keyval_v, half_v, keyval_half_v, sems, half_sems,
+    packed, pay_out, inputs_out,
+    codes_v, exponents_v, stored_v, gain_v, keyval_v, half_v, keyval_half_v, pay, inputs_v,
+    sems, half_sems,
 ):
     section = lax.axis_index("section")
     far = lax.axis_index("y") ^ 1
@@ -70,15 +71,14 @@
         item.start()
 
     step = ZN // PIECES
+    moves = [
+        (query.at[pl.ds(i * step, step), far], half_v.at[i], packed.at[pl.ds(i * step, step)])
+        for i in range(PIECES)
+    ]
     loads, stores = [], []
-    for i in range(PIECES):
-        part = pl.ds(i * step, step)
-        loads.append(
-            pltpu.make_async_copy(query.at[part, far], half_v.at[i], half_sems.at[0, i])
-        )
-        stores.append(
-            pltpu.make_async_copy(half_v.at[i], packed.at[part], half_sems.at[1, i])
-        )
+    for i, (source, between, target) in enumerate(moves):
+        loads.append(pltpu.make_async_copy(source, between, half_sems.at[0, i]))
+        stores.append(pltpu.make_async_copy(between, target, half_sems.at[1, i]))
         loads[-1].start()
     for item in copies[:5]:
         item.wait()
@@ -95,7 +95,7 @@
         )
         stored = stored_v[s].astype(jnp.float32)
         inputs = (stored + codes_v[0, s].astype(jnp.float32) * scales).astype(jnp.bfloat16)
-        inputs_out[s] = inputs
+        inputs_v[s] = inputs
         widened = inputs.astype(jnp.float32)
         pay[s * LEN : (s + 1) * LEN, :] = (widened * gains).astype(jnp.bfloat16)
         squares = widened * widened
@@ -111,6 +111,10 @@
     second = value - first
     tail = jnp.where(row < 2, first, jnp.where(row < 4, second, 0.0))
     pay[ROWS:PAY, :] = tail.astype(jnp.bfloat16)
+    stores.append(pltpu.make_async_copy(pay, pay_out, sems.at[7]))
+    stores[-1].start()
+    stores.append(pltpu.make_async_copy(inputs_v, inputs_out, sems.at[8]))
+    stores[-1].start()
 
     copies[5].wait()
     kv_width = keyval.shape[1]
@@ -191,27 +195,25 @@
 
 
 def sum_kernel(near, far, cos_t, sin_t, out, factors_out):
-    z_odd, y, core = lax.axis_index("z") % 2, lax.axis_index("y"), lax.axis_index("core")
-    width = (near.shape[0] - (PAY - ROWS)) // 4
-    tail = near[4 * width :, :].astype(jnp.float32) + far[4 * width :, :].astype(jnp.float32)
+    even, y, core = lax.axis_index("z") % 2 == 0, lax.axis_index("y"), lax.axis_index("core")
+    width = (near.shape[0] - (PAY - ROWS)) // 2
+    tail = near[2 * width :, :].astype(jnp.float32) + far[2 * width :, :].astype(jnp.float32)
     square_sum = tail[0:1, :] + tail[1:2, :]
     inverse = lax.rsqrt(square_sum / (ZN * YN * CN * HEAD) + norm_eps)
     factors = jnp.broadcast_to(inverse, (width, ROWS))
     factors_out[...] = jnp.broadcast_to(inverse, (HEAD, ROWS)).T
 
-    def piece(kind, which):
-        plane = z_odd ^ kind
-        a = near[pl.ds(pl.multiple_of((plane * 2 + (which ^ y)) * width, width), width), :]
-        b = far[pl.ds(pl.multiple_of((plane * 2 + 1 - (which ^ y)) * width, width), width), :]
-        return ((a.astype(jnp.float32) + b.astype(jnp.float32)) * factors).astype(jnp.bfloat16)
-
-    first, second = piece(0, 0).astype(jnp.float32), piece(0, 1).astype(jnp.float32)
+    def piece(which):
+        a = near[pl.ds(pl.multiple_of((which ^ y) * width, width), width), :]
+        b = far[pl.ds(pl.multiple_of((1 - (which ^ y)) * width, width), width), :]
+        total = (a.astype(jnp.float32) + b.astype(jnp.float32)) * factors
+        return total.astype(jnp.bfloat16).astype(jnp.float32)
+
+    first, second = piece(0), piece(1)
     rows = pl.ds(pl.multiple_of(core * width, width), width)
     c, s = cos_t[rows, :], sin_t[rows, :]
-    out[0] = (first * c - second * s).astype(jnp.bfloat16)
-    out[1] = (second * c + first * s).astype(jnp.bfloat16)
-    out[2] = piece(1, 0)
-    out[3] = piece(1, 1)
+    out[0] = jnp.where(even, first * c - second * s, first).astype(jnp.bfloat16)
+    out[1] = jnp.where(even, second * c + first * s, second).astype(jnp.bfloat16)
 
 
 def rope_kernel(mine, other, factors, cos, sin, out):
@@ -224,15 +226,16 @@
 
 
 def attention_kernel(query, own, sibling, out):
-    core = lax.axis_index("core")
-    keys_values = []
-    for kind in range(2):
+    even, core = lax.axis_index("z") % 2 == 0, lax.axis_index("core")
+    planes = []
+    for plane in range(2):
         parts = []
         for which in range(2):
-            a, b = own[2 * kind + which], sibling[2 * kind + which]
+            a, b = own[plane, which], sibling[plane, which]
             parts += [jnp.where(core == 0, a, b), jnp.where(core == 0, b, a)]
-        keys_values.append(jnp.concatenate(parts, axis=0))
-    keys, values = keys_values
+        planes.append(jnp.concatenate(parts, axis=0))
+    keys = jnp.where(even, planes[0], planes[1])
+    values = jnp.where(even, planes[1], planes[0])
     scores = jnp.dot(query[...], keys, preferred_element_type=jnp.float32) / math.sqrt(HEAD)
     row = lax.broadcasted_iota(jnp.int32, (ROWS, ROWS), 0)
     column = lax.broadcasted_iota(jnp.int32, (ROWS, ROWS), 1)
@@ -327,6 +330,7 @@
     partial_flops = 2 * ROWS * half * 256
     wide = shape((ROWS, HEAD), jnp.float32)
 
+    by_half = (ZN, YN, CN * HEAD, HEAD)
     any_spec = pl.BlockSpec(memory_space=pl.ANY)
     bf16, int32 = jnp.bfloat16, jnp.int32
     packed, pay, inputs = pl.pallas_call(
@@ -337,7 +341,7 @@
             shape((SEQS, LEN, HEAD)),
         ),
         in_specs=[SMEM] + [any_spec] * 6,
-        out_specs=(any_spec, VMEM, VMEM),
+        out_specs=(any_spec,) * 3,
         scratch_shapes=[
             pltpu.VMEM(codes.shape, int32),
             pltpu.VMEM(exponents.shape, int32),
@@ -346,21 +350,22 @@
             pltpu.VMEM(w_keyval.shape, bf16),
             pltpu.VMEM((PIECES, ZN // PIECES, CN * HEAD, HEAD), bf16),
             pltpu.VMEM((ZN * kv_width // HEAD, CN * HEAD, HEAD), bf16),
-            pltpu.SemaphoreType.DMA((7,)),
+            pltpu.VMEM((PAY, HEAD), bf16),
+            pltpu.VMEM((SEQS, LEN, HEAD), bf16),
+            pltpu.SemaphoreType.DMA((9,)),
             pltpu.SemaphoreType.DMA((2, PIECES)),
         ],
         cost_estimate=pl.CostEstimate(flops=10**7, bytes_accessed=4 * 10**6, transcendentals=0),
     )(
         sample_ids, codes, exponents, buffer_in, norm_gain,
-        w_query.reshape(ZN, YN, CN * HEAD, HEAD), w_keyval,
+        w_query.reshape(by_half), w_keyval,
     )
     received = swap(packed, 1, 0).reshape(-1, HEAD)
     here = gather_z(pay)
     there = swap(here, 0, 1)
     packed_out = call(pack_kernel, shape((ZN, CN * HEAD, HEAD)), 1, 10**6, 2 * 10**6)(
-        w_output.reshape(ZN, YN, CN * HEAD, HEAD)
-    )
-    received_out = swap(packed_out, 1, 0).reshape(half, HEAD)
+        w_output.reshape(by_half)
+    )
 
     keyval, sums = call(
         keyval_kernel,
@@ -369,17 +374,18 @@
         partial_flops,
         5 * 10**6,
     )(here, there, w_keyval, received)
-    even = permute(keyval, lambda z, y, c: (2 * z if z < 8 else 2 * (z - 8) + 1, y, c))
-    odd = permute(keyval, lambda z, y, c: (2 * z + 1 if z < 8 else 2 * (z - 8), y, c))
+    keyval = permute(keyval, lambda z, y, c: (2 * z if z < 8 else 2 * (z - 8) + 1, y, c))
     mine, other = call(
         query_kernel, (wide, shape((ROWS, HEAD))), 4, partial_flops, 6 * 10**6
-    )(here, there, w_query, after(received, keyval))
+    )(here, there, w_query, after(received, sums))
     other = swap(other, 1, 0)
-    near = after(jnp.concatenate([even, odd, sums]), mine)
+    near = after(jnp.concatenate([keyval, sums]), other)
     far = swap(near, 1, 0)
+    received_out = swap(after(packed_out, near), 1, 0).reshape(half, HEAD)
     own, factors = call(
-        sum_kernel, (shape((4, kv_width, ROWS)), wide), 4, 10**6, 10**6
-    )(after(near, received_out), far, cos.T.copy(), sin.T.copy())
+        sum_kernel, (shape((2, kv_width, ROWS)), wide), 4, 10**6, 10**6
+    )(near, far, cos.T.copy(), sin.T.copy())
+    own = jnp.stack([own, permute(own, lambda z, y, c: (z ^ 1, y, c))])
     sibling = swap(own, 0, 1)
     queries = call(rope_kernel, shape((ROWS, HEAD)), 5, 10**6, 10**6)(
         mine, other, factors, cos, sin

time: 139 us -> 139 us (level)
  waiting for transfers between devices: 26.6 us -> 18.8 us
  starting transfers between devices: 27.6 us -> 33.7 us
  blocking collectives: 73.7 us -> 75.7 us
    ppermute x10, waiting for transfers between devices: 24.1 us -> 16.6 us  [permute(): return lax.ppermute(x, LANES, pairs)]
    ppermute x10, starting transfers between devices: 22.8 us -> 28.6 us  [permute(): return lax.ppermute(x, LANES, pairs)]
    all_gather x2, blocking collectives: 73.7 us -> 75.7 us  [gather_z(): return lax.all_gather(x, 'z', axis=0)]
where the time goes in v4:
time: 139 us
  blocking collectives  75.7 us (54%)
  starting transfers between devices  33.7 us (24%)
  waiting for transfers between devices  18.8 us (14%)
  Pallas kernels  9.55 us (7%)
    all_gather x2, blocking collectives, gather_z(): return lax.all_gather(x, 'z', axis=0)  75.7 us
    ppermute x10, starting transfers between devices, permute(): return lax.ppermute(x, LANES, pairs)  28.6 us
    ppermute x10, waiting for transfers between devices, permute(): return lax.ppermute(x, LANES, pairs)  16.6 us
    ppermute x1, starting transfers between devices, per_device(): lax.ppermute(message, 'section', [(i, i + 1) for i in range(sections - 1)])  5.11 us
    pallas_call x1, Pallas kernels, per_device(): pl.pallas_call(prepare, out_shape=(shape((ZN + ZN * kv_width // HEAD, CN...  3.59 us
  transfers between devices with their start and end apart: 11, of which 7 were waited for; matrix products, arithmetic and copies ran while one was open for 0% of the time, Pallas kernels for 2%

profile of v4, /device:TPU:6, one launch (start us, length us, event | category | flops | bytes accessed | tf_op | source)
XLA Modules:
  0.0 138.7 jit_solution(12596355647867478527)
XLA Ops:
  0.6 0.0 copy-start.2
  0.6 3.6 %shard_map.148 = (bf16[20,256,128]{2,1,0:T(8,128)(2,1)}, bf16[240,128]{1,0:T(8,128)(2,1)}, bf16[2,112,128]{2,1,0:T(8,128)(2,1)}) custom-call(s32[2,8]{1,0:T(2,128)} %bitcast.23, s32[1,2,112,128]{3,2,1,0:T(8,128)} %codes.1, s32[1,2,112]{2,1,0:T(2,128)} %exponents.1, bf16[1,3,112,128]{3,2,1,0:T(8,128)(2,1)} %buffer_in.3, bf16[1,128]{1,0:T(2,128)(2,1)} %gain.1, ...), custom_call_target="tpu_custom_call" | custom-call | flops 10000000 | bytes 4000000 | tf_op jit(solution)/shard_map/pallas_call | solution.py:336
  4.2 3.5 %collective-permute-start.1 = (bf16[20,256,128]{2,1,0:T(8,128)(2,1)}, bf16[20,256,128]{2,1,0:T(8,128)(2,1)S(1)}, u32[]{:S(2)}, u32[]{:S(2)}) collective-permute-start(bf16[20,256,128]{2,1,0:T(8,128)(2,1)} %get-tuple-element.21), channel_id=1, source_target_pairs={{0,2},{1,3},{2,0},{3,1},{4,6},{5,7},{6,4},{7,5},{8,10},{9,11},{10,... | collective-permute-start | bytes 3932168 | tf_op jit(solution)/shard_map/ppermute | solution.py:307
  7.7 42.2 %all-gather = bf16[3840,128]{1,0:T(8,128)(2,1)S(1)} all-gather(bf16[240,128]{1,0:T(8,128)(2,1)} %get-tuple-element.20), channel_id=2, replica_groups=mesh['section'=8,'z'=16,'y'=2,'core'=2] {'z'}, dimensions={0}, use_global_device_ids=true | all-gather | bytes 1044480 | tf_op jit(solution)/shard_map/all_gather | solution.py:319
  49.9 2.0 %collective-permute-start = (bf16[16,240,128]{2,1,0:T(8,128)(2,1)S(1)}, bf16[16,240,128]{2,1,0:T(8,128)(2,1)S(1)}, u32[]{:S(2)}, u32[]{:S(2)}) collective-permute-start(bf16[16,240,128]{2,1,0:T(8,128)(2,1)S(1)} %bitcast.10), channel_id=1, source_target_pairs={{0,1},{1,0},{2,3},{3,2},{4,5},{5,4},{6,7},{7,6},{8,9},{9,8},{10,11... | collective-permute-start | bytes 2949128 | tf_op jit(solution)/shard_map/ppermute | solution.py:307
  51.9 2.5 %collective-permute-done.there = bf16[16,240,128]{2,1,0:T(8,128)(2,1)S(1)} collective-permute-done((bf16[16,240,128]{2,1,0:T(8,128)(2,1)S(1)}, bf16[16,240,128]{2,1,0:T(8,128)(2,1)S(1)}, u32[]{:S(2)}, u32[]{:S(2)}) %collective-permute-start) | collective-permute-done | bytes 983072 | tf_op jit(solution)/shard_map/ppermute | solution.py:307
  54.5 0.0 collective-permute-done.1
  54.5 0.0 copy-done.2
  54.5 0.7 shard_map.149
  55.2 0.0 copy-start.8
  55.2 0.0 copy-start.9
  55.2 0.0 copy-start
  55.2 0.8 collective-permute-start.3
  56.0 0.0 copy-done.1
  56.0 0.7 shard_map.150
  56.7 0.0 copy-start.6
  56.7 0.0 copy-start.7
  56.7 2.5 %collective-permute-start.2 = (bf16[224,128]{1,0:T(8,128)(2,1)S(1)}, bf16[224,128]{1,0:T(8,128)(2,1)S(1)}, u32[]{:S(2)}, u32[]{:S(2)}) collective-permute-start(bf16[224,128]{1,0:T(8,128)(2,1)S(1)} %get-tuple-element.25), channel_id=1, source_target_pairs={{0,2},{1,3},{2,0},{3,1},{4,6},{5,7},{6,4},{7,5},{8,10},{9,11},{10,... | collective-permute-start | bytes 172040 | tf_op jit(solution)/shard_map/ppermute | solution.py:307
  59.2 0.0 collective-permute-done.3
  59.2 3.7 %collective-permute-done.2.other = bf16[224,128]{1,0:T(8,128)(2,1)S(1)} collective-permute-done((bf16[224,128]{1,0:T(8,128)(2,1)S(1)}, bf16[224,128]{1,0:T(8,128)(2,1)S(1)}, u32[]{:S(2)}, u32[]{:S(2)}) %collective-permute-start.2) | collective-permute-done | bytes 57376 | tf_op jit(solution)/shard_map/ppermute | solution.py:307
  62.9 2.3 %collective-permute-start.4 = (bf16[80,224]{1,0:T(8,128)(2,1)S(1)}, bf16[80,224]{1,0:T(8,128)(2,1)S(1)}, u32[]{:S(2)}, u32[]{:S(2)}) collective-permute-start(bf16[80,224]{1,0:T(8,128)(2,1)S(1)} %pad_maximum_fusion.1.near), channel_id=1, source_target_pairs={{0,2},{1,3},{2,0},{3,1},{4,6},{5,7},{6,4},{7,5},{8,10},{9,11},{10,... | collective-permute-start | bytes 107528 | tf_op jit(solution)/shard_map/ppermute | solution.py:307
  65.3 3.5 %collective-permute-done.4.far = bf16[80,224]{1,0:T(8,128)(2,1)S(1)} collective-permute-done((bf16[80,224]{1,0:T(8,128)(2,1)S(1)}, bf16[80,224]{1,0:T(8,128)(2,1)S(1)}, u32[]{:S(2)}, u32[]{:S(2)}) %collective-permute-start.4) | collective-permute-done | bytes 35872 | tf_op jit(solution)/shard_map/ppermute | solution.py:307
  68.8 0.0 copy-done.8
  68.8 0.0 copy-done.9
  68.8 0.1 shard_map.151
  68.9 7.8 %collective-permute-start.5 = (bf16[2,32,224]{2,1,0:T(8,128)(2,1)S(1)}, bf16[2,32,224]{2,1,0:T(8,128)(2,1)S(1)}, u32[]{:S(2)}, u32[]{:S(2)}) collective-permute-start(bf16[2,32,224]{2,1,0:T(8,128)(2,1)S(1)} %get-tuple-element.29), channel_id=1, source_target_pairs={{0,4},{1,5},{2,6},{3,7},{4,0},{5,1},{6,2},{7,3},{8,12},{9,13},{10,... | collective-permute-start | bytes 86024 | tf_op jit(solution)/shard_map/ppermute | solution.py:307
  76.7 1.9 %collective-permute-done.5 = bf16[2,32,224]{2,1,0:T(8,128)(2,1)S(1)} collective-permute-done((bf16[2,32,224]{2,1,0:T(8,128)(2,1)S(1)}, bf16[2,32,224]{2,1,0:T(8,128)(2,1)S(1)}, u32[]{:S(2)}, u32[]{:S(2)}) %collective-permute-start.5) | collective-permute-done | bytes 28704 | tf_op jit(solution)/shard_map/ppermute | solution.py:307
  78.6 1.9 %collective-permute-start.6 = (bf16[2,2,32,224]{3,2,1,0:T(8,128)(2,1)S(1)}, bf16[2,2,32,224]{3,2,1,0:T(8,128)(2,1)S(1)}, u32[]{:S(2)}, u32[]{:S(2)}) collective-permute-start(bf16[2,2,32,224]{3,2,1,0:T(8,128)(2,1)S(1)} %pad_maximum_fusion.own), channel_id=1, source_target_pairs={{0,1},{1,0},{2,3},{3,2},{4,5},{5,4},{6,7},{7,6},{8,9},{9,8},{10,11... | collective-permute-start | bytes 172040 | tf_op jit(solution)/shard_map/ppermute | solution.py:307
  80.5 0.0 copy-done
  80.5 0.1 shard_map.154
  80.6 2.4 %collective-permute-start.8 = (bf16[16,256,128]{2,1,0:T(8,128)(2,1)S(1)}, bf16[16,256,128]{2,1,0:T(8,128)(2,1)S(1)}, u32[]{:S(2)}, u32[]{:S(2)}) collective-permute-start(bf16[16,256,128]{2,1,0:T(8,128)(2,1)S(1)} %shard_map.154), channel_id=1, source_target_pairs={{0,2},{1,3},{2,0},{3,1},{4,6},{5,7},{6,4},{7,5},{8,10},{9,11},{10,... | collective-permute-start | bytes 3145736 | tf_op jit(solution)/shard_map/ppermute | solution.py:307
  83.0 0.0 copy-done.6
  83.0 0.2 shard_map.152.query
  83.2 0.0 collective-permute-done.6.sibling
  83.3 0.5 shard_map.153
  83.8 33.5 %all-gather.1 = bf16[3584,128]{1,0:T(8,128)(2,1)S(1)} all-gather(bf16[224,128]{1,0:T(8,128)(2,1)S(1)} %shard_map.153), channel_id=3, replica_groups=mesh['section'=8,'z'=16,'y'=2,'core'=2] {'z'}, dimensions={0}, use_global_device_ids=true | all-gather | bytes 974848 | tf_op jit(solution)/shard_map/all_gather | solution.py:319
  117.3 1.9 %collective-permute-start.7 = (bf16[16,224,128]{2,1,0:T(8,128)(2,1)S(1)}, bf16[16,224,128]{2,1,0:T(8,128)(2,1)S(1)}, u32[]{:S(2)}, u32[]{:S(2)}) collective-permute-start(bf16[16,224,128]{2,1,0:T(8,128)(2,1)S(1)} %bitcast.17), channel_id=1, source_target_pairs={{0,1},{1,0},{2,3},{3,2},{4,5},{5,4},{6,7},{7,6},{8,9},{9,8},{10,11... | collective-permute-start | bytes 2752520 | tf_op jit(solution)/shard_map/ppermute | solution.py:307
  119.2 2.4 %collective-permute-done.7.there = bf16[16,224,128]{2,1,0:T(8,128)(2,1)S(1)} collective-permute-done((bf16[16,224,128]{2,1,0:T(8,128)(2,1)S(1)}, bf16[16,224,128]{2,1,0:T(8,128)(2,1)S(1)}, u32[]{:S(2)}, u32[]{:S(2)}) %collective-permute-start.7) | collective-permute-done | bytes 917536 | tf_op jit(solution)/shard_map/ppermute | solution.py:307
  121.6 0.0 collective-permute-done.8
  121.7 0.0 copy-start.4
  121.7 0.7 shard_map.155
  122.4 3.5 %collective-permute-start.9 = (bf16[224,128]{1,0:T(8,128)(2,1)S(1)}, bf16[224,128]{1,0:T(8,128)(2,1)S(1)}, u32[]{:S(2)}, u32[]{:S(2)}) collective-permute-start(bf16[224,128]{1,0:T(8,128)(2,1)S(1)} %get-tuple-element.32), channel_id=1, source_target_pairs={{0,2},{1,3},{2,0},{3,1},{4,6},{5,7},{6,4},{7,5},{8,10},{9,11},{10,... | collective-permute-start | bytes 172040 | tf_op jit(solution)/shard_map/ppermute | solution.py:307
  125.9 2.6 %collective-permute-done.9.other = bf16[224,128]{1,0:T(8,128)(2,1)S(1)} collective-permute-done((bf16[224,128]{1,0:T(8,128)(2,1)S(1)}, bf16[224,128]{1,0:T(8,128)(2,1)S(1)}, u32[]{:S(2)}, u32[]{:S(2)}) %collective-permute-start.9) | collective-permute-done | bytes 57376 | tf_op jit(solution)/shard_map/ppermute | solution.py:307
  128.4 0.6 shard_map.156.message
  129.0 5.1 %collective-permute-start.10 = (bf16[2,112,128]{2,1,0:T(8,128)(2,1)S(1)}, bf16[2,112,128]{2,1,0:T(8,128)(2,1)S(1)}, u32[]{:S(2)}, u32[]{:S(2)}) collective-permute-start(bf16[2,112,128]{2,1,0:T(8,128)(2,1)S(1)} %shard_map.156.message), channel_id=1, source_target_pairs={{0,64},{64,128},{128,192},{192,256},{256,320},{320,384},{384,448},... | collective-permute-start | bytes 172040 | tf_op jit(solution)/shard_map/ppermute | solution.py:408
  134.1 1.2 shard_map.158
  135.4 2.1 %collective-permute-done.10.arrived = bf16[2,112,128]{2,1,0:T(8,128)(2,1)S(1)} collective-permute-done((bf16[2,112,128]{2,1,0:T(8,128)(2,1)S(1)}, bf16[2,112,128]{2,1,0:T(8,128)(2,1)S(1)}, u32[]{:S(2)}, u32[]{:S(2)}) %collective-permute-start.10) | collective-permute-done | bytes 57376 | tf_op jit(solution)/shard_map/ppermute | solution.py:408
  137.5 1.2 shard_map.157
  (11 shorter events, 0.0 us)
Async XLA Ops:
  0.6 53.8 %copy-start.2 = (bf16[1,8192,32]{1,2,0:T(8,128)(2,1)S(1)}, bf16[1,8192,32]{1,2,0:T(8,128)(2,1)}, u32[]{:S(2)}) copy-start(bf16[1,8192,32]{1,2,0:T(8,128)(2,1)} %param.20) | copy-start | bytes 1572868
  4.2 50.2 %collective-permute-start.1 = (bf16[20,256,128]{2,1,0:T(8,128)(2,1)}, bf16[20,256,128]{2,1,0:T(8,128)(2,1)S(1)}, u32[]{:S(2)}, u32[]{:S(2)}) collective-permute-start(bf16[20,256,128]{2,1,0:T(8,128)(2,1)} %get-tuple-element.21), channel_id=1, source_target_pairs={{0,2},{1,3},{2,0},{3,1},{4,6},{5,7},{6,4},{7,5},{8,10},{9,11},{10,... | collective-permute-start | bytes 3932168 | tf_op jit(solution)/shard_map/ppermute | solution.py:307
  49.9 6.1 %copy-start.1 = (bf16[1,8192,128]{2,1,0:T(8,128)(2,1)S(1)}, bf16[1,8192,128]{2,1,0:T(8,128)(2,1)}, u32[]{:S(2)}) copy-start(bf16[1,8192,128]{2,1,0:T(8,128)(2,1)} %weight.2) | copy-start | bytes 6291460
  49.9 4.6 %collective-permute-start = (bf16[16,240,128]{2,1,0:T(8,128)(2,1)S(1)}, bf16[16,240,128]{2,1,0:T(8,128)(2,1)S(1)}, u32[]{:S(2)}, u32[]{:S(2)}) collective-permute-start(bf16[16,240,128]{2,1,0:T(8,128)(2,1)S(1)} %bitcast.10), channel_id=1, source_target_pairs={{0,1},{1,0},{2,3},{3,2},{4,5},{5,4},{6,7},{7,6},{8,9},{9,8},{10,11... | collective-permute-start | bytes 2949128 | tf_op jit(solution)/shard_map/ppermute | solution.py:307
  55.2 13.6 %copy-start.8 = (f32[64,224]{1,0:T(8,128)S(1)}, f32[64,224]{1,0:T(8,128)}, u32[]{:S(2)}) copy-start(f32[64,224]{1,0:T(8,128)} %constant.8.clone.cos_t) | copy-start | bytes 172036
  55.2 13.6 %copy-start.9 = (f32[64,224]{1,0:T(8,128)S(1)}, f32[64,224]{1,0:T(8,128)}, u32[]{:S(2)}) copy-start(f32[64,224]{1,0:T(8,128)} %constant.9.clone.sin_t) | copy-start | bytes 172036
  55.2 25.4 %copy-start = (bf16[1,8192,128]{2,1,0:T(8,128)(2,1)S(1)}, bf16[1,8192,128]{2,1,0:T(8,128)(2,1)}, u32[]{:S(2)}) copy-start(bf16[1,8192,128]{2,1,0:T(8,128)(2,1)} %weight.3) | copy-start | bytes 6291460
  55.2 4.0 %collective-permute-start.3 = (bf16[64,224]{1,0:T(8,128)(2,1)S(1)}, bf16[64,224]{1,0:T(8,128)(2,1)S(1)}, u32[]{:S(2)}, u32[]{:S(2)}) collective-permute-start(bf16[64,224]{1,0:T(8,128)(2,1)S(1)} %get-tuple-element.26), channel_id=1, source_target_pairs={{0,0},{1,1},{2,2},{3,3},{4,8},{5,9},{6,10},{7,11},{8,16},{9,17},{1... | collective-permute-start | bytes 86024 | tf_op jit(solution)/shard_map/ppermute | solution.py:307
  56.7 26.3 %copy-start.6 = (f32[224,64]{1,0:T(8,128)S(1)}, f32[224,64]{1,0:T(8,128)}, u32[]{:S(2)}) copy-start(f32[224,64]{1,0:T(8,128)} %constant.10.clone.cos) | copy-start | bytes 172036
  56.7 26.3 %copy-start.7 = (f32[224,64]{1,0:T(8,128)S(1)}, f32[224,64]{1,0:T(8,128)}, u32[]{:S(2)}) copy-start(f32[224,64]{1,0:T(8,128)} %constant.11.clone.sin) | copy-start | bytes 172036
  56.7 6.2 %collective-permute-start.2 = (bf16[224,128]{1,0:T(8,128)(2,1)S(1)}, bf16[224,128]{1,0:T(8,128)(2,1)S(1)}, u32[]{:S(2)}, u32[]{:S(2)}) collective-permute-start(bf16[224,128]{1,0:T(8,128)(2,1)S(1)} %get-tuple-element.25), channel_id=1, source_target_pairs={{0,2},{1,3},{2,0},{3,1},{4,6},{5,7},{6,4},{7,5},{8,10},{9,11},{10,... | collective-permute-start | bytes 172040 | tf_op jit(solution)/shard_map/ppermute | solution.py:307
  62.9 5.9 %collective-permute-start.4 = (bf16[80,224]{1,0:T(8,128)(2,1)S(1)}, bf16[80,224]{1,0:T(8,128)(2,1)S(1)}, u32[]{:S(2)}, u32[]{:S(2)}) collective-permute-start(bf16[80,224]{1,0:T(8,128)(2,1)S(1)} %pad_maximum_fusion.1.near), channel_id=1, source_target_pairs={{0,2},{1,3},{2,0},{3,1},{4,6},{5,7},{6,4},{7,5},{8,10},{9,11},{10,... | collective-permute-start | bytes 107528 | tf_op jit(solution)/shard_map/ppermute | solution.py:307
  68.9 9.7 %collective-permute-start.5 = (bf16[2,32,224]{2,1,0:T(8,128)(2,1)S(1)}, bf16[2,32,224]{2,1,0:T(8,128)(2,1)S(1)}, u32[]{:S(2)}, u32[]{:S(2)}) collective-permute-start(bf16[2,32,224]{2,1,0:T(8,128)(2,1)S(1)} %get-tuple-element.29), channel_id=1, source_target_pairs={{0,4},{1,5},{2,6},{3,7},{4,0},{5,1},{6,2},{7,3},{8,12},{9,13},{10,... | collective-permute-start | bytes 86024 | tf_op jit(solution)/shard_map/ppermute | solution.py:307
  78.6 4.6 %collective-permute-start.6 = (bf16[2,2,32,224]{3,2,1,0:T(8,128)(2,1)S(1)}, bf16[2,2,32,224]{3,2,1,0:T(8,128)(2,1)S(1)}, u32[]{:S(2)}, u32[]{:S(2)}) collective-permute-start(bf16[2,2,32,224]{3,2,1,0:T(8,128)(2,1)S(1)} %pad_maximum_fusion.own), channel_id=1, source_target_pairs={{0,1},{1,0},{2,3},{3,2},{4,5},{5,4},{6,7},{7,6},{8,9},{9,8},{10,11... | collective-permute-start | bytes 172040 | tf_op jit(solution)/shard_map/ppermute | solution.py:307
  80.6 41.0 %collective-permute-start.8 = (bf16[16,256,128]{2,1,0:T(8,128)(2,1)S(1)}, bf16[16,256,128]{2,1,0:T(8,128)(2,1)S(1)}, u32[]{:S(2)}, u32[]{:S(2)}) collective-permute-start(bf16[16,256,128]{2,1,0:T(8,128)(2,1)S(1)} %shard_map.154), channel_id=1, source_target_pairs={{0,2},{1,3},{2,0},{3,1},{4,6},{5,7},{6,4},{7,5},{8,10},{9,11},{10,... | collective-permute-start | bytes 3145736 | tf_op jit(solution)/shard_map/ppermute | solution.py:307
  117.3 4.4 %collective-permute-start.7 = (bf16[16,224,128]{2,1,0:T(8,128)(2,1)S(1)}, bf16[16,224,128]{2,1,0:T(8,128)(2,1)S(1)}, u32[]{:S(2)}, u32[]{:S(2)}) collective-permute-start(bf16[16,224,128]{2,1,0:T(8,128)(2,1)S(1)} %bitcast.17), channel_id=1, source_target_pairs={{0,1},{1,0},{2,3},{3,2},{4,5},{5,4},{6,7},{7,6},{8,9},{9,8},{10,11... | collective-permute-start | bytes 2752520 | tf_op jit(solution)/shard_map/ppermute | solution.py:307
  121.6 6.8 %copy-start.3 = (bf16[1,3,112,128]{3,2,1,0:T(8,128)(2,1)S(1)}, bf16[1,3,112,128]{3,2,1,0:T(8,128)(2,1)}, u32[]{:S(2)}) copy-start(bf16[1,3,112,128]{3,2,1,0:T(8,128)(2,1)} %buffer_out.3) | copy-start | bytes 258052
  121.6 6.8 %copy-start.5 = (bf16[2,112,128]{2,1,0:T(8,128)(2,1)S(1)}, bf16[2,112,128]{2,1,0:T(8,128)(2,1)}, u32[]{:S(2)}) copy-start(bf16[2,112,128]{2,1,0:T(8,128)(2,1)} %get-tuple-element.19.inputs) | copy-start | bytes 172036
  121.6 6.8 %copy-start.10 = (s32[8,2]{0,1:T(2,128)S(1)}, s32[8,2]{0,1:T(2,128)}, u32[]{:S(2)}) copy-start(s32[8,2]{0,1:T(2,128)} %param.15) | copy-start | bytes 196
  121.7 15.8 %copy-start.4 = (bf16[1,3,112,128]{3,2,1,0:T(8,128)(2,1)S(1)}, bf16[1,3,112,128]{3,2,1,0:T(8,128)(2,1)}, u32[]{:S(2)}) copy-start(bf16[1,3,112,128]{3,2,1,0:T(8,128)(2,1)} %buffer_in.3) | copy-start | bytes 258052
  122.4 6.1 %collective-permute-start.9 = (bf16[224,128]{1,0:T(8,128)(2,1)S(1)}, bf16[224,128]{1,0:T(8,128)(2,1)S(1)}, u32[]{:S(2)}, u32[]{:S(2)}) collective-permute-start(bf16[224,128]{1,0:T(8,128)(2,1)S(1)} %get-tuple-element.32), channel_id=1, source_target_pairs={{0,2},{1,3},{2,0},{3,1},{4,6},{5,7},{6,4},{7,5},{8,10},{9,11},{10,... | collective-permute-start | bytes 172040 | tf_op jit(solution)/shard_map/ppermute | solution.py:307
  129.0 8.5 %collective-permute-start.10 = (bf16[2,112,128]{2,1,0:T(8,128)(2,1)S(1)}, bf16[2,112,128]{2,1,0:T(8,128)(2,1)S(1)}, u32[]{:S(2)}, u32[]{:S(2)}) collective-permute-start(bf16[2,112,128]{2,1,0:T(8,128)(2,1)S(1)} %shard_map.156.message), channel_id=1, source_target_pairs={{0,64},{64,128},{128,192},{192,256},{256,320},{320,384},{384,448},... | collective-permute-start | bytes 172040 | tf_op jit(solution)/shard_map/ppermute | solution.py:408

commit v5 on v3

--- a/solution.py
+++ b/solution.py
@@ -15,7 +15,7 @@
 PAY = ROWS + 16
 ZN, YN, CN = 16, 2, 2
 PIECES = 4
-EARLY = 3
+EARLY = 4
 LANES = ("z", "y", "core")
 rope_base = 500000.0
 norm_eps = 1e-05
@@ -119,6 +119,9 @@
     stores.append(pltpu.make_async_copy(inputs_v, inputs_out, sems.at[8]))
     stores[-1].start()
 
+    for load, store in zip(loads, stores):
+        load.wait()
+        store.start()
     copies[5].wait()
     kv_width = keyval.shape[1]
     per_row = CN * HEAD // kv_width
@@ -133,9 +136,6 @@
         keyval_half_v, packed.at[pl.ds(ZN, keyval_half_v.shape[0])], sems.at[6]
     )
     last.start()
-    for load, store in zip(loads, stores):
-        load.wait()
-        store.start()
     last.wait()
     for store in stores:
         store.wait()
@@ -386,7 +386,7 @@
         5 * 10**6,
     )(here, there, w_keyval, received)
     even = permute(keyval, lambda z, y, c: (2 * z if z < 8 else 2 * (z - 8) + 1, y, c))
-    odd = permute(keyval, lambda z, y, c: (2 * z + 1 if z < 8 else 2 * (z - 8), y, c))
+    odd = permute(after(keyval, even), lambda z, y, c: (2 * z + 1 if z < 8 else 2 * (z - 8), y, c))
     mine, other = call(
         query_kernel, (wide, shape((ROWS, HEAD))), 4, partial_flops, 6 * 10**6
     )(here, there, w_query, after(received, keyval))

time: 137 us -> 138 us (level)
  starting transfers between devices: 29.3 us -> 42.3 us
  waiting for transfers between devices: 20.8 us -> 10.4 us
    ppermute x10, starting transfers between devices: 24 us -> 36.9 us  [permute(): return lax.ppermute(x, LANES, pairs)]
    ppermute x10, waiting for transfers between devices: 18.8 us -> 8.51 us  [permute(): return lax.ppermute(x, LANES, pairs)]
where the time goes in v5:
time: 138 us
  blocking collectives  74.4 us (54%)
  starting transfers between devices  42.3 us (31%)
  waiting for transfers between devices  10.4 us (8%)
  Pallas kernels  9.66 us (7%)
    all_gather x2, blocking collectives, gather_z(): return lax.all_gather(x, 'z', axis=0)  74.4 us
    ppermute x10, starting transfers between devices, permute(): return lax.ppermute(x, LANES, pairs)  36.9 us
    ppermute x10, waiting for transfers between devices, permute(): return lax.ppermute(x, LANES, pairs)  8.51 us
    ppermute x1, starting transfers between devices, per_device(): lax.ppermute(message, 'section', [(i, i + 1) for i in range(sections - 1)])  5.4 us
    pallas_call x1, Pallas kernels, per_device(): pl.pallas_call(prepare, out_shape=(shape((ZN + ZN * kv_width // HEAD + EA...  3.74 us
  transfers between devices with their start and end apart: 11, of which 6 were waited for; matrix products, arithmetic and copies ran while one was open for 0% of the time, Pallas kernels for 2%

profile of v5, /device:TPU:6, one launch (start us, length us, event | category | flops | bytes accessed | tf_op | source)
XLA Modules:
  0.0 137.8 jit_solution(16693224552202633987)
XLA Ops:
  0.6 0.0 copy-start
  0.6 3.7 %shard_map.148 = (bf16[24,256,128]{2,1,0:T(8,128)(2,1)}, bf16[240,128]{1,0:T(8,128)(2,1)}, bf16[2,112,128]{2,1,0:T(8,128)(2,1)}) custom-call(s32[2,8]{1,0:T(2,128)} %bitcast.23, s32[1,2,112,128]{3,2,1,0:T(8,128)} %codes.1, s32[1,2,112]{2,1,0:T(2,128)} %exponents.1, bf16[1,3,112,128]{3,2,1,0:T(8,128)(2,1)} %buffer_in.3, bf16[1,128]{1,0:T(2,128)(2,1)} %gain.1, ...), custom_call_target="tpu_custom_call" | custom-call | flops 10000000 | bytes 4000000 | tf_op jit(solution)/shard_map/pallas_call | solution.py:345
  4.4 0.0 copy-start.2
  4.4 3.6 %collective-permute-start.1 = (bf16[24,256,128]{2,1,0:T(8,128)(2,1)}, bf16[24,256,128]{2,1,0:T(8,128)(2,1)S(1)}, u32[]{:S(2)}, u32[]{:S(2)}) collective-permute-start(bf16[24,256,128]{2,1,0:T(8,128)(2,1)} %get-tuple-element.22), channel_id=1, source_target_pairs={{0,2},{1,3},{2,0},{3,1},{4,6},{5,7},{6,4},{7,5},{8,10},{9,11},{10,... | collective-permute-start | bytes 4718600 | tf_op jit(solution)/shard_map/ppermute | solution.py:316
  8.0 42.1 %all-gather = bf16[3840,128]{1,0:T(8,128)(2,1)S(1)} all-gather(bf16[240,128]{1,0:T(8,128)(2,1)} %get-tuple-element.21), channel_id=2, replica_groups=mesh['section'=8,'z'=16,'y'=2,'core'=2] {'z'}, dimensions={0}, use_global_device_ids=true | all-gather | bytes 1044480 | tf_op jit(solution)/shard_map/all_gather | solution.py:328
  50.2 1.9 %collective-permute-start = (bf16[16,240,128]{2,1,0:T(8,128)(2,1)S(1)}, bf16[16,240,128]{2,1,0:T(8,128)(2,1)S(1)}, u32[]{:S(2)}, u32[]{:S(2)}) collective-permute-start(bf16[16,240,128]{2,1,0:T(8,128)(2,1)S(1)} %bitcast.11), channel_id=1, source_target_pairs={{0,1},{1,0},{2,3},{3,2},{4,5},{5,4},{6,7},{7,6},{8,9},{9,8},{10,11... | collective-permute-start | bytes 2949128 | tf_op jit(solution)/shard_map/ppermute | solution.py:316
  52.1 0.0 copy-done
  52.1 0.1 shard_map.151
  52.2 0.0 copy-start.1
  52.2 2.5 %collective-permute-start.5 = (bf16[12,256,128]{2,1,0:T(8,128)(2,1)S(1)}, bf16[12,256,128]{2,1,0:T(8,128)(2,1)S(1)}, u32[]{:S(2)}, u32[]{:S(2)}) collective-permute-start(bf16[12,256,128]{2,1,0:T(8,128)(2,1)S(1)} %shard_map.151), channel_id=1, source_target_pairs={{0,2},{1,3},{2,0},{3,1},{4,6},{5,7},{6,4},{7,5},{8,10},{9,11},{10,... | collective-permute-start | bytes 2359304 | tf_op jit(solution)/shard_map/ppermute | solution.py:316
  54.7 0.0 collective-permute-done.there
  54.7 0.0 collective-permute-done.1
  54.7 0.0 copy-done.2
  54.7 0.7 shard_map.149
  55.4 0.0 copy-start.8
  55.4 0.0 copy-start.9
  55.4 0.0 copy-start.6
  55.4 0.0 copy-start.7
  55.5 0.8 collective-permute-start.3
  56.3 0.0 collective-permute-done.3
  56.3 14.6 %collective-permute-start.4 = (bf16[64,224]{1,0:T(8,128)(2,1)S(1)}, bf16[64,224]{1,0:T(8,128)(2,1)S(1)}, u32[]{:S(2)}, u32[]{:S(2)}) collective-permute-start(bf16[64,224]{1,0:T(8,128)(2,1)S(1)} %get-tuple-element.27), channel_id=1, source_target_pairs={{0,4},{1,5},{2,6},{3,7},{4,12},{5,13},{6,14},{7,15},{8,20},{9,21},... | collective-permute-start | bytes 86024 | tf_op jit(solution)/shard_map/ppermute | solution.py:316
  70.9 0.0 copy-done.1
  70.9 0.7 shard_map.150
  71.6 2.1 %collective-permute-done.4 = bf16[64,224]{1,0:T(8,128)(2,1)S(1)} collective-permute-done((bf16[64,224]{1,0:T(8,128)(2,1)S(1)}, bf16[64,224]{1,0:T(8,128)(2,1)S(1)}, u32[]{:S(2)}, u32[]{:S(2)}) %collective-permute-start.4) | collective-permute-done | bytes 28704 | tf_op jit(solution)/shard_map/ppermute | solution.py:316
  73.7 3.5 %collective-permute-start.6 = (bf16[144,224]{1,0:T(8,128)(2,1)S(1)}, bf16[144,224]{1,0:T(8,128)(2,1)S(1)}, u32[]{:S(2)}, u32[]{:S(2)}) collective-permute-start(bf16[144,224]{1,0:T(8,128)(2,1)S(1)} %pad_maximum_fusion.near), channel_id=1, source_target_pairs={{0,2},{1,3},{2,0},{3,1},{4,6},{5,7},{6,4},{7,5},{8,10},{9,11},{10,... | collective-permute-start | bytes 193544 | tf_op jit(solution)/shard_map/ppermute | solution.py:316
  77.2 2.3 %collective-permute-start.2 = (bf16[224,128]{1,0:T(8,128)(2,1)S(1)}, bf16[224,128]{1,0:T(8,128)(2,1)S(1)}, u32[]{:S(2)}, u32[]{:S(2)}) collective-permute-start(bf16[224,128]{1,0:T(8,128)(2,1)S(1)} %get-tuple-element.26), channel_id=1, source_target_pairs={{0,2},{1,3},{2,0},{3,1},{4,6},{5,7},{6,4},{7,5},{8,10},{9,11},{10,... | collective-permute-start | bytes 172040 | tf_op jit(solution)/shard_map/ppermute | solution.py:316
  79.6 0.0 collective-permute-done.5
  79.6 0.7 collective-permute-done.6.far
  80.3 0.0 copy-done.8
  80.3 0.0 copy-done.9
  80.3 0.1 shard_map.152
  80.4 1.9 %collective-permute-start.7 = (bf16[4,32,224]{2,1,0:T(8,128)(2,1)S(1)}, bf16[4,32,224]{2,1,0:T(8,128)(2,1)S(1)}, u32[]{:S(2)}, u32[]{:S(2)}) collective-permute-start(bf16[4,32,224]{2,1,0:T(8,128)(2,1)S(1)} %get-tuple-element.32.own), channel_id=1, source_target_pairs={{0,1},{1,0},{2,3},{3,2},{4,5},{5,4},{6,7},{7,6},{8,9},{9,8},{10,11... | collective-permute-start | bytes 172040 | tf_op jit(solution)/shard_map/ppermute | solution.py:316
  82.3 1.0 collective-permute-done.2.other
  83.3 0.0 copy-done.7
  83.3 0.2 shard_map.153.query
  83.5 0.0 collective-permute-done.7.sibling
  83.5 0.5 shard_map.154
  84.0 32.3 %all-gather.1 = bf16[3584,128]{1,0:T(8,128)(2,1)S(1)} all-gather(bf16[224,128]{1,0:T(8,128)(2,1)S(1)} %shard_map.154), channel_id=3, replica_groups=mesh['section'=8,'z'=16,'y'=2,'core'=2] {'z'}, dimensions={0}, use_global_device_ids=true | all-gather | bytes 974848 | tf_op jit(solution)/shard_map/all_gather | solution.py:328
  116.3 1.9 %collective-permute-start.8 = (bf16[16,224,128]{2,1,0:T(8,128)(2,1)S(1)}, bf16[16,224,128]{2,1,0:T(8,128)(2,1)S(1)}, u32[]{:S(2)}, u32[]{:S(2)}) collective-permute-start(bf16[16,224,128]{2,1,0:T(8,128)(2,1)S(1)} %bitcast.17), channel_id=1, source_target_pairs={{0,1},{1,0},{2,3},{3,2},{4,5},{5,4},{6,7},{7,6},{8,9},{9,8},{10,11... | collective-permute-start | bytes 2752520 | tf_op jit(solution)/shard_map/ppermute | solution.py:316
  118.3 2.4 %collective-permute-done.8.there = bf16[16,224,128]{2,1,0:T(8,128)(2,1)S(1)} collective-permute-done((bf16[16,224,128]{2,1,0:T(8,128)(2,1)S(1)}, bf16[16,224,128]{2,1,0:T(8,128)(2,1)S(1)}, u32[]{:S(2)}, u32[]{:S(2)}) %collective-permute-start.8) | collective-permute-done | bytes 917536 | tf_op jit(solution)/shard_map/ppermute | solution.py:316
  120.7 0.7 shard_map.155
  121.4 3.8 %collective-permute-start.9 = (bf16[224,128]{1,0:T(8,128)(2,1)S(1)}, bf16[224,128]{1,0:T(8,128)(2,1)S(1)}, u32[]{:S(2)}, u32[]{:S(2)}) collective-permute-start(bf16[224,128]{1,0:T(8,128)(2,1)S(1)} %get-tuple-element.34), channel_id=1, source_target_pairs={{0,2},{1,3},{2,0},{3,1},{4,6},{5,7},{6,4},{7,5},{8,10},{9,11},{10,... | collective-permute-start | bytes 172040 | tf_op jit(solution)/shard_map/ppermute | solution.py:316
  125.1 2.3 %collective-permute-done.9.other = bf16[224,128]{1,0:T(8,128)(2,1)S(1)} collective-permute-done((bf16[224,128]{1,0:T(8,128)(2,1)S(1)}, bf16[224,128]{1,0:T(8,128)(2,1)S(1)}, u32[]{:S(2)}, u32[]{:S(2)}) %collective-permute-start.9) | collective-permute-done | bytes 57376 | tf_op jit(solution)/shard_map/ppermute | solution.py:316
  127.5 0.6 shard_map.156.message
  128.0 5.4 %collective-permute-start.10 = (bf16[2,112,128]{2,1,0:T(8,128)(2,1)S(1)}, bf16[2,112,128]{2,1,0:T(8,128)(2,1)S(1)}, u32[]{:S(2)}, u32[]{:S(2)}) collective-permute-start(bf16[2,112,128]{2,1,0:T(8,128)(2,1)S(1)} %shard_map.156.message), channel_id=1, source_target_pairs={{0,64},{64,128},{128,192},{192,256},{256,320},{320,384},{384,448},... | collective-permute-start | bytes 172040 | tf_op jit(solution)/shard_map/ppermute | solution.py:418
  133.5 1.2 shard_map.158
  134.7 1.9 %collective-permute-done.10.arrived = bf16[2,112,128]{2,1,0:T(8,128)(2,1)S(1)} collective-permute-done((bf16[2,112,128]{2,1,0:T(8,128)(2,1)S(1)}, bf16[2,112,128]{2,1,0:T(8,128)(2,1)S(1)}, u32[]{:S(2)}, u32[]{:S(2)}) %collective-permute-start.10) | collective-permute-done | bytes 57376 | tf_op jit(solution)/shard_map/ppermute | solution.py:418
  136.5 1.2 shard_map.157
  (11 shorter events, 0.0 us)
Async XLA Ops:
  0.6 51.5 %copy-start = (bf16[1,8192,128]{2,1,0:T(8,128)(2,1)S(1)}, bf16[1,8192,128]{2,1,0:T(8,128)(2,1)}, u32[]{:S(2)}) copy-start(bf16[1,8192,128]{2,1,0:T(8,128)(2,1)} %weight.3) | copy-start | bytes 6291460
  4.4 50.3 %copy-start.2 = (bf16[1,8192,32]{1,2,0:T(8,128)(2,1)S(1)}, bf16[1,8192,32]{1,2,0:T(8,128)(2,1)}, u32[]{:S(2)}) copy-start(bf16[1,8192,32]{1,2,0:T(8,128)(2,1)} %param.20) | copy-start | bytes 1572868
  4.4 50.3 %collective-permute-start.1 = (bf16[24,256,128]{2,1,0:T(8,128)(2,1)}, bf16[24,256,128]{2,1,0:T(8,128)(2,1)S(1)}, u32[]{:S(2)}, u32[]{:S(2)}) collective-permute-start(bf16[24,256,128]{2,1,0:T(8,128)(2,1)} %get-tuple-element.22), channel_id=1, source_target_pairs={{0,2},{1,3},{2,0},{3,1},{4,6},{5,7},{6,4},{7,5},{8,10},{9,11},{10,... | collective-permute-start | bytes 4718600 | tf_op jit(solution)/shard_map/ppermute | solution.py:316
  50.2 4.5 %collective-permute-start = (bf16[16,240,128]{2,1,0:T(8,128)(2,1)S(1)}, bf16[16,240,128]{2,1,0:T(8,128)(2,1)S(1)}, u32[]{:S(2)}, u32[]{:S(2)}) collective-permute-start(bf16[16,240,128]{2,1,0:T(8,128)(2,1)S(1)} %bitcast.11), channel_id=1, source_target_pairs={{0,1},{1,0},{2,3},{3,2},{4,5},{5,4},{6,7},{7,6},{8,9},{9,8},{10,11... | collective-permute-start | bytes 2949128 | tf_op jit(solution)/shard_map/ppermute | solution.py:316
  52.2 18.7 %copy-start.1 = (bf16[1,8192,128]{2,1,0:T(8,128)(2,1)S(1)}, bf16[1,8192,128]{2,1,0:T(8,128)(2,1)}, u32[]{:S(2)}) copy-start(bf16[1,8192,128]{2,1,0:T(8,128)(2,1)} %weight.2) | copy-start | bytes 6291460
  52.2 27.4 %collective-permute-start.5 = (bf16[12,256,128]{2,1,0:T(8,128)(2,1)S(1)}, bf16[12,256,128]{2,1,0:T(8,128)(2,1)S(1)}, u32[]{:S(2)}, u32[]{:S(2)}) collective-permute-start(bf16[12,256,128]{2,1,0:T(8,128)(2,1)S(1)} %shard_map.151), channel_id=1, source_target_pairs={{0,2},{1,3},{2,0},{3,1},{4,6},{5,7},{6,4},{7,5},{8,10},{9,11},{10,... | collective-permute-start | bytes 2359304 | tf_op jit(solution)/shard_map/ppermute | solution.py:316
  55.4 24.9 %copy-start.8 = (f32[64,224]{1,0:T(8,128)S(1)}, f32[64,224]{1,0:T(8,128)}, u32[]{:S(2)}) copy-start(f32[64,224]{1,0:T(8,128)} %constant.8.clone.cos_t) | copy-start | bytes 172036
  55.4 24.9 %copy-start.9 = (f32[64,224]{1,0:T(8,128)S(1)}, f32[64,224]{1,0:T(8,128)}, u32[]{:S(2)}) copy-start(f32[64,224]{1,0:T(8,128)} %constant.9.clone.sin_t) | copy-start | bytes 172036
  55.4 27.9 %copy-start.6 = (f32[224,64]{1,0:T(8,128)S(1)}, f32[224,64]{1,0:T(8,128)}, u32[]{:S(2)}) copy-start(f32[224,64]{1,0:T(8,128)} %constant.10.clone.cos) | copy-start | bytes 172036
  55.4 27.9 %copy-start.7 = (f32[224,64]{1,0:T(8,128)S(1)}, f32[224,64]{1,0:T(8,128)}, u32[]{:S(2)}) copy-start(f32[224,64]{1,0:T(8,128)} %constant.11.clone.sin) | copy-start | bytes 172036
  55.5 0.8 collective-permute-start.3
  56.3 17.4 %collective-permute-start.4 = (bf16[64,224]{1,0:T(8,128)(2,1)S(1)}, bf16[64,224]{1,0:T(8,128)(2,1)S(1)}, u32[]{:S(2)}, u32[]{:S(2)}) collective-permute-start(bf16[64,224]{1,0:T(8,128)(2,1)S(1)} %get-tuple-element.27), channel_id=1, source_target_pairs={{0,4},{1,5},{2,6},{3,7},{4,12},{5,13},{6,14},{7,15},{8,20},{9,21},... | collective-permute-start | bytes 86024 | tf_op jit(solution)/shard_map/ppermute | solution.py:316
  73.7 6.6 %collective-permute-start.6 = (bf16[144,224]{1,0:T(8,128)(2,1)S(1)}, bf16[144,224]{1,0:T(8,128)(2,1)S(1)}, u32[]{:S(2)}, u32[]{:S(2)}) collective-permute-start(bf16[144,224]{1,0:T(8,128)(2,1)S(1)} %pad_maximum_fusion.near), channel_id=1, source_target_pairs={{0,2},{1,3},{2,0},{3,1},{4,6},{5,7},{6,4},{7,5},{8,10},{9,11},{10,... | collective-permute-start | bytes 193544 | tf_op jit(solution)/shard_map/ppermute | solution.py:316
  77.2 6.1 %collective-permute-start.2 = (bf16[224,128]{1,0:T(8,128)(2,1)S(1)}, bf16[224,128]{1,0:T(8,128)(2,1)S(1)}, u32[]{:S(2)}, u32[]{:S(2)}) collective-permute-start(bf16[224,128]{1,0:T(8,128)(2,1)S(1)} %get-tuple-element.26), channel_id=1, source_target_pairs={{0,2},{1,3},{2,0},{3,1},{4,6},{5,7},{6,4},{7,5},{8,10},{9,11},{10,... | collective-permute-start | bytes 172040 | tf_op jit(solution)/shard_map/ppermute | solution.py:316
  80.4 3.1 %collective-permute-start.7 = (bf16[4,32,224]{2,1,0:T(8,128)(2,1)S(1)}, bf16[4,32,224]{2,1,0:T(8,128)(2,1)S(1)}, u32[]{:S(2)}, u32[]{:S(2)}) collective-permute-start(bf16[4,32,224]{2,1,0:T(8,128)(2,1)S(1)} %get-tuple-element.32.own), channel_id=1, source_target_pairs={{0,1},{1,0},{2,3},{3,2},{4,5},{5,4},{6,7},{7,6},{8,9},{9,8},{10,11... | collective-permute-start | bytes 172040 | tf_op jit(solution)/shard_map/ppermute | solution.py:316
  116.3 4.4 %collective-permute-start.8 = (bf16[16,224,128]{2,1,0:T(8,128)(2,1)S(1)}, bf16[16,224,128]{2,1,0:T(8,128)(2,1)S(1)}, u32[]{:S(2)}, u32[]{:S(2)}) collective-permute-start(bf16[16,224,128]{2,1,0:T(8,128)(2,1)S(1)} %bitcast.17), channel_id=1, source_target_pairs={{0,1},{1,0},{2,3},{3,2},{4,5},{5,4},{6,7},{7,6},{8,9},{9,8},{10,11... | collective-permute-start | bytes 2752520 | tf_op jit(solution)/shard_map/ppermute | solution.py:316
  120.7 6.8 %copy-start.3 = (bf16[1,3,112,128]{3,2,1,0:T(8,128)(2,1)S(1)}, bf16[1,3,112,128]{3,2,1,0:T(8,128)(2,1)}, u32[]{:S(2)}) copy-start(bf16[1,3,112,128]{3,2,1,0:T(8,128)(2,1)} %buffer_out.3) | copy-start | bytes 258052
  120.7 6.8 %copy-start.5 = (bf16[2,112,128]{2,1,0:T(8,128)(2,1)S(1)}, bf16[2,112,128]{2,1,0:T(8,128)(2,1)}, u32[]{:S(2)}) copy-start(bf16[2,112,128]{2,1,0:T(8,128)(2,1)} %get-tuple-element.20.inputs) | copy-start | bytes 172036
  120.7 6.8 %copy-start.10 = (s32[8,2]{0,1:T(2,128)S(1)}, s32[8,2]{0,1:T(2,128)}, u32[]{:S(2)}) copy-start(s32[8,2]{0,1:T(2,128)} %param.15) | copy-start | bytes 196
  120.7 15.8 %copy-start.4 = (bf16[1,3,112,128]{3,2,1,0:T(8,128)(2,1)S(1)}, bf16[1,3,112,128]{3,2,1,0:T(8,128)(2,1)}, u32[]{:S(2)}) copy-start(bf16[1,3,112,128]{3,2,1,0:T(8,128)(2,1)} %buffer_in.3) | copy-start | bytes 258052
  121.4 6.1 %collective-permute-start.9 = (bf16[224,128]{1,0:T(8,128)(2,1)S(1)}, bf16[224,128]{1,0:T(8,128)(2,1)S(1)}, u32[]{:S(2)}, u32[]{:S(2)}) collective-permute-start(bf16[224,128]{1,0:T(8,128)(2,1)S(1)} %get-tuple-element.34), channel_id=1, source_target_pairs={{0,2},{1,3},{2,0},{3,1},{4,6},{5,7},{6,4},{7,5},{8,10},{9,11},{10,... | collective-permute-start | bytes 172040 | tf_op jit(solution)/shard_map/ppermute | solution.py:316
  128.0 8.5 %collective-permute-start.10 = (bf16[2,112,128]{2,1,0:T(8,128)(2,1)S(1)}, bf16[2,112,128]{2,1,0:T(8,128)(2,1)S(1)}, u32[]{:S(2)}, u32[]{:S(2)}) collective-permute-start(bf16[2,112,128]{2,1,0:T(8,128)(2,1)S(1)} %shard_map.156.message), channel_id=1, source_target_pairs={{0,64},{64,128},{128,192},{192,256},{256,320},{320,384},{384,448},... | collective-permute-start | bytes 172040 | tf_op jit(solution)/shard_map/ppermute | solution.py:418

commit v6 on v5

--- a/solution.py
+++ b/solution.py
@@ -176,7 +176,7 @@
     out[...] = acc.astype(jnp.bfloat16)
 
 
-def both_partials(here, there, weight, received_rows):
+def both_partials(here, there, weight, received):
     y, core = lax.axis_index("y"), lax.axis_index("core")
     acc = jnp.zeros((ROWS, 2 * HEAD), jnp.float32)
     for z in range(ZN):
@@ -184,7 +184,7 @@
         parts = []
         for side in (core, core ^ 1):
             mine = weight[0, head_rows(z, y, side), :]
-            other = received_rows(z, side)
+            other = received[half_rows(z, side), :]
             parts.append(jnp.concatenate([mine, other], axis=1))
         part = jnp.concatenate(parts, axis=0)
         acc += jnp.dot(block, part, preferred_element_type=jnp.float32)
@@ -192,7 +192,7 @@
 
 
 def query_kernel(here, there, weight, received, mine_out, other_out):
-    acc = both_partials(here, there, weight, lambda z, side: received[half_rows(z, side), :])
+    acc = both_partials(here, there, weight, received)
     mine_out[...] = acc[:, :HEAD]
     other_out[...] = acc[:, HEAD:].astype(jnp.bfloat16)
 
@@ -258,15 +258,41 @@
         out[z - EARLY] = weight[z, far]
 
 
-def output_kernel(here, there, weight, early, received, mine_out, other_out):
-    def received_rows(z, side):
-        if z < EARLY:
-            return early[half_rows(z, side), :]
-        return received[half_rows(z - EARLY, side), :]
-
-    acc = both_partials(here, there, weight, received_rows)
-    mine_out[...] = acc[:, :HEAD]
-    other_out[...] = acc[:, HEAD:].astype(jnp.bfloat16)
+def line_product(line, rows):
+    acc = None
+    for z in range(0, ZN, 2):
+        block = jnp.concatenate([line[z], line[z + 1]], axis=1)
+        part = jnp.concatenate([rows(z), rows(z + 1)], axis=0)
+        term = jnp.dot(block, part, preferred_element_type=jnp.float32)
+        acc = term if acc is None else acc + term
+    return acc
+
+
+def far_rows(z, core, early, received):
+    if z < EARLY:
+        return early[half_rows(z, core), :]
+    return received[half_rows(z - EARLY, core), :]
+
+
+def own_line_kernel(line, weight, early, received, out):
+    y, core = lax.axis_index("y"), lax.axis_index("core")
+
+    def rows(z):
+        mine = weight[0, head_rows(z, y, core), :]
+        return jnp.concatenate([mine, far_rows(z, core, early, received)], axis=1)
+
+    out[...] = line_product(line, rows)
+
+
+def far_columns_kernel(line, acc, early, received, out):
+    side = lax.axis_index("core") ^ 1
+    total = line_product(line, lambda z: far_rows(z, side, early, received))
+    out[...] = (acc[:, HEAD:] + total).astype(jnp.bfloat16)
+
+
+def own_columns_kernel(line, acc, weight, out):
+    y, side = lax.axis_index("y"), lax.axis_index("core") ^ 1
+    out[...] = acc[:, :HEAD] + line_product(line, lambda z: weight[0, head_rows(z, y, side), :])
 
 
 def message_kernel(ids, mine, other, inputs, buffer_out, message_out):
@@ -287,19 +313,26 @@
         new_out[0, slot] = (stored + message[s].astype(jnp.float32)).astype(jnp.bfloat16)
 
 
-def finish_kernel(ids, buffer_in, inputs, arrived, following_out, stored_out):
+def finish_kernel(ids, buffer_in, inputs, arrived, following_out, stored_out, following, stored, sems):
     section = lax.axis_index("section")
     before = jnp.maximum(section - 1, 0)
-    stored_out[...] = buffer_in[...]
+    stored[...] = buffer_in[0]
     for s in range(SEQS):
-        stored_out[0, ids[s, section]] = inputs[s]
-    results = []
+        stored[ids[s, section]] = inputs[s]
+    copies = []
     for s in range(SEQS):
-        current = stored_out[0, ids[s, before]].astype(jnp.float32)
-        results.append((current + arrived[s].astype(jnp.float32)).astype(jnp.bfloat16))
+        current = stored[ids[s, before]].astype(jnp.float32)
+        following[s] = (current + arrived[s].astype(jnp.float32)).astype(jnp.bfloat16)
+        copies.append(
+            pltpu.make_async_copy(following.at[s], following_out.at[0, s], sems.at[s])
+        )
+        copies[-1].start()
     for s in range(SEQS):
-        following_out[0, s] = results[s]
-        stored_out[0, ids[s, before]] = results[s]
+        stored[ids[s, before]] = following[s]
+    copies.append(pltpu.make_async_copy(stored, stored_out.at[0], sems.at[SEQS]))
+    copies[-1].start()
+    for item in copies:
+        item.wait()
 
 
 def lane(z, y, core):
@@ -386,7 +419,7 @@
         5 * 10**6,
     )(here, there, w_keyval, received)
     even = permute(keyval, lambda z, y, c: (2 * z if z < 8 else 2 * (z - 8) + 1, y, c))
-    odd = permute(after(keyval, even), lambda z, y, c: (2 * z + 1 if z < 8 else 2 * (z - 8), y, c))
+    odd = permute(keyval, lambda z, y, c: (2 * z + 1 if z < 8 else 2 * (z - 8), y, c))
     mine, other = call(
         query_kernel, (wide, shape((ROWS, HEAD))), 4, partial_flops, 6 * 10**6
     )(here, there, w_query, after(received, keyval))
@@ -406,23 +439,34 @@
 
     here = gather_z(context)
     there = swap(here, 0, 1)
-    mine, other = call(
-        output_kernel, (wide, shape((ROWS, HEAD))), 5, partial_flops, 6 * 10**6
-    )(here, there, w_output, received[-EARLY * CN * HEAD :], received_out)
+    early = received[-EARLY * CN * HEAD :]
+    line_flops = partial_flops // 2
+    both = call(
+        own_line_kernel, shape((ROWS, 2 * HEAD), jnp.float32), 4, line_flops, 4 * 10**6
+    )(here, w_output, early, received_out)
+    other = call(far_columns_kernel, shape((ROWS, HEAD)), 4, line_flops, 2 * 10**6)(
+        there, both, early, received_out
+    )
     other = swap(other, 1, 0)
+    mine = call(own_columns_kernel, wide, 3, line_flops, 3 * 10**6)(there, both, w_output)
     message = call(
         message_kernel, shape((SEQS, LEN, HEAD)), 5, 10**6, 10**6, smem=(0,)
     )(sample_ids, mine, other, inputs, buffer_out)
 
     sections = lax.axis_size("section")
     arrived = lax.ppermute(message, "section", [(i, i + 1) for i in range(sections - 1)])
-    following, new_in = call(
+    following, new_in = pl.pallas_call(
         finish_kernel,
-        (shape((1, SEQS, LEN, HEAD)), shape(buffer_in.shape)),
-        4,
-        10**6,
-        10**6,
-        smem=(0,),
+        out_shape=(shape((1, SEQS, LEN, HEAD)), shape(buffer_in.shape)),
+        in_specs=[SMEM] + [VMEM] * 3,
+        out_specs=(any_spec,) * 2,
+        scratch_shapes=[
+            pltpu.VMEM((SEQS, LEN, HEAD), bf16),
+            pltpu.VMEM((SLOTS, LEN, HEAD), bf16),
+            pltpu.SemaphoreType.DMA((SEQS + 1,)),
+        ],
+        compiler_params=PARAMS,
+        cost_estimate=pl.CostEstimate(flops=10**6, bytes_accessed=10**6, transcendentals=0),
     )(sample_ids, buffer_in, inputs, arrived)
     new_out = call(refresh_kernel, shape(buffer_out.shape), 3, 10**6, 10**6, smem=(0,))(
         sample_ids, message, buffer_out

time: 138 us -> 137 us (level)
  starting transfers between devices: 42.3 us -> 29.5 us
  waiting for transfers between devices: 10.4 us -> 19.9 us
    ppermute x10, starting transfers between devices: 36.9 us -> 24.1 us  [permute(): return lax.ppermute(x, LANES, pairs)]
    ppermute x10, waiting for transfers between devices: 8.51 us -> 18 us  [permute(): return lax.ppermute(x, LANES, pairs)]
  transfers between devices with their start and end apart: 11 -> 11, of which waited for: 6 -> 6; matrix products, arithmetic and copies ran while one was open for 0% -> 0% of each run, Pallas kernels for 2% -> 3%
where the time goes in v6:
time: 137 us; the launch traced here: 136 us
  blocking collectives  75.5 us (55%)
  starting transfers between devices  29.5 us (22%)
  waiting for transfers between devices  19.9 us (15%)
  Pallas kernels  10.3 us (8%)
    all_gather x2, blocking collectives, gather_z(): return lax.all_gather(x, 'z', axis=0)  75.5 us
    ppermute x10, starting transfers between devices, permute(): return lax.ppermute(x, LANES, pairs)  24.1 us
    ppermute x10, waiting for transfers between devices, permute(): return lax.ppermute(x, LANES, pairs)  18 us
    ppermute x1, starting transfers between devices, per_device(): lax.ppermute(message, 'section', [(i, i + 1) for i in range(sections - 1)])  5.35 us
    pallas_call x1, Pallas kernels, per_device(): pl.pallas_call(prepare, out_shape=(shape((ZN + ZN * kv_width // HEAD + EA...  3.76 us
  transfers between devices with their start and end apart: 11, of which 6 were waited for; matrix products, arithmetic and copies ran while one was open for 0% of the time, Pallas kernels for 3%

profile of v6, /device:TPU:6, one launch (start us, length us, event | category | flops | bytes accessed | tf_op | source)
XLA Modules:
  0.0 136.1 jit_solution(17712328621442128660)
XLA Ops:
  0.6 0.0 copy-start
  0.6 3.8 %shard_map.148 = (bf16[24,256,128]{2,1,0:T(8,128)(2,1)}, bf16[240,128]{1,0:T(8,128)(2,1)}, bf16[2,112,128]{2,1,0:T(8,128)(2,1)}) custom-call(s32[2,8]{1,0:T(2,128)} %bitcast.25, s32[1,2,112,128]{3,2,1,0:T(8,128)} %codes.1, s32[1,2,112]{2,1,0:T(2,128)} %exponents.1, bf16[1,3,112,128]{3,2,1,0:T(8,128)(2,1)} %buffer_in.3, bf16[1,128]{1,0:T(2,128)(2,1)} %gain.1, ...), custom_call_target="tpu_custom_call" | custom-call | flops 10000000 | bytes 4000000 | tf_op jit(solution)/shard_map/pallas_call | solution.py:378
  4.4 0.0 copy-start.2
  4.4 3.6 %collective-permute-start.1 = (bf16[24,256,128]{2,1,0:T(8,128)(2,1)}, bf16[24,256,128]{2,1,0:T(8,128)(2,1)S(1)}, u32[]{:S(2)}, u32[]{:S(2)}) collective-permute-start(bf16[24,256,128]{2,1,0:T(8,128)(2,1)} %get-tuple-element.19), channel_id=1, source_target_pairs={{0,2},{1,3},{2,0},{3,1},{4,6},{5,7},{6,4},{7,5},{8,10},{9,11},{10,... | collective-permute-start | bytes 4718600 | tf_op jit(solution)/shard_map/ppermute | solution.py:349
  8.0 42.1 %all-gather = bf16[3840,128]{1,0:T(8,128)(2,1)S(1)} all-gather(bf16[240,128]{1,0:T(8,128)(2,1)} %get-tuple-element.18), channel_id=2, replica_groups=mesh['section'=8,'z'=16,'y'=2,'core'=2] {'z'}, dimensions={0}, use_global_device_ids=true | all-gather | bytes 1044480 | tf_op jit(solution)/shard_map/all_gather | solution.py:361
  50.2 1.9 %collective-permute-start = (bf16[16,240,128]{2,1,0:T(8,128)(2,1)S(1)}, bf16[16,240,128]{2,1,0:T(8,128)(2,1)S(1)}, u32[]{:S(2)}, u32[]{:S(2)}) collective-permute-start(bf16[16,240,128]{2,1,0:T(8,128)(2,1)S(1)} %bitcast.11), channel_id=1, source_target_pairs={{0,1},{1,0},{2,3},{3,2},{4,5},{5,4},{6,7},{7,6},{8,9},{9,8},{10,11... | collective-permute-start | bytes 2949128 | tf_op jit(solution)/shard_map/ppermute | solution.py:349
  52.1 0.1 shard_map.151
  52.2 0.0 copy-start.1
  52.2 2.5 %collective-permute-start.5 = (bf16[12,256,128]{2,1,0:T(8,128)(2,1)S(1)}, bf16[12,256,128]{2,1,0:T(8,128)(2,1)S(1)}, u32[]{:S(2)}, u32[]{:S(2)}) collective-permute-start(bf16[12,256,128]{2,1,0:T(8,128)(2,1)S(1)} %shard_map.151), channel_id=1, source_target_pairs={{0,2},{1,3},{2,0},{3,1},{4,6},{5,7},{6,4},{7,5},{8,10},{9,11},{10,... | collective-permute-start | bytes 2359304 | tf_op jit(solution)/shard_map/ppermute | solution.py:349
  54.7 0.0 collective-permute-done.there
  54.7 0.0 collective-permute-done.1
  54.7 0.7 shard_map.149
  55.4 0.0 copy-start.8
  55.4 0.0 copy-start.9
  55.4 0.0 copy-start.6
  55.5 0.0 copy-start.7
  55.5 2.1 %collective-permute-start.4 = (bf16[64,224]{1,0:T(8,128)(2,1)S(1)}, bf16[64,224]{1,0:T(8,128)(2,1)S(1)}, u32[]{:S(2)}, u32[]{:S(2)}) collective-permute-start(bf16[64,224]{1,0:T(8,128)(2,1)S(1)} %get-tuple-element.20), channel_id=1, source_target_pairs={{0,4},{1,5},{2,6},{3,7},{4,12},{5,13},{6,14},{7,15},{8,20},{9,21},... | collective-permute-start | bytes 86024 | tf_op jit(solution)/shard_map/ppermute | solution.py:349
  57.5 0.7 collective-permute-start.3
  58.2 0.7 shard_map.150
  58.9 12.2 %collective-permute-done.4 = bf16[64,224]{1,0:T(8,128)(2,1)S(1)} collective-permute-done((bf16[64,224]{1,0:T(8,128)(2,1)S(1)}, bf16[64,224]{1,0:T(8,128)(2,1)S(1)}, u32[]{:S(2)}, u32[]{:S(2)}) %collective-permute-start.4) | collective-permute-done | bytes 28704 | tf_op jit(solution)/shard_map/ppermute | solution.py:349
  71.1 0.0 collective-permute-done.3
  71.1 3.5 %collective-permute-start.6 = (bf16[144,224]{1,0:T(8,128)(2,1)S(1)}, bf16[144,224]{1,0:T(8,128)(2,1)S(1)}, u32[]{:S(2)}, u32[]{:S(2)}) collective-permute-start(bf16[144,224]{1,0:T(8,128)(2,1)S(1)} %pad_maximum_fusion.near), channel_id=1, source_target_pairs={{0,2},{1,3},{2,0},{3,1},{4,6},{5,7},{6,4},{7,5},{8,10},{9,11},{10,... | collective-permute-start | bytes 193544 | tf_op jit(solution)/shard_map/ppermute | solution.py:349
  74.7 2.3 %collective-permute-start.2 = (bf16[224,128]{1,0:T(8,128)(2,1)S(1)}, bf16[224,128]{1,0:T(8,128)(2,1)S(1)}, u32[]{:S(2)}, u32[]{:S(2)}) collective-permute-start(bf16[224,128]{1,0:T(8,128)(2,1)S(1)} %get-tuple-element.23), channel_id=1, source_target_pairs={{0,2},{1,3},{2,0},{3,1},{4,6},{5,7},{6,4},{7,5},{8,10},{9,11},{10,... | collective-permute-start | bytes 172040 | tf_op jit(solution)/shard_map/ppermute | solution.py:349
  77.0 0.0 collective-permute-done.5
  77.0 0.4 collective-permute-done.6.far
  77.4 0.1 shard_map.152
  77.5 1.9 %collective-permute-start.7 = (bf16[4,32,224]{2,1,0:T(8,128)(2,1)S(1)}, bf16[4,32,224]{2,1,0:T(8,128)(2,1)S(1)}, u32[]{:S(2)}, u32[]{:S(2)}) collective-permute-start(bf16[4,32,224]{2,1,0:T(8,128)(2,1)S(1)} %get-tuple-element.28.own), channel_id=1, source_target_pairs={{0,1},{1,0},{2,3},{3,2},{4,5},{5,4},{6,7},{7,6},{8,9},{9,8},{10,11... | collective-permute-start | bytes 172040 | tf_op jit(solution)/shard_map/ppermute | solution.py:349
  79.4 1.3 collective-permute-done.2.other
  80.8 0.2 shard_map.153.query
  81.0 0.0 collective-permute-done.7.sibling
  81.0 0.5 shard_map.154
  81.5 33.3 %all-gather.1 = bf16[3584,128]{1,0:T(8,128)(2,1)S(1)} all-gather(bf16[224,128]{1,0:T(8,128)(2,1)S(1)} %shard_map.154), channel_id=3, replica_groups=mesh['section'=8,'z'=16,'y'=2,'core'=2] {'z'}, dimensions={0}, use_global_device_ids=true | all-gather | bytes 974848 | tf_op jit(solution)/shard_map/all_gather | solution.py:361
  114.8 1.9 %collective-permute-start.8 = (bf16[16,224,128]{2,1,0:T(8,128)(2,1)S(1)}, bf16[16,224,128]{2,1,0:T(8,128)(2,1)S(1)}, u32[]{:S(2)}, u32[]{:S(2)}) collective-permute-start(bf16[16,224,128]{2,1,0:T(8,128)(2,1)S(1)} %bitcast.17), channel_id=1, source_target_pairs={{0,1},{1,0},{2,3},{3,2},{4,5},{5,4},{6,7},{7,6},{8,9},{9,8},{10,11... | collective-permute-start | bytes 2752520 | tf_op jit(solution)/shard_map/ppermute | solution.py:349
  116.7 0.4 shard_map.155.acc
  117.2 2.0 %collective-permute-done.8.line = bf16[16,224,128]{2,1,0:T(8,128)(2,1)S(1)} collective-permute-done((bf16[16,224,128]{2,1,0:T(8,128)(2,1)S(1)}, bf16[16,224,128]{2,1,0:T(8,128)(2,1)S(1)}, u32[]{:S(2)}, u32[]{:S(2)}) %collective-permute-start.8) | collective-permute-done | bytes 917536 | tf_op jit(solution)/shard_map/ppermute | solution.py:349
  119.2 0.4 shard_map.157
  119.6 0.0 copy-start.3
  119.6 0.0 copy-start.5
  119.6 0.0 copy-start.10
  119.6 0.0 copy-start.4
  119.6 3.7 %collective-permute-start.9 = (bf16[224,128]{1,0:T(8,128)(2,1)S(1)}, bf16[224,128]{1,0:T(8,128)(2,1)S(1)}, u32[]{:S(2)}, u32[]{:S(2)}) collective-permute-start(bf16[224,128]{1,0:T(8,128)(2,1)S(1)} %shard_map.157), channel_id=1, source_target_pairs={{0,2},{1,3},{2,0},{3,1},{4,6},{5,7},{6,4},{7,5},{8,10},{9,11},{10,... | collective-permute-start | bytes 172040 | tf_op jit(solution)/shard_map/ppermute | solution.py:349
  123.3 0.4 shard_map.156.mine
  123.8 2.1 %collective-permute-done.9.other = bf16[224,128]{1,0:T(8,128)(2,1)S(1)} collective-permute-done((bf16[224,128]{1,0:T(8,128)(2,1)S(1)}, bf16[224,128]{1,0:T(8,128)(2,1)S(1)}, u32[]{:S(2)}, u32[]{:S(2)}) %collective-permute-start.9) | collective-permute-done | bytes 57376 | tf_op jit(solution)/shard_map/ppermute | solution.py:349
  125.8 0.6 shard_map.158.message
  126.4 5.3 %collective-permute-start.10 = (bf16[2,112,128]{2,1,0:T(8,128)(2,1)S(1)}, bf16[2,112,128]{2,1,0:T(8,128)(2,1)S(1)}, u32[]{:S(2)}, u32[]{:S(2)}) collective-permute-start(bf16[2,112,128]{2,1,0:T(8,128)(2,1)S(1)} %shard_map.158.message), channel_id=1, source_target_pairs={{0,64},{64,128},{128,192},{192,256},{256,320},{320,384},{384,448},... | collective-permute-start | bytes 172040 | tf_op jit(solution)/shard_map/ppermute | solution.py:457
  131.8 1.2 shard_map.160
  133.0 1.9 %collective-permute-done.10.arrived = bf16[2,112,128]{2,1,0:T(8,128)(2,1)S(1)} collective-permute-done((bf16[2,112,128]{2,1,0:T(8,128)(2,1)S(1)}, bf16[2,112,128]{2,1,0:T(8,128)(2,1)S(1)}, u32[]{:S(2)}, u32[]{:S(2)}) %collective-permute-start.10) | collective-permute-done | bytes 57376 | tf_op jit(solution)/shard_map/ppermute | solution.py:457
  134.9 1.3 shard_map.159
  (13 shorter events, 0.1 us)
Async XLA Ops:
  0.6 51.5 %copy-start = (bf16[1,8192,128]{2,1,0:T(8,128)(2,1)S(1)}, bf16[1,8192,128]{2,1,0:T(8,128)(2,1)}, u32[]{:S(2)}) copy-start(bf16[1,8192,128]{2,1,0:T(8,128)(2,1)} %weight.5) | copy-start | bytes 6291460
  4.4 50.3 %copy-start.2 = (bf16[1,8192,32]{1,2,0:T(8,128)(2,1)S(1)}, bf16[1,8192,32]{1,2,0:T(8,128)(2,1)}, u32[]{:S(2)}) copy-start(bf16[1,8192,32]{1,2,0:T(8,128)(2,1)} %param.20) | copy-start | bytes 1572868
  4.4 50.3 %collective-permute-start.1 = (bf16[24,256,128]{2,1,0:T(8,128)(2,1)}, bf16[24,256,128]{2,1,0:T(8,128)(2,1)S(1)}, u32[]{:S(2)}, u32[]{:S(2)}) collective-permute-start(bf16[24,256,128]{2,1,0:T(8,128)(2,1)} %get-tuple-element.19), channel_id=1, source_target_pairs={{0,2},{1,3},{2,0},{3,1},{4,6},{5,7},{6,4},{7,5},{8,10},{9,11},{10,... | collective-permute-start | bytes 4718600 | tf_op jit(solution)/shard_map/ppermute | solution.py:349
  50.2 4.5 %collective-permute-start = (bf16[16,240,128]{2,1,0:T(8,128)(2,1)S(1)}, bf16[16,240,128]{2,1,0:T(8,128)(2,1)S(1)}, u32[]{:S(2)}, u32[]{:S(2)}) collective-permute-start(bf16[16,240,128]{2,1,0:T(8,128)(2,1)S(1)} %bitcast.11), channel_id=1, source_target_pairs={{0,1},{1,0},{2,3},{3,2},{4,5},{5,4},{6,7},{7,6},{8,9},{9,8},{10,11... | collective-permute-start | bytes 2949128 | tf_op jit(solution)/shard_map/ppermute | solution.py:349
  52.2 6.0 %copy-start.1 = (bf16[1,8192,128]{2,1,0:T(8,128)(2,1)S(1)}, bf16[1,8192,128]{2,1,0:T(8,128)(2,1)}, u32[]{:S(2)}) copy-start(bf16[1,8192,128]{2,1,0:T(8,128)(2,1)} %weight.3) | copy-start | bytes 6291460
  52.2 24.8 %collective-permute-start.5 = (bf16[12,256,128]{2,1,0:T(8,128)(2,1)S(1)}, bf16[12,256,128]{2,1,0:T(8,128)(2,1)S(1)}, u32[]{:S(2)}, u32[]{:S(2)}) collective-permute-start(bf16[12,256,128]{2,1,0:T(8,128)(2,1)S(1)} %shard_map.151), channel_id=1, source_target_pairs={{0,2},{1,3},{2,0},{3,1},{4,6},{5,7},{6,4},{7,5},{8,10},{9,11},{10,... | collective-permute-start | bytes 2359304 | tf_op jit(solution)/shard_map/ppermute | solution.py:349
  55.4 22.0 %copy-start.8 = (f32[64,224]{1,0:T(8,128)S(1)}, f32[64,224]{1,0:T(8,128)}, u32[]{:S(2)}) copy-start(f32[64,224]{1,0:T(8,128)} %constant.8.clone.cos_t) | copy-start | bytes 172036
  55.4 22.0 %copy-start.9 = (f32[64,224]{1,0:T(8,128)S(1)}, f32[64,224]{1,0:T(8,128)}, u32[]{:S(2)}) copy-start(f32[64,224]{1,0:T(8,128)} %constant.9.clone.sin_t) | copy-start | bytes 172036
  55.4 25.3 %copy-start.6 = (f32[224,64]{1,0:T(8,128)S(1)}, f32[224,64]{1,0:T(8,128)}, u32[]{:S(2)}) copy-start(f32[224,64]{1,0:T(8,128)} %constant.10.clone.cos) | copy-start | bytes 172036
  55.5 25.3 %copy-start.7 = (f32[224,64]{1,0:T(8,128)S(1)}, f32[224,64]{1,0:T(8,128)}, u32[]{:S(2)}) copy-start(f32[224,64]{1,0:T(8,128)} %constant.11.clone.sin) | copy-start | bytes 172036
  55.5 15.6 %collective-permute-start.4 = (bf16[64,224]{1,0:T(8,128)(2,1)S(1)}, bf16[64,224]{1,0:T(8,128)(2,1)S(1)}, u32[]{:S(2)}, u32[]{:S(2)}) collective-permute-start(bf16[64,224]{1,0:T(8,128)(2,1)S(1)} %get-tuple-element.20), channel_id=1, source_target_pairs={{0,4},{1,5},{2,6},{3,7},{4,12},{5,13},{6,14},{7,15},{8,20},{9,21},... | collective-permute-start | bytes 86024 | tf_op jit(solution)/shard_map/ppermute | solution.py:349
  57.5 13.6 %collective-permute-start.3 = (bf16[64,224]{1,0:T(8,128)(2,1)S(1)}, bf16[64,224]{1,0:T(8,128)(2,1)S(1)}, u32[]{:S(2)}, u32[]{:S(2)}) collective-permute-start(bf16[64,224]{1,0:T(8,128)(2,1)S(1)} %get-tuple-element.20), channel_id=1, source_target_pairs={{0,0},{1,1},{2,2},{3,3},{4,8},{5,9},{6,10},{7,11},{8,16},{9,17},{1... | collective-permute-start | bytes 86024 | tf_op jit(solution)/shard_map/ppermute | solution.py:349
  71.1 6.2 %collective-permute-start.6 = (bf16[144,224]{1,0:T(8,128)(2,1)S(1)}, bf16[144,224]{1,0:T(8,128)(2,1)S(1)}, u32[]{:S(2)}, u32[]{:S(2)}) collective-permute-start(bf16[144,224]{1,0:T(8,128)(2,1)S(1)} %pad_maximum_fusion.near), channel_id=1, source_target_pairs={{0,2},{1,3},{2,0},{3,1},{4,6},{5,7},{6,4},{7,5},{8,10},{9,11},{10,... | collective-permute-start | bytes 193544 | tf_op jit(solution)/shard_map/ppermute | solution.py:349
  74.7 6.1 %collective-permute-start.2 = (bf16[224,128]{1,0:T(8,128)(2,1)S(1)}, bf16[224,128]{1,0:T(8,128)(2,1)S(1)}, u32[]{:S(2)}, u32[]{:S(2)}) collective-permute-start(bf16[224,128]{1,0:T(8,128)(2,1)S(1)} %get-tuple-element.23), channel_id=1, source_target_pairs={{0,2},{1,3},{2,0},{3,1},{4,6},{5,7},{6,4},{7,5},{8,10},{9,11},{10,... | collective-permute-start | bytes 172040 | tf_op jit(solution)/shard_map/ppermute | solution.py:349
  77.5 3.5 %collective-permute-start.7 = (bf16[4,32,224]{2,1,0:T(8,128)(2,1)S(1)}, bf16[4,32,224]{2,1,0:T(8,128)(2,1)S(1)}, u32[]{:S(2)}, u32[]{:S(2)}) collective-permute-start(bf16[4,32,224]{2,1,0:T(8,128)(2,1)S(1)} %get-tuple-element.28.own), channel_id=1, source_target_pairs={{0,1},{1,0},{2,3},{3,2},{4,5},{5,4},{6,7},{7,6},{8,9},{9,8},{10,11... | collective-permute-start | bytes 172040 | tf_op jit(solution)/shard_map/ppermute | solution.py:349
  114.8 4.4 %collective-permute-start.8 = (bf16[16,224,128]{2,1,0:T(8,128)(2,1)S(1)}, bf16[16,224,128]{2,1,0:T(8,128)(2,1)S(1)}, u32[]{:S(2)}, u32[]{:S(2)}) collective-permute-start(bf16[16,224,128]{2,1,0:T(8,128)(2,1)S(1)} %bitcast.17), channel_id=1, source_target_pairs={{0,1},{1,0},{2,3},{3,2},{4,5},{5,4},{6,7},{7,6},{8,9},{9,8},{10,11... | collective-permute-start | bytes 2752520 | tf_op jit(solution)/shard_map/ppermute | solution.py:349
  119.6 6.3 %copy-start.3 = (bf16[1,3,112,128]{3,2,1,0:T(8,128)(2,1)S(1)}, bf16[1,3,112,128]{3,2,1,0:T(8,128)(2,1)}, u32[]{:S(2)}) copy-start(bf16[1,3,112,128]{3,2,1,0:T(8,128)(2,1)} %buffer_out.3) | copy-start | bytes 258052
  119.6 6.2 %copy-start.5 = (bf16[2,112,128]{2,1,0:T(8,128)(2,1)S(1)}, bf16[2,112,128]{2,1,0:T(8,128)(2,1)}, u32[]{:S(2)}) copy-start(bf16[2,112,128]{2,1,0:T(8,128)(2,1)} %get-tuple-element.17.inputs) | copy-start | bytes 172036
  119.6 6.2 %copy-start.10 = (s32[8,2]{0,1:T(2,128)S(1)}, s32[8,2]{0,1:T(2,128)}, u32[]{:S(2)}) copy-start(s32[8,2]{0,1:T(2,128)} %param.15) | copy-start | bytes 196
  119.6 15.3 %copy-start.4 = (bf16[1,3,112,128]{3,2,1,0:T(8,128)(2,1)S(1)}, bf16[1,3,112,128]{3,2,1,0:T(8,128)(2,1)}, u32[]{:S(2)}) copy-start(bf16[1,3,112,128]{3,2,1,0:T(8,128)(2,1)} %buffer_in.3) | copy-start | bytes 258052
  119.6 6.2 %collective-permute-start.9 = (bf16[224,128]{1,0:T(8,128)(2,1)S(1)}, bf16[224,128]{1,0:T(8,128)(2,1)S(1)}, u32[]{:S(2)}, u32[]{:S(2)}) collective-permute-start(bf16[224,128]{1,0:T(8,128)(2,1)S(1)} %shard_map.157), channel_id=1, source_target_pairs={{0,2},{1,3},{2,0},{3,1},{4,6},{5,7},{6,4},{7,5},{8,10},{9,11},{10,... | collective-permute-start | bytes 172040 | tf_op jit(solution)/shard_map/ppermute | solution.py:349
  126.4 8.5 %collective-permute-start.10 = (bf16[2,112,128]{2,1,0:T(8,128)(2,1)S(1)}, bf16[2,112,128]{2,1,0:T(8,128)(2,1)S(1)}, u32[]{:S(2)}, u32[]{:S(2)}) collective-permute-start(bf16[2,112,128]{2,1,0:T(8,128)(2,1)S(1)} %shard_map.158.message), channel_id=1, source_target_pairs={{0,64},{64,128},{128,192},{192,256},{256,320},{320,384},{384,448},... | collective-permute-start | bytes 172040 | tf_op jit(solution)/shard_map/ppermute | solution.py:457

commit v7 on v6

--- a/solution.py
+++ b/solution.py
@@ -419,12 +419,12 @@
         5 * 10**6,
     )(here, there, w_keyval, received)
     even = permute(keyval, lambda z, y, c: (2 * z if z < 8 else 2 * (z - 8) + 1, y, c))
-    odd = permute(keyval, lambda z, y, c: (2 * z + 1 if z < 8 else 2 * (z - 8), y, c))
     mine, other = call(
         query_kernel, (wide, shape((ROWS, HEAD))), 4, partial_flops, 6 * 10**6
     )(here, there, w_query, after(received, keyval))
     other = swap(other, 1, 0)
-    near = after(jnp.concatenate([even, odd, sums]), mine)
+    odd = permute(after(even, mine), lambda z, y, c: (z ^ 1, y, c))
+    near = jnp.concatenate([even, odd, sums])
     far = swap(near, 1, 0)
     own, factors = call(
         sum_kernel, (shape((4, kv_width, ROWS)), wide), 4, 10**6, 10**6

time: 137 us -> 139 us (1.015)
  starting transfers between devices: 29.5 us -> 41.1 us
  waiting for transfers between devices: 19.9 us -> 9.86 us
    ppermute x10, starting transfers between devices: 24.1 us -> 36.1 us  [permute(): return lax.ppermute(x, LANES, pairs)]
    ppermute x10, waiting for transfers between devices: 18 us -> 7.64 us  [permute(): return lax.ppermute(x, LANES, pairs)]
where the time goes in v7:
time: 139 us; the launch traced here: 138 us
  blocking collectives  75.8 us (55%)
  starting transfers between devices  41.1 us (30%)
  Pallas kernels  10.3 us (7%)
  waiting for transfers between devices  9.86 us (7%)
    all_gather x2, blocking collectives, gather_z(): return lax.all_gather(x, 'z', axis=0)  75.8 us
    ppermute x10, starting transfers between devices, permute(): return lax.ppermute(x, LANES, pairs)  36.1 us
    ppermute x10, waiting for transfers between devices, permute(): return lax.ppermute(x, LANES, pairs)  7.64 us
    ppermute x1, starting transfers between devices, per_device(): lax.ppermute(message, 'section', [(i, i + 1) for i in range(sections - 1)])  5.04 us
    pallas_call x1, Pallas kernels, per_device(): pl.pallas_call(prepare, out_shape=(shape((ZN + ZN * kv_width // HEAD + EA...  3.76 us
  transfers between devices with their start and end apart: 11, of which 6 were waited for; matrix products, arithmetic and copies ran while one was open for 0% of the time, Pallas kernels for 3%

profile of v7, /device:TPU:6, one launch (start us, length us, event | category | flops | bytes accessed | tf_op | source)
XLA Modules:
  0.0 138.1 jit_solution(12440636089824906397)
XLA Ops:
  0.6 3.8 %shard_map.148 = (bf16[24,256,128]{2,1,0:T(8,128)(2,1)}, bf16[240,128]{1,0:T(8,128)(2,1)}, bf16[2,112,128]{2,1,0:T(8,128)(2,1)}) custom-call(s32[2,8]{1,0:T(2,128)} %bitcast.25, s32[1,2,112,128]{3,2,1,0:T(8,128)} %codes.1, s32[1,2,112]{2,1,0:T(2,128)} %exponents.1, bf16[1,3,112,128]{3,2,1,0:T(8,128)(2,1)} %buffer_in.3, bf16[1,128]{1,0:T(2,128)(2,1)} %gain.1, ...), custom_call_target="tpu_custom_call" | custom-call | flops 10000000 | bytes 4000000 | tf_op jit(solution)/shard_map/pallas_call | solution.py:378
  4.4 0.0 copy-start.2
  4.4 3.6 %collective-permute-start.1 = (bf16[24,256,128]{2,1,0:T(8,128)(2,1)}, bf16[24,256,128]{2,1,0:T(8,128)(2,1)S(1)}, u32[]{:S(2)}, u32[]{:S(2)}) collective-permute-start(bf16[24,256,128]{2,1,0:T(8,128)(2,1)} %get-tuple-element.19), channel_id=1, source_target_pairs={{0,2},{1,3},{2,0},{3,1},{4,6},{5,7},{6,4},{7,5},{8,10},{9,11},{10,... | collective-permute-start | bytes 4718600 | tf_op jit(solution)/shard_map/ppermute | solution.py:349
  8.0 42.1 %all-gather = bf16[3840,128]{1,0:T(8,128)(2,1)S(1)} all-gather(bf16[240,128]{1,0:T(8,128)(2,1)} %get-tuple-element.18), channel_id=2, replica_groups=mesh['section'=8,'z'=16,'y'=2,'core'=2] {'z'}, dimensions={0}, use_global_device_ids=true | all-gather | bytes 1044480 | tf_op jit(solution)/shard_map/all_gather | solution.py:361
  50.2 1.9 %collective-permute-start = (bf16[16,240,128]{2,1,0:T(8,128)(2,1)S(1)}, bf16[16,240,128]{2,1,0:T(8,128)(2,1)S(1)}, u32[]{:S(2)}, u32[]{:S(2)}) collective-permute-start(bf16[16,240,128]{2,1,0:T(8,128)(2,1)S(1)} %bitcast.11), channel_id=1, source_target_pairs={{0,1},{1,0},{2,3},{3,2},{4,5},{5,4},{6,7},{7,6},{8,9},{9,8},{10,11... | collective-permute-start | bytes 2949128 | tf_op jit(solution)/shard_map/ppermute | solution.py:349
  52.1 0.1 shard_map.151
  52.2 0.0 copy-start.1
  52.2 2.5 %collective-permute-start.5 = (bf16[12,256,128]{2,1,0:T(8,128)(2,1)S(1)}, bf16[12,256,128]{2,1,0:T(8,128)(2,1)S(1)}, u32[]{:S(2)}, u32[]{:S(2)}) collective-permute-start(bf16[12,256,128]{2,1,0:T(8,128)(2,1)S(1)} %shard_map.151), channel_id=1, source_target_pairs={{0,2},{1,3},{2,0},{3,1},{4,6},{5,7},{6,4},{7,5},{8,10},{9,11},{10,... | collective-permute-start | bytes 2359304 | tf_op jit(solution)/shard_map/ppermute | solution.py:349
  54.7 0.0 collective-permute-done.there
  54.7 0.0 collective-permute-done.1
  54.7 0.7 shard_map.149
  55.4 0.0 copy-start.8
  55.4 0.0 copy-start.9
  55.4 0.0 copy-start.6
  55.5 0.0 copy-start.7
  55.5 0.8 collective-permute-start.3
  56.3 0.0 copy-done.1
  56.3 0.7 shard_map.150
  57.0 0.0 collective-permute-done.3
  57.0 13.9 %collective-permute-start.4 = (bf16[64,224]{1,0:T(8,128)(2,1)S(1)}, bf16[64,224]{1,0:T(8,128)(2,1)S(1)}, u32[]{:S(2)}, u32[]{:S(2)}) collective-permute-start(bf16[64,224]{1,0:T(8,128)(2,1)S(1)} %collective-permute-done.3), channel_id=1, source_target_pairs={{0,4},{1,5},{2,6},{3,7},{4,0},{5,1},{6,2},{7,3},{8,12},{9,13},{10,... | collective-permute-start | bytes 86024 | tf_op jit(solution)/shard_map/ppermute | solution.py:349
  70.9 1.9 %collective-permute-done.4 = bf16[64,224]{1,0:T(8,128)(2,1)S(1)} collective-permute-done((bf16[64,224]{1,0:T(8,128)(2,1)S(1)}, bf16[64,224]{1,0:T(8,128)(2,1)S(1)}, u32[]{:S(2)}, u32[]{:S(2)}) %collective-permute-start.4) | collective-permute-done | bytes 28704 | tf_op jit(solution)/shard_map/ppermute | solution.py:349
  72.8 3.5 %collective-permute-start.6 = (bf16[144,224]{1,0:T(8,128)(2,1)S(1)}, bf16[144,224]{1,0:T(8,128)(2,1)S(1)}, u32[]{:S(2)}, u32[]{:S(2)}) collective-permute-start(bf16[144,224]{1,0:T(8,128)(2,1)S(1)} %constant_dynamic-update-slice_fusion.near), channel_id=1, source_target_pairs={{0,2},{1,3},{2,0},{3,1},{4,6},{5,7},{6,4},{7,5},{8,10},{9,11},{10,... | collective-permute-start | bytes 193544 | tf_op jit(solution)/shard_map/ppermute | solution.py:349
  76.3 2.4 %collective-permute-start.2 = (bf16[224,128]{1,0:T(8,128)(2,1)S(1)}, bf16[224,128]{1,0:T(8,128)(2,1)S(1)}, u32[]{:S(2)}, u32[]{:S(2)}) collective-permute-start(bf16[224,128]{1,0:T(8,128)(2,1)S(1)} %get-tuple-element.23), channel_id=1, source_target_pairs={{0,2},{1,3},{2,0},{3,1},{4,6},{5,7},{6,4},{7,5},{8,10},{9,11},{10,... | collective-permute-start | bytes 172040 | tf_op jit(solution)/shard_map/ppermute | solution.py:349
  78.7 0.0 collective-permute-done.5
  78.7 0.4 collective-permute-done.6.far
  79.1 0.1 shard_map.152
  79.2 1.9 %collective-permute-start.7 = (bf16[4,32,224]{2,1,0:T(8,128)(2,1)S(1)}, bf16[4,32,224]{2,1,0:T(8,128)(2,1)S(1)}, u32[]{:S(2)}, u32[]{:S(2)}) collective-permute-start(bf16[4,32,224]{2,1,0:T(8,128)(2,1)S(1)} %get-tuple-element.28.own), channel_id=1, source_target_pairs={{0,1},{1,0},{2,3},{3,2},{4,5},{5,4},{6,7},{7,6},{8,9},{9,8},{10,11... | collective-permute-start | bytes 172040 | tf_op jit(solution)/shard_map/ppermute | solution.py:349
  81.1 1.3 collective-permute-done.2.other
  82.4 0.2 shard_map.153.query
  82.6 0.0 collective-permute-done.7.sibling
  82.6 0.5 shard_map.154
  83.1 33.6 %all-gather.1 = bf16[3584,128]{1,0:T(8,128)(2,1)S(1)} all-gather(bf16[224,128]{1,0:T(8,128)(2,1)S(1)} %shard_map.154), channel_id=3, replica_groups=mesh['section'=8,'z'=16,'y'=2,'core'=2] {'z'}, dimensions={0}, use_global_device_ids=true | all-gather | bytes 974848 | tf_op jit(solution)/shard_map/all_gather | solution.py:361
  116.7 1.9 %collective-permute-start.8 = (bf16[16,224,128]{2,1,0:T(8,128)(2,1)S(1)}, bf16[16,224,128]{2,1,0:T(8,128)(2,1)S(1)}, u32[]{:S(2)}, u32[]{:S(2)}) collective-permute-start(bf16[16,224,128]{2,1,0:T(8,128)(2,1)S(1)} %bitcast.17), channel_id=1, source_target_pairs={{0,1},{1,0},{2,3},{3,2},{4,5},{5,4},{6,7},{7,6},{8,9},{9,8},{10,11... | collective-permute-start | bytes 2752520 | tf_op jit(solution)/shard_map/ppermute | solution.py:349
  118.7 0.4 shard_map.155.acc
  119.1 2.0 %collective-permute-done.8.line = bf16[16,224,128]{2,1,0:T(8,128)(2,1)S(1)} collective-permute-done((bf16[16,224,128]{2,1,0:T(8,128)(2,1)S(1)}, bf16[16,224,128]{2,1,0:T(8,128)(2,1)S(1)}, u32[]{:S(2)}, u32[]{:S(2)}) %collective-permute-start.8) | collective-permute-done | bytes 917536 | tf_op jit(solution)/shard_map/ppermute | solution.py:349
  121.1 0.4 shard_map.157
  121.5 0.0 copy-start.3
  121.5 0.0 copy-start.5
  121.5 0.0 copy-start.10
  121.5 0.0 copy-start.4
  121.5 3.7 %collective-permute-start.9 = (bf16[224,128]{1,0:T(8,128)(2,1)S(1)}, bf16[224,128]{1,0:T(8,128)(2,1)S(1)}, u32[]{:S(2)}, u32[]{:S(2)}) collective-permute-start(bf16[224,128]{1,0:T(8,128)(2,1)S(1)} %shard_map.157), channel_id=1, source_target_pairs={{0,2},{1,3},{2,0},{3,1},{4,6},{5,7},{6,4},{7,5},{8,10},{9,11},{10,... | collective-permute-start | bytes 172040 | tf_op jit(solution)/shard_map/ppermute | solution.py:349
  125.2 0.4 shard_map.156.mine
  125.6 2.1 %collective-permute-done.9.other = bf16[224,128]{1,0:T(8,128)(2,1)S(1)} collective-permute-done((bf16[224,128]{1,0:T(8,128)(2,1)S(1)}, bf16[224,128]{1,0:T(8,128)(2,1)S(1)}, u32[]{:S(2)}, u32[]{:S(2)}) %collective-permute-start.9) | collective-permute-done | bytes 57376 | tf_op jit(solution)/shard_map/ppermute | solution.py:349
  127.7 0.6 shard_map.158.message
  128.3 5.0 %collective-permute-start.10 = (bf16[2,112,128]{2,1,0:T(8,128)(2,1)S(1)}, bf16[2,112,128]{2,1,0:T(8,128)(2,1)S(1)}, u32[]{:S(2)}, u32[]{:S(2)}) collective-permute-start(bf16[2,112,128]{2,1,0:T(8,128)(2,1)S(1)} %shard_map.158.message), channel_id=1, source_target_pairs={{0,64},{64,128},{128,192},{192,256},{256,320},{320,384},{384,448},... | collective-permute-start | bytes 172040 | tf_op jit(solution)/shard_map/ppermute | solution.py:457
  133.4 1.2 shard_map.160
  134.6 2.2 %collective-permute-done.10.arrived = bf16[2,112,128]{2,1,0:T(8,128)(2,1)S(1)} collective-permute-done((bf16[2,112,128]{2,1,0:T(8,128)(2,1)S(1)}, bf16[2,112,128]{2,1,0:T(8,128)(2,1)S(1)}, u32[]{:S(2)}, u32[]{:S(2)}) %collective-permute-start.10) | collective-permute-done | bytes 57376 | tf_op jit(solution)/shard_map/ppermute | solution.py:457
  136.8 1.3 shard_map.159
  (15 shorter events, 0.1 us)
Async XLA Ops:
  0.6 51.5 %copy-start = (bf16[1,8192,128]{2,1,0:T(8,128)(2,1)S(1)}, bf16[1,8192,128]{2,1,0:T(8,128)(2,1)}, u32[]{:S(2)}) copy-start(bf16[1,8192,128]{2,1,0:T(8,128)(2,1)} %weight.5) | copy-start | bytes 6291460
  4.4 50.3 %copy-start.2 = (bf16[1,8192,32]{1,2,0:T(8,128)(2,1)S(1)}, bf16[1,8192,32]{1,2,0:T(8,128)(2,1)}, u32[]{:S(2)}) copy-start(bf16[1,8192,32]{1,2,0:T(8,128)(2,1)} %param.20) | copy-start | bytes 1572868
  4.4 50.3 %collective-permute-start.1 = (bf16[24,256,128]{2,1,0:T(8,128)(2,1)}, bf16[24,256,128]{2,1,0:T(8,128)(2,1)S(1)}, u32[]{:S(2)}, u32[]{:S(2)}) collective-permute-start(bf16[24,256,128]{2,1,0:T(8,128)(2,1)} %get-tuple-element.19), channel_id=1, source_target_pairs={{0,2},{1,3},{2,0},{3,1},{4,6},{5,7},{6,4},{7,5},{8,10},{9,11},{10,... | collective-permute-start | bytes 4718600 | tf_op jit(solution)/shard_map/ppermute | solution.py:349
  50.2 4.5 %collective-permute-start = (bf16[16,240,128]{2,1,0:T(8,128)(2,1)S(1)}, bf16[16,240,128]{2,1,0:T(8,128)(2,1)S(1)}, u32[]{:S(2)}, u32[]{:S(2)}) collective-permute-start(bf16[16,240,128]{2,1,0:T(8,128)(2,1)S(1)} %bitcast.11), channel_id=1, source_target_pairs={{0,1},{1,0},{2,3},{3,2},{4,5},{5,4},{6,7},{7,6},{8,9},{9,8},{10,11... | collective-permute-start | bytes 2949128 | tf_op jit(solution)/shard_map/ppermute | solution.py:349
  52.2 4.1 %copy-start.1 = (bf16[1,8192,128]{2,1,0:T(8,128)(2,1)S(1)}, bf16[1,8192,128]{2,1,0:T(8,128)(2,1)}, u32[]{:S(2)}) copy-start(bf16[1,8192,128]{2,1,0:T(8,128)(2,1)} %weight.3) | copy-start | bytes 6291460
  52.2 26.5 %collective-permute-start.5 = (bf16[12,256,128]{2,1,0:T(8,128)(2,1)S(1)}, bf16[12,256,128]{2,1,0:T(8,128)(2,1)S(1)}, u32[]{:S(2)}, u32[]{:S(2)}) collective-permute-start(bf16[12,256,128]{2,1,0:T(8,128)(2,1)S(1)} %shard_map.151), channel_id=1, source_target_pairs={{0,2},{1,3},{2,0},{3,1},{4,6},{5,7},{6,4},{7,5},{8,10},{9,11},{10,... | collective-permute-start | bytes 2359304 | tf_op jit(solution)/shard_map/ppermute | solution.py:349
  55.4 23.6 %copy-start.8 = (f32[64,224]{1,0:T(8,128)S(1)}, f32[64,224]{1,0:T(8,128)}, u32[]{:S(2)}) copy-start(f32[64,224]{1,0:T(8,128)} %constant.8.clone.cos_t) | copy-start | bytes 172036
  55.4 23.6 %copy-start.9 = (f32[64,224]{1,0:T(8,128)S(1)}, f32[64,224]{1,0:T(8,128)}, u32[]{:S(2)}) copy-start(f32[64,224]{1,0:T(8,128)} %constant.9.clone.sin_t) | copy-start | bytes 172036
  55.4 26.9 %copy-start.6 = (f32[224,64]{1,0:T(8,128)S(1)}, f32[224,64]{1,0:T(8,128)}, u32[]{:S(2)}) copy-start(f32[224,64]{1,0:T(8,128)} %constant.10.clone.cos) | copy-start | bytes 172036
  55.5 26.9 %copy-start.7 = (f32[224,64]{1,0:T(8,128)S(1)}, f32[224,64]{1,0:T(8,128)}, u32[]{:S(2)}) copy-start(f32[224,64]{1,0:T(8,128)} %constant.11.clone.sin) | copy-start | bytes 172036
  55.5 1.5 %collective-permute-start.3 = (bf16[64,224]{1,0:T(8,128)(2,1)S(1)}, bf16[64,224]{1,0:T(8,128)(2,1)S(1)}, u32[]{:S(2)}, u32[]{:S(2)}) collective-permute-start(bf16[64,224]{1,0:T(8,128)(2,1)S(1)} %get-tuple-element.20), channel_id=1, source_target_pairs={{0,0},{1,1},{2,2},{3,3},{4,8},{5,9},{6,10},{7,11},{8,16},{9,17},{1... | collective-permute-start | bytes 86024 | tf_op jit(solution)/shard_map/ppermute | solution.py:349
  57.0 15.8 %collective-permute-start.4 = (bf16[64,224]{1,0:T(8,128)(2,1)S(1)}, bf16[64,224]{1,0:T(8,128)(2,1)S(1)}, u32[]{:S(2)}, u32[]{:S(2)}) collective-permute-start(bf16[64,224]{1,0:T(8,128)(2,1)S(1)} %collective-permute-done.3), channel_id=1, source_target_pairs={{0,4},{1,5},{2,6},{3,7},{4,0},{5,1},{6,2},{7,3},{8,12},{9,13},{10,... | collective-permute-start | bytes 86024 | tf_op jit(solution)/shard_map/ppermute | solution.py:349
  72.8 6.2 %collective-permute-start.6 = (bf16[144,224]{1,0:T(8,128)(2,1)S(1)}, bf16[144,224]{1,0:T(8,128)(2,1)S(1)}, u32[]{:S(2)}, u32[]{:S(2)}) collective-permute-start(bf16[144,224]{1,0:T(8,128)(2,1)S(1)} %constant_dynamic-update-slice_fusion.near), channel_id=1, source_target_pairs={{0,2},{1,3},{2,0},{3,1},{4,6},{5,7},{6,4},{7,5},{8,10},{9,11},{10,... | collective-permute-start | bytes 193544 | tf_op jit(solution)/shard_map/ppermute | solution.py:349
  76.3 6.1 %collective-permute-start.2 = (bf16[224,128]{1,0:T(8,128)(2,1)S(1)}, bf16[224,128]{1,0:T(8,128)(2,1)S(1)}, u32[]{:S(2)}, u32[]{:S(2)}) collective-permute-start(bf16[224,128]{1,0:T(8,128)(2,1)S(1)} %get-tuple-element.23), channel_id=1, source_target_pairs={{0,2},{1,3},{2,0},{3,1},{4,6},{5,7},{6,4},{7,5},{8,10},{9,11},{10,... | collective-permute-start | bytes 172040 | tf_op jit(solution)/shard_map/ppermute | solution.py:349
  79.2 3.4 %collective-permute-start.7 = (bf16[4,32,224]{2,1,0:T(8,128)(2,1)S(1)}, bf16[4,32,224]{2,1,0:T(8,128)(2,1)S(1)}, u32[]{:S(2)}, u32[]{:S(2)}) collective-permute-start(bf16[4,32,224]{2,1,0:T(8,128)(2,1)S(1)} %get-tuple-element.28.own), channel_id=1, source_target_pairs={{0,1},{1,0},{2,3},{3,2},{4,5},{5,4},{6,7},{7,6},{8,9},{9,8},{10,11... | collective-permute-start | bytes 172040 | tf_op jit(solution)/shard_map/ppermute | solution.py:349
  116.7 4.4 %collective-permute-start.8 = (bf16[16,224,128]{2,1,0:T(8,128)(2,1)S(1)}, bf16[16,224,128]{2,1,0:T(8,128)(2,1)S(1)}, u32[]{:S(2)}, u32[]{:S(2)}) collective-permute-start(bf16[16,224,128]{2,1,0:T(8,128)(2,1)S(1)} %bitcast.17), channel_id=1, source_target_pairs={{0,1},{1,0},{2,3},{3,2},{4,5},{5,4},{6,7},{7,6},{8,9},{9,8},{10,11... | collective-permute-start | bytes 2752520 | tf_op jit(solution)/shard_map/ppermute | solution.py:349
  121.5 6.3 %copy-start.3 = (bf16[1,3,112,128]{3,2,1,0:T(8,128)(2,1)S(1)}, bf16[1,3,112,128]{3,2,1,0:T(8,128)(2,1)}, u32[]{:S(2)}) copy-start(bf16[1,3,112,128]{3,2,1,0:T(8,128)(2,1)} %buffer_out.3) | copy-start | bytes 258052
  121.5 6.2 %copy-start.5 = (bf16[2,112,128]{2,1,0:T(8,128)(2,1)S(1)}, bf16[2,112,128]{2,1,0:T(8,128)(2,1)}, u32[]{:S(2)}) copy-start(bf16[2,112,128]{2,1,0:T(8,128)(2,1)} %get-tuple-element.17.inputs) | copy-start | bytes 172036
  121.5 6.2 %copy-start.10 = (s32[8,2]{0,1:T(2,128)S(1)}, s32[8,2]{0,1:T(2,128)}, u32[]{:S(2)}) copy-start(s32[8,2]{0,1:T(2,128)} %param.15) | copy-start | bytes 196
  121.5 15.3 %copy-start.4 = (bf16[1,3,112,128]{3,2,1,0:T(8,128)(2,1)S(1)}, bf16[1,3,112,128]{3,2,1,0:T(8,128)(2,1)}, u32[]{:S(2)}) copy-start(bf16[1,3,112,128]{3,2,1,0:T(8,128)(2,1)} %buffer_in.3) | copy-start | bytes 258052
  121.5 6.2 %collective-permute-start.9 = (bf16[224,128]{1,0:T(8,128)(2,1)S(1)}, bf16[224,128]{1,0:T(8,128)(2,1)S(1)}, u32[]{:S(2)}, u32[]{:S(2)}) collective-permute-start(bf16[224,128]{1,0:T(8,128)(2,1)S(1)} %shard_map.157), channel_id=1, source_target_pairs={{0,2},{1,3},{2,0},{3,1},{4,6},{5,7},{6,4},{7,5},{8,10},{9,11},{10,... | collective-permute-start | bytes 172040 | tf_op jit(solution)/shard_map/ppermute | solution.py:349
  128.3 8.5 %collective-permute-start.10 = (bf16[2,112,128]{2,1,0:T(8,128)(2,1)S(1)}, bf16[2,112,128]{2,1,0:T(8,128)(2,1)S(1)}, u32[]{:S(2)}, u32[]{:S(2)}) collective-permute-start(bf16[2,112,128]{2,1,0:T(8,128)(2,1)S(1)} %shard_map.158.message), channel_id=1, source_target_pairs={{0,64},{64,128},{128,192},{192,256},{256,320},{320,384},{384,448},... | collective-permute-start | bytes 172040 | tf_op jit(solution)/shard_map/ppermute | solution.py:457

commit v8 on v7

--- a/solution.py
+++ b/solution.py
@@ -198,7 +198,8 @@
 
 
 def sum_kernel(near, far, cos_t, sin_t, out, factors_out):
-    z_odd, y, core = lax.axis_index("z") % 2, lax.axis_index("y"), lax.axis_index("core")
+    y, core = lax.axis_index("y"), lax.axis_index("core")
+    keys = lax.axis_index("z") % 2 == core
     width = (near.shape[0] - (PAY - ROWS)) // 4
     tail = near[4 * width :, :].astype(jnp.float32) + far[4 * width :, :].astype(jnp.float32)
     square_sum = tail[0:1, :] + tail[1:2, :]
@@ -206,19 +207,19 @@
     factors = jnp.broadcast_to(inverse, (width, ROWS))
     factors_out[...] = jnp.broadcast_to(inverse, (HEAD, ROWS)).T
 
-    def piece(kind, which):
-        plane = z_odd ^ kind
-        a = near[pl.ds(pl.multiple_of((plane * 2 + (which ^ y)) * width, width), width), :]
-        b = far[pl.ds(pl.multiple_of((plane * 2 + 1 - (which ^ y)) * width, width), width), :]
-        return ((a.astype(jnp.float32) + b.astype(jnp.float32)) * factors).astype(jnp.bfloat16)
-
-    first, second = piece(0, 0).astype(jnp.float32), piece(0, 1).astype(jnp.float32)
-    rows = pl.ds(pl.multiple_of(core * width, width), width)
-    c, s = cos_t[rows, :], sin_t[rows, :]
-    out[0] = (first * c - second * s).astype(jnp.bfloat16)
-    out[1] = (second * c + first * s).astype(jnp.bfloat16)
-    out[2] = piece(1, 0)
-    out[3] = piece(1, 1)
+    def piece(which, side):
+        spot = (side ^ core) * 2
+        a = near[pl.ds(pl.multiple_of((spot + (which ^ y)) * width, width), width), :]
+        b = far[pl.ds(pl.multiple_of((spot + 1 - (which ^ y)) * width, width), width), :]
+        total = (a.astype(jnp.float32) + b.astype(jnp.float32)) * factors
+        return total.astype(jnp.bfloat16).astype(jnp.float32)
+
+    for side in range(CN):
+        first, second = piece(0, side), piece(1, side)
+        rows = slice(side * width, (side + 1) * width)
+        c, s = cos_t[rows, :], sin_t[rows, :]
+        out[0, rows, :] = jnp.where(keys, first * c - second * s, first).astype(jnp.bfloat16)
+        out[1, rows, :] = jnp.where(keys, second * c + first * s, second).astype(jnp.bfloat16)
 
 
 def rope_kernel(mine, other, factors, cos, sin, out):
@@ -231,15 +232,10 @@
 
 
 def attention_kernel(query, own, sibling, out):
-    core = lax.axis_index("core")
-    keys_values = []
-    for kind in range(2):
-        parts = []
-        for which in range(2):
-            a, b = own[2 * kind + which], sibling[2 * kind + which]
-            parts += [jnp.where(core == 0, a, b), jnp.where(core == 0, b, a)]
-        keys_values.append(jnp.concatenate(parts, axis=0))
-    keys, values = keys_values
+    here = jnp.concatenate([own[0], own[1]], axis=0)
+    there = jnp.concatenate([sibling[0], sibling[1]], axis=0)
+    has_keys = lax.axis_index("z") % 2 == lax.axis_index("core")
+    keys, values = jnp.where(has_keys, here, there), jnp.where(has_keys, there, here)
     scores = jnp.dot(query[...], keys, preferred_element_type=jnp.float32) / math.sqrt(HEAD)
     row = lax.broadcasted_iota(jnp.int32, (ROWS, ROWS), 0)
     column = lax.broadcasted_iota(jnp.int32, (ROWS, ROWS), 1)
@@ -351,6 +347,11 @@
 
 def swap(x, flip_y, flip_core):
     return permute(x, lambda z, y, c: (z, y ^ flip_y, c ^ flip_core))
+
+
+def pair_plane(z, y, c):
+    kind, g = z // KV_HEADS, z % KV_HEADS
+    return 2 * g + (kind ^ c), y, c
 
 
 def after(x, earlier):
@@ -418,16 +419,16 @@
         partial_flops,
         5 * 10**6,
     )(here, there, w_keyval, received)
-    even = permute(keyval, lambda z, y, c: (2 * z if z < 8 else 2 * (z - 8) + 1, y, c))
+    keyval = jnp.concatenate([keyval, swap(keyval, 0, 1)])
+    keyval = permute(keyval, pair_plane)
     mine, other = call(
         query_kernel, (wide, shape((ROWS, HEAD))), 4, partial_flops, 6 * 10**6
-    )(here, there, w_query, after(received, keyval))
+    )(here, there, w_query, after(received, sums))
     other = swap(other, 1, 0)
-    odd = permute(after(even, mine), lambda z, y, c: (z ^ 1, y, c))
-    near = jnp.concatenate([even, odd, sums])
+    near = after(jnp.concatenate([keyval, sums]), mine)
     far = swap(near, 1, 0)
     own, factors = call(
-        sum_kernel, (shape((4, kv_width, ROWS)), wide), 4, 10**6, 10**6
+        sum_kernel, (shape((2, HEAD // 2, ROWS)), wide), 4, 10**6, 10**6
     )(after(near, received_out), far, cos.T.copy(), sin.T.copy())
     sibling = swap(own, 0, 1)
     queries = call(rope_kernel, shape((ROWS, HEAD)), 5, 10**6, 10**6)(

time: 139 us -> 137 us (0.986)
  starting transfers between devices: 41.1 us -> 33.1 us
  waiting for transfers between devices: 9.86 us -> 17.7 us
    ppermute x10, starting transfers between devices: 36.1 us -> 28.3 us  [permute(): return lax.ppermute(x, LANES, pairs)]
    ppermute x10, waiting for transfers between devices: 7.64 us -> 15.3 us  [permute(): return lax.ppermute(x, LANES, pairs)]
  transfers between devices with their start and end apart: 11 -> 11, of which waited for: 6 -> 8; matrix products, arithmetic and copies ran while one was open for 0% -> 0% of each run, Pallas kernels for 3% -> 3%
where the time goes in v8:
time: 137 us
  blocking collectives  74.8 us (55%)
  starting transfers between devices  33.1 us (24%)
  waiting for transfers between devices  17.7 us (13%)
  Pallas kernels  10.3 us (8%)
    all_gather x2, blocking collectives, gather_z(): return lax.all_gather(x, 'z', axis=0)  74.8 us
    ppermute x10, starting transfers between devices, permute(): return lax.ppermute(x, LANES, pairs)  28.3 us
    ppermute x10, waiting for transfers between devices, permute(): return lax.ppermute(x, LANES, pairs)  15.3 us
    ppermute x1, starting transfers between devices, per_device(): lax.ppermute(message, 'section', [(i, i + 1) for i in range(sections - 1)])  4.76 us
    pallas_call x1, Pallas kernels, per_device(): pl.pallas_call(prepare, out_shape=(shape((ZN + ZN * kv_width // HEAD + EA...  3.76 us
  transfers between devices with their start and end apart: 11, of which 8 were waited for; matrix products, arithmetic and copies ran while one was open for 0% of the time, Pallas kernels for 3%

profile of v8, /device:TPU:6, one launch (start us, length us, event | category | flops | bytes accessed | tf_op | source)
XLA Modules:
  0.0 136.9 jit_solution(2879558202784968019)
XLA Ops:
  0.6 3.8 %shard_map.148 = (bf16[24,256,128]{2,1,0:T(8,128)(2,1)}, bf16[240,128]{1,0:T(8,128)(2,1)}, bf16[2,112,128]{2,1,0:T(8,128)(2,1)}) custom-call(s32[2,8]{1,0:T(2,128)} %bitcast.25, s32[1,2,112,128]{3,2,1,0:T(8,128)} %codes.1, s32[1,2,112]{2,1,0:T(2,128)} %exponents.1, bf16[1,3,112,128]{3,2,1,0:T(8,128)(2,1)} %buffer_in.3, bf16[1,128]{1,0:T(2,128)(2,1)} %gain.1, ...), custom_call_target="tpu_custom_call" | custom-call | flops 10000000 | bytes 4000000 | tf_op jit(solution)/shard_map/pallas_call | solution.py:379
  4.4 0.0 copy-start.2
  4.4 3.6 %collective-permute-start.1 = (bf16[24,256,128]{2,1,0:T(8,128)(2,1)}, bf16[24,256,128]{2,1,0:T(8,128)(2,1)S(1)}, u32[]{:S(2)}, u32[]{:S(2)}) collective-permute-start(bf16[24,256,128]{2,1,0:T(8,128)(2,1)} %get-tuple-element.19), channel_id=1, source_target_pairs={{0,2},{1,3},{2,0},{3,1},{4,6},{5,7},{6,4},{7,5},{8,10},{9,11},{10,... | collective-permute-start | bytes 4718600 | tf_op jit(solution)/shard_map/ppermute | solution.py:345
  8.0 42.1 %all-gather = bf16[3840,128]{1,0:T(8,128)(2,1)S(1)} all-gather(bf16[240,128]{1,0:T(8,128)(2,1)} %get-tuple-element.18), channel_id=2, replica_groups=mesh['section'=8,'z'=16,'y'=2,'core'=2] {'z'}, dimensions={0}, use_global_device_ids=true | all-gather | bytes 1044480 | tf_op jit(solution)/shard_map/all_gather | solution.py:362
  50.2 1.9 %collective-permute-start = (bf16[16,240,128]{2,1,0:T(8,128)(2,1)S(1)}, bf16[16,240,128]{2,1,0:T(8,128)(2,1)S(1)}, u32[]{:S(2)}, u32[]{:S(2)}) collective-permute-start(bf16[16,240,128]{2,1,0:T(8,128)(2,1)S(1)} %bitcast.11), channel_id=1, source_target_pairs={{0,1},{1,0},{2,3},{3,2},{4,5},{5,4},{6,7},{7,6},{8,9},{9,8},{10,11... | collective-permute-start | bytes 2949128 | tf_op jit(solution)/shard_map/ppermute | solution.py:345
  52.1 0.1 shard_map.151
  52.2 2.4 %collective-permute-start.5 = (bf16[12,256,128]{2,1,0:T(8,128)(2,1)S(1)}, bf16[12,256,128]{2,1,0:T(8,128)(2,1)S(1)}, u32[]{:S(2)}, u32[]{:S(2)}) collective-permute-start(bf16[12,256,128]{2,1,0:T(8,128)(2,1)S(1)} %shard_map.151), channel_id=1, source_target_pairs={{0,2},{1,3},{2,0},{3,1},{4,6},{5,7},{6,4},{7,5},{8,10},{9,11},{10,... | collective-permute-start | bytes 2359304 | tf_op jit(solution)/shard_map/ppermute | solution.py:345
  54.6 0.1 collective-permute-done.there
  54.6 0.0 collective-permute-done.1
  54.6 0.0 copy-done.2
  54.6 0.7 shard_map.149
  55.3 2.1 %collective-permute-start.3 = (bf16[64,224]{1,0:T(8,128)(2,1)S(1)}, bf16[64,224]{1,0:T(8,128)(2,1)S(1)}, u32[]{:S(2)}, u32[]{:S(2)}) collective-permute-start(bf16[64,224]{1,0:T(8,128)(2,1)S(1)} %get-tuple-element.24), channel_id=1, source_target_pairs={{0,1},{1,0},{2,3},{3,2},{4,5},{5,4},{6,7},{7,6},{8,9},{9,8},{10,11... | collective-permute-start | bytes 86024 | tf_op jit(solution)/shard_map/ppermute | solution.py:345
  57.4 1.0 collective-permute-done.3
  58.5 0.7 collective-permute-start.4
  59.1 0.0 copy-start.8
  59.1 0.0 copy-start.9
  59.2 0.0 copy-start.6
  59.2 0.0 copy-start.7
  59.2 0.7 shard_map.150
  59.9 0.0 collective-permute-done.4
  59.9 3.4 %collective-permute-start.6 = (bf16[144,224]{1,0:T(8,128)(2,1)S(1)}, bf16[144,224]{1,0:T(8,128)(2,1)S(1)}, u32[]{:S(2)}, u32[]{:S(2)}) collective-permute-start(bf16[144,224]{1,0:T(8,128)(2,1)S(1)} %pad_maximum_fusion.near), channel_id=1, source_target_pairs={{0,2},{1,3},{2,0},{3,1},{4,6},{5,7},{6,4},{7,5},{8,10},{9,11},{10,... | collective-permute-start | bytes 193544 | tf_op jit(solution)/shard_map/ppermute | solution.py:345
  63.3 2.4 %collective-permute-start.2 = (bf16[224,128]{1,0:T(8,128)(2,1)S(1)}, bf16[224,128]{1,0:T(8,128)(2,1)S(1)}, u32[]{:S(2)}, u32[]{:S(2)}) collective-permute-start(bf16[224,128]{1,0:T(8,128)(2,1)S(1)} %get-tuple-element.23), channel_id=1, source_target_pairs={{0,2},{1,3},{2,0},{3,1},{4,6},{5,7},{6,4},{7,5},{8,10},{9,11},{10,... | collective-permute-start | bytes 172040 | tf_op jit(solution)/shard_map/ppermute | solution.py:345
  65.8 8.3 %collective-permute-done.5 = bf16[12,256,128]{2,1,0:T(8,128)(2,1)S(1)} collective-permute-done((bf16[12,256,128]{2,1,0:T(8,128)(2,1)S(1)}, bf16[12,256,128]{2,1,0:T(8,128)(2,1)S(1)}, u32[]{:S(2)}, u32[]{:S(2)}) %collective-permute-start.5) | collective-permute-done | bytes 786464 | tf_op jit(solution)/shard_map/ppermute | solution.py:345
  74.0 0.8 collective-permute-done.6.far
  74.8 0.1 shard_map.152
  74.9 6.6 %collective-permute-start.7 = (bf16[2,64,224]{2,1,0:T(8,128)(2,1)S(1)}, bf16[2,64,224]{2,1,0:T(8,128)(2,1)S(1)}, u32[]{:S(2)}, u32[]{:S(2)}) collective-permute-start(bf16[2,64,224]{2,1,0:T(8,128)(2,1)S(1)} %get-tuple-element.28.own), channel_id=1, source_target_pairs={{0,1},{1,0},{2,3},{3,2},{4,5},{5,4},{6,7},{7,6},{8,9},{9,8},{10,11... | collective-permute-start | bytes 172040 | tf_op jit(solution)/shard_map/ppermute | solution.py:345
  81.5 0.0 collective-permute-done.2.other
  81.6 0.0 copy-done.6
  81.6 0.2 shard_map.153.query
  81.8 0.6 collective-permute-done.7.sibling
  82.4 0.5 shard_map.154
  82.9 32.7 %all-gather.1 = bf16[3584,128]{1,0:T(8,128)(2,1)S(1)} all-gather(bf16[224,128]{1,0:T(8,128)(2,1)S(1)} %shard_map.154), channel_id=3, replica_groups=mesh['section'=8,'z'=16,'y'=2,'core'=2] {'z'}, dimensions={0}, use_global_device_ids=true | all-gather | bytes 974848 | tf_op jit(solution)/shard_map/all_gather | solution.py:362
  115.6 1.9 %collective-permute-start.8 = (bf16[16,224,128]{2,1,0:T(8,128)(2,1)S(1)}, bf16[16,224,128]{2,1,0:T(8,128)(2,1)S(1)}, u32[]{:S(2)}, u32[]{:S(2)}) collective-permute-start(bf16[16,224,128]{2,1,0:T(8,128)(2,1)S(1)} %bitcast.17), channel_id=1, source_target_pairs={{0,1},{1,0},{2,3},{3,2},{4,5},{5,4},{6,7},{7,6},{8,9},{9,8},{10,11... | collective-permute-start | bytes 2752520 | tf_op jit(solution)/shard_map/ppermute | solution.py:345
  117.5 0.4 shard_map.155.acc
  118.0 2.0 %collective-permute-done.8.line = bf16[16,224,128]{2,1,0:T(8,128)(2,1)S(1)} collective-permute-done((bf16[16,224,128]{2,1,0:T(8,128)(2,1)S(1)}, bf16[16,224,128]{2,1,0:T(8,128)(2,1)S(1)}, u32[]{:S(2)}, u32[]{:S(2)}) %collective-permute-start.8) | collective-permute-done | bytes 917536 | tf_op jit(solution)/shard_map/ppermute | solution.py:345
  120.0 0.4 shard_map.157
  120.4 0.0 copy-start.3
  120.4 0.0 copy-start.5
  120.4 0.0 copy-start.10
  120.4 0.0 copy-start.4
  120.4 3.3 %collective-permute-start.9 = (bf16[224,128]{1,0:T(8,128)(2,1)S(1)}, bf16[224,128]{1,0:T(8,128)(2,1)S(1)}, u32[]{:S(2)}, u32[]{:S(2)}) collective-permute-start(bf16[224,128]{1,0:T(8,128)(2,1)S(1)} %shard_map.157), channel_id=1, source_target_pairs={{0,2},{1,3},{2,0},{3,1},{4,6},{5,7},{6,4},{7,5},{8,10},{9,11},{10,... | collective-permute-start | bytes 172040 | tf_op jit(solution)/shard_map/ppermute | solution.py:345
  123.7 0.4 shard_map.156.mine
  124.1 2.5 %collective-permute-done.9.other = bf16[224,128]{1,0:T(8,128)(2,1)S(1)} collective-permute-done((bf16[224,128]{1,0:T(8,128)(2,1)S(1)}, bf16[224,128]{1,0:T(8,128)(2,1)S(1)}, u32[]{:S(2)}, u32[]{:S(2)}) %collective-permute-start.9) | collective-permute-done | bytes 57376 | tf_op jit(solution)/shard_map/ppermute | solution.py:345
  126.6 0.6 shard_map.158.message
  127.2 4.8 %collective-permute-start.10 = (bf16[2,112,128]{2,1,0:T(8,128)(2,1)S(1)}, bf16[2,112,128]{2,1,0:T(8,128)(2,1)S(1)}, u32[]{:S(2)}, u32[]{:S(2)}) collective-permute-start(bf16[2,112,128]{2,1,0:T(8,128)(2,1)S(1)} %shard_map.158.message), channel_id=1, source_target_pairs={{0,64},{64,128},{128,192},{192,256},{256,320},{320,384},{384,448},... | collective-permute-start | bytes 172040 | tf_op jit(solution)/shard_map/ppermute | solution.py:458
  132.0 1.2 shard_map.160
  133.2 2.5 %collective-permute-done.10.arrived = bf16[2,112,128]{2,1,0:T(8,128)(2,1)S(1)} collective-permute-done((bf16[2,112,128]{2,1,0:T(8,128)(2,1)S(1)}, bf16[2,112,128]{2,1,0:T(8,128)(2,1)S(1)}, u32[]{:S(2)}, u32[]{:S(2)}) %collective-permute-start.10) | collective-permute-done | bytes 57376 | tf_op jit(solution)/shard_map/ppermute | solution.py:458
  135.7 1.3 shard_map.159
  (14 shorter events, 0.1 us)
Async XLA Ops:
  0.6 51.5 %copy-start = (bf16[1,8192,128]{2,1,0:T(8,128)(2,1)S(1)}, bf16[1,8192,128]{2,1,0:T(8,128)(2,1)}, u32[]{:S(2)}) copy-start(bf16[1,8192,128]{2,1,0:T(8,128)(2,1)} %weight.5) | copy-start | bytes 6291460
  4.4 50.2 %copy-start.2 = (bf16[1,8192,32]{1,2,0:T(8,128)(2,1)S(1)}, bf16[1,8192,32]{1,2,0:T(8,128)(2,1)}, u32[]{:S(2)}) copy-start(bf16[1,8192,32]{1,2,0:T(8,128)(2,1)} %param.20) | copy-start | bytes 1572868
  4.4 50.2 %collective-permute-start.1 = (bf16[24,256,128]{2,1,0:T(8,128)(2,1)}, bf16[24,256,128]{2,1,0:T(8,128)(2,1)S(1)}, u32[]{:S(2)}, u32[]{:S(2)}) collective-permute-start(bf16[24,256,128]{2,1,0:T(8,128)(2,1)} %get-tuple-element.19), channel_id=1, source_target_pairs={{0,2},{1,3},{2,0},{3,1},{4,6},{5,7},{6,4},{7,5},{8,10},{9,11},{10,... | collective-permute-start | bytes 4718600 | tf_op jit(solution)/shard_map/ppermute | solution.py:345
  50.2 4.4 %collective-permute-start = (bf16[16,240,128]{2,1,0:T(8,128)(2,1)S(1)}, bf16[16,240,128]{2,1,0:T(8,128)(2,1)S(1)}, u32[]{:S(2)}, u32[]{:S(2)}) collective-permute-start(bf16[16,240,128]{2,1,0:T(8,128)(2,1)S(1)} %bitcast.11), channel_id=1, source_target_pairs={{0,1},{1,0},{2,3},{3,2},{4,5},{5,4},{6,7},{7,6},{8,9},{9,8},{10,11... | collective-permute-start | bytes 2949128 | tf_op jit(solution)/shard_map/ppermute | solution.py:345
  52.2 21.8 %collective-permute-start.5 = (bf16[12,256,128]{2,1,0:T(8,128)(2,1)S(1)}, bf16[12,256,128]{2,1,0:T(8,128)(2,1)S(1)}, u32[]{:S(2)}, u32[]{:S(2)}) collective-permute-start(bf16[12,256,128]{2,1,0:T(8,128)(2,1)S(1)} %shard_map.151), channel_id=1, source_target_pairs={{0,2},{1,3},{2,0},{3,1},{4,6},{5,7},{6,4},{7,5},{8,10},{9,11},{10,... | collective-permute-start | bytes 2359304 | tf_op jit(solution)/shard_map/ppermute | solution.py:345
  54.6 4.5 %copy-start.1 = (bf16[1,8192,128]{2,1,0:T(8,128)(2,1)S(1)}, bf16[1,8192,128]{2,1,0:T(8,128)(2,1)}, u32[]{:S(2)}) copy-start(bf16[1,8192,128]{2,1,0:T(8,128)(2,1)} %weight.3) | copy-start | bytes 6291460
  55.3 3.1 %collective-permute-start.3 = (bf16[64,224]{1,0:T(8,128)(2,1)S(1)}, bf16[64,224]{1,0:T(8,128)(2,1)S(1)}, u32[]{:S(2)}, u32[]{:S(2)}) collective-permute-start(bf16[64,224]{1,0:T(8,128)(2,1)S(1)} %get-tuple-element.24), channel_id=1, source_target_pairs={{0,1},{1,0},{2,3},{3,2},{4,5},{5,4},{6,7},{7,6},{8,9},{9,8},{10,11... | collective-permute-start | bytes 86024 | tf_op jit(solution)/shard_map/ppermute | solution.py:345
  58.5 1.4 %collective-permute-start.4 = (bf16[128,224]{1,0:T(8,128)(2,1)S(1)}, bf16[128,224]{1,0:T(8,128)(2,1)S(1)}, u32[]{:S(2)}, u32[]{:S(2)}) collective-permute-start(bf16[128,224]{1,0:T(8,128)(2,1)S(1)} %pad_maximum_fusion.1), channel_id=1, source_target_pairs={{0,0},{1,5},{2,2},{3,7},{4,8},{5,13},{6,10},{7,15},{8,16},{9,21},{... | collective-permute-start | bytes 172040 | tf_op jit(solution)/shard_map/ppermute | solution.py:345
  59.1 15.7 %copy-start.8 = (f32[64,224]{1,0:T(8,128)S(1)}, f32[64,224]{1,0:T(8,128)}, u32[]{:S(2)}) copy-start(f32[64,224]{1,0:T(8,128)} %constant.8.clone.cos_t) | copy-start | bytes 172036
  59.1 15.7 %copy-start.9 = (f32[64,224]{1,0:T(8,128)S(1)}, f32[64,224]{1,0:T(8,128)}, u32[]{:S(2)}) copy-start(f32[64,224]{1,0:T(8,128)} %constant.9.clone.sin_t) | copy-start | bytes 172036
  59.2 22.4 %copy-start.6 = (f32[224,64]{1,0:T(8,128)S(1)}, f32[224,64]{1,0:T(8,128)}, u32[]{:S(2)}) copy-start(f32[224,64]{1,0:T(8,128)} %constant.10.clone.cos) | copy-start | bytes 172036
  59.2 22.4 %copy-start.7 = (f32[224,64]{1,0:T(8,128)S(1)}, f32[224,64]{1,0:T(8,128)}, u32[]{:S(2)}) copy-start(f32[224,64]{1,0:T(8,128)} %constant.11.clone.sin) | copy-start | bytes 172036
  59.9 14.9 %collective-permute-start.6 = (bf16[144,224]{1,0:T(8,128)(2,1)S(1)}, bf16[144,224]{1,0:T(8,128)(2,1)S(1)}, u32[]{:S(2)}, u32[]{:S(2)}) collective-permute-start(bf16[144,224]{1,0:T(8,128)(2,1)S(1)} %pad_maximum_fusion.near), channel_id=1, source_target_pairs={{0,2},{1,3},{2,0},{3,1},{4,6},{5,7},{6,4},{7,5},{8,10},{9,11},{10,... | collective-permute-start | bytes 193544 | tf_op jit(solution)/shard_map/ppermute | solution.py:345
  63.3 18.2 %collective-permute-start.2 = (bf16[224,128]{1,0:T(8,128)(2,1)S(1)}, bf16[224,128]{1,0:T(8,128)(2,1)S(1)}, u32[]{:S(2)}, u32[]{:S(2)}) collective-permute-start(bf16[224,128]{1,0:T(8,128)(2,1)S(1)} %get-tuple-element.23), channel_id=1, source_target_pairs={{0,2},{1,3},{2,0},{3,1},{4,6},{5,7},{6,4},{7,5},{8,10},{9,11},{10,... | collective-permute-start | bytes 172040 | tf_op jit(solution)/shard_map/ppermute | solution.py:345
  74.9 7.5 %collective-permute-start.7 = (bf16[2,64,224]{2,1,0:T(8,128)(2,1)S(1)}, bf16[2,64,224]{2,1,0:T(8,128)(2,1)S(1)}, u32[]{:S(2)}, u32[]{:S(2)}) collective-permute-start(bf16[2,64,224]{2,1,0:T(8,128)(2,1)S(1)} %get-tuple-element.28.own), channel_id=1, source_target_pairs={{0,1},{1,0},{2,3},{3,2},{4,5},{5,4},{6,7},{7,6},{8,9},{9,8},{10,11... | collective-permute-start | bytes 172040 | tf_op jit(solution)/shard_map/ppermute | solution.py:345
  115.6 4.4 %collective-permute-start.8 = (bf16[16,224,128]{2,1,0:T(8,128)(2,1)S(1)}, bf16[16,224,128]{2,1,0:T(8,128)(2,1)S(1)}, u32[]{:S(2)}, u32[]{:S(2)}) collective-permute-start(bf16[16,224,128]{2,1,0:T(8,128)(2,1)S(1)} %bitcast.17), channel_id=1, source_target_pairs={{0,1},{1,0},{2,3},{3,2},{4,5},{5,4},{6,7},{7,6},{8,9},{9,8},{10,11... | collective-permute-start | bytes 2752520 | tf_op jit(solution)/shard_map/ppermute | solution.py:345
  120.4 6.3 %copy-start.3 = (bf16[1,3,112,128]{3,2,1,0:T(8,128)(2,1)S(1)}, bf16[1,3,112,128]{3,2,1,0:T(8,128)(2,1)}, u32[]{:S(2)}) copy-start(bf16[1,3,112,128]{3,2,1,0:T(8,128)(2,1)} %buffer_out.3) | copy-start | bytes 258052
  120.4 6.2 %copy-start.5 = (bf16[2,112,128]{2,1,0:T(8,128)(2,1)S(1)}, bf16[2,112,128]{2,1,0:T(8,128)(2,1)}, u32[]{:S(2)}) copy-start(bf16[2,112,128]{2,1,0:T(8,128)(2,1)} %get-tuple-element.17.inputs) | copy-start | bytes 172036
  120.4 6.2 %copy-start.10 = (s32[8,2]{0,1:T(2,128)S(1)}, s32[8,2]{0,1:T(2,128)}, u32[]{:S(2)}) copy-start(s32[8,2]{0,1:T(2,128)} %param.15) | copy-start | bytes 196
  120.4 15.3 %copy-start.4 = (bf16[1,3,112,128]{3,2,1,0:T(8,128)(2,1)S(1)}, bf16[1,3,112,128]{3,2,1,0:T(8,128)(2,1)}, u32[]{:S(2)}) copy-start(bf16[1,3,112,128]{3,2,1,0:T(8,128)(2,1)} %buffer_in.3) | copy-start | bytes 258052
  120.4 6.2 %collective-permute-start.9 = (bf16[224,128]{1,0:T(8,128)(2,1)S(1)}, bf16[224,128]{1,0:T(8,128)(2,1)S(1)}, u32[]{:S(2)}, u32[]{:S(2)}) collective-permute-start(bf16[224,128]{1,0:T(8,128)(2,1)S(1)} %shard_map.157), channel_id=1, source_target_pairs={{0,2},{1,3},{2,0},{3,1},{4,6},{5,7},{6,4},{7,5},{8,10},{9,11},{10,... | collective-permute-start | bytes 172040 | tf_op jit(solution)/shard_map/ppermute | solution.py:345
  127.2 8.5 %collective-permute-start.10 = (bf16[2,112,128]{2,1,0:T(8,128)(2,1)S(1)}, bf16[2,112,128]{2,1,0:T(8,128)(2,1)S(1)}, u32[]{:S(2)}, u32[]{:S(2)}) collective-permute-start(bf16[2,112,128]{2,1,0:T(8,128)(2,1)S(1)} %shard_map.158.message), channel_id=1, source_target_pairs={{0,64},{64,128},{128,192},{192,256},{256,320},{320,384},{384,448},... | collective-permute-start | bytes 172040 | tf_op jit(solution)/shard_map/ppermute | solution.py:458

commit v9 on v6

--- a/solution.py
+++ b/solution.py
@@ -155,12 +155,11 @@
     kv_width = weight.shape[1]
     sums = jnp.sum(here[:, ROWS:PAY, :].astype(jnp.float32), axis=0)
     sums += jnp.sum(there[:, ROWS:PAY, :].astype(jnp.float32), axis=0)
-    sums = jnp.concatenate(
-        [sums[s : s + 1, :LEN] + sums[SEQS + s : SEQS + s + 1, :LEN] for s in range(SEQS)], axis=1
-    )
-    high = sums.astype(jnp.bfloat16).astype(jnp.float32)
-    row = lax.broadcasted_iota(jnp.int32, (PAY - ROWS, ROWS), 0)
-    tail = jnp.where(row == 0, high, jnp.where(row == 1, sums - high, 0.0))
+    totals = [sums[s : s + 1, :] + sums[SEQS + s : SEQS + s + 1, :] for s in range(SEQS)]
+    row = lax.broadcasted_iota(jnp.int32, (PAY - ROWS, HEAD), 0)
+    value = jnp.where(row % SEQS == 0, totals[0], totals[1])
+    high = value.astype(jnp.bfloat16).astype(jnp.float32)
+    tail = jnp.where(row < SEQS, high, jnp.where(row < 2 * SEQS, value - high, 0.0))
     sums_out[...] = tail.astype(jnp.bfloat16)
     acc = jnp.zeros((2 * kv_width, ROWS), jnp.float32)
     for z in range(ZN):
@@ -173,7 +172,7 @@
             parts.append(jnp.concatenate([mine, other], axis=0))
         part = jnp.concatenate(parts, axis=1)
         acc += lax.dot_general(part, block, NT, preferred_element_type=jnp.float32)
-    out[...] = acc.astype(jnp.bfloat16)
+    out[...] = jnp.concatenate([acc[:, :LEN], acc[:, LEN:]], axis=0).T.astype(jnp.bfloat16)
 
 
 def both_partials(here, there, weight, received):
@@ -199,18 +198,29 @@
 
 def sum_kernel(near, far, cos_t, sin_t, out, factors_out):
     z_odd, y, core = lax.axis_index("z") % 2, lax.axis_index("y"), lax.axis_index("core")
-    width = (near.shape[0] - (PAY - ROWS)) // 4
-    tail = near[4 * width :, :].astype(jnp.float32) + far[4 * width :, :].astype(jnp.float32)
-    square_sum = tail[0:1, :] + tail[1:2, :]
+    width = HEAD // SEQS // 2
+    tail = near[2 * LEN :, :].astype(jnp.float32) + far[2 * LEN :, :].astype(jnp.float32)
+    square_sum = jnp.concatenate(
+        [tail[s : s + 1, :LEN] + tail[SEQS + s : SEQS + s + 1, :LEN] for s in range(SEQS)], axis=1
+    )
     inverse = lax.rsqrt(square_sum / (ZN * YN * CN * HEAD) + norm_eps)
     factors = jnp.broadcast_to(inverse, (width, ROWS))
     factors_out[...] = jnp.broadcast_to(inverse, (HEAD, ROWS)).T
 
+    def columns(source, kind):
+        start = pl.multiple_of((z_odd ^ kind) * LEN, LEN)
+        turned = source[pl.ds(start, LEN), :].astype(jnp.float32).T
+        both = jnp.concatenate([turned[: HEAD // 2], turned[HEAD // 2 :]], axis=1)
+        return both[:width], both[width:]
+
+    held = {(side, kind): columns(ref, kind) for side, ref in enumerate((near, far)) for kind in range(2)}
+
     def piece(kind, which):
-        plane = z_odd ^ kind
-        a = near[pl.ds(pl.multiple_of((plane * 2 + (which ^ y)) * width, width), width), :]
-        b = far[pl.ds(pl.multiple_of((plane * 2 + 1 - (which ^ y)) * width, width), width), :]
-        return ((a.astype(jnp.float32) + b.astype(jnp.float32)) * factors).astype(jnp.bfloat16)
+        near_own, near_other = held[0, kind]
+        far_own, far_other = held[1, kind]
+        own = which == y
+        total = jnp.where(own, near_own, near_other) + jnp.where(own, far_other, far_own)
+        return (total * factors).astype(jnp.bfloat16)
 
     first, second = piece(0, 0).astype(jnp.float32), piece(0, 1).astype(jnp.float32)
     rows = pl.ds(pl.multiple_of(core * width, width), width)
@@ -413,7 +423,7 @@
 
     keyval, sums = call(
         keyval_kernel,
-        (shape((2 * kv_width, ROWS)), shape((PAY - ROWS, ROWS))),
+        (shape((LEN, HEAD)), shape((PAY - ROWS, HEAD))),
         4,
         partial_flops,
         5 * 10**6,

time: 137 us -> 137 us (level)
  no operation moved by 1% of the time
where the time goes in v9:
time: 137 us; the launch traced here: 136 us
  blocking collectives  75.6 us (55%)
  starting transfers between devices  29.7 us (22%)
  waiting for transfers between devices  19.1 us (14%)
  Pallas kernels  10.7 us (8%)
    all_gather x2, blocking collectives, gather_z(): return lax.all_gather(x, 'z', axis=0)  75.6 us
    ppermute x10, starting transfers between devices, permute(): return lax.ppermute(x, LANES, pairs)  24.5 us
    ppermute x10, waiting for transfers between devices, permute(): return lax.ppermute(x, LANES, pairs)  17.1 us
    ppermute x1, starting transfers between devices, per_device(): lax.ppermute(message, 'section', [(i, i + 1) for i in range(sections - 1)])  5.26 us
    pallas_call x1, Pallas kernels, per_device(): pl.pallas_call(prepare, out_shape=(shape((ZN + ZN * kv_width // HEAD + EA...  3.76 us
  transfers between devices with their start and end apart: 11, of which 6 were waited for; matrix products, arithmetic and copies ran while one was open for 0% of the time, Pallas kernels for 3%

profile of v9, /device:TPU:6, one launch (start us, length us, event | category | flops | bytes accessed | tf_op | source)
XLA Modules:
  0.0 136.2 jit_solution(13833683977887428235)
XLA Ops:
  0.6 3.8 %shard_map.148 = (bf16[24,256,128]{2,1,0:T(8,128)(2,1)}, bf16[240,128]{1,0:T(8,128)(2,1)}, bf16[2,112,128]{2,1,0:T(8,128)(2,1)}) custom-call(s32[2,8]{1,0:T(2,128)} %bitcast.25, s32[1,2,112,128]{3,2,1,0:T(8,128)} %codes.1, s32[1,2,112]{2,1,0:T(2,128)} %exponents.1, bf16[1,3,112,128]{3,2,1,0:T(8,128)(2,1)} %buffer_in.3, bf16[1,128]{1,0:T(2,128)(2,1)} %gain.1, ...), custom_call_target="tpu_custom_call" | custom-call | flops 10000000 | bytes 4000000 | tf_op jit(solution)/shard_map/pallas_call | solution.py:388
  4.4 0.0 copy-start.2
  4.4 3.6 %collective-permute-start.1 = (bf16[24,256,128]{2,1,0:T(8,128)(2,1)}, bf16[24,256,128]{2,1,0:T(8,128)(2,1)S(1)}, u32[]{:S(2)}, u32[]{:S(2)}) collective-permute-start(bf16[24,256,128]{2,1,0:T(8,128)(2,1)} %get-tuple-element.19), channel_id=1, source_target_pairs={{0,2},{1,3},{2,0},{3,1},{4,6},{5,7},{6,4},{7,5},{8,10},{9,11},{10,... | collective-permute-start | bytes 4718600 | tf_op jit(solution)/shard_map/ppermute | solution.py:359
  8.0 42.1 %all-gather = bf16[3840,128]{1,0:T(8,128)(2,1)S(1)} all-gather(bf16[240,128]{1,0:T(8,128)(2,1)} %get-tuple-element.18), channel_id=2, replica_groups=mesh['section'=8,'z'=16,'y'=2,'core'=2] {'z'}, dimensions={0}, use_global_device_ids=true | all-gather | bytes 1044480 | tf_op jit(solution)/shard_map/all_gather | solution.py:371
  50.2 1.9 %collective-permute-start = (bf16[16,240,128]{2,1,0:T(8,128)(2,1)S(1)}, bf16[16,240,128]{2,1,0:T(8,128)(2,1)S(1)}, u32[]{:S(2)}, u32[]{:S(2)}) collective-permute-start(bf16[16,240,128]{2,1,0:T(8,128)(2,1)S(1)} %bitcast.11), channel_id=1, source_target_pairs={{0,1},{1,0},{2,3},{3,2},{4,5},{5,4},{6,7},{7,6},{8,9},{9,8},{10,11... | collective-permute-start | bytes 2949128 | tf_op jit(solution)/shard_map/ppermute | solution.py:359
  52.1 0.1 shard_map.151
  52.2 0.0 copy-start.1
  52.2 2.5 %collective-permute-start.5 = (bf16[12,256,128]{2,1,0:T(8,128)(2,1)S(1)}, bf16[12,256,128]{2,1,0:T(8,128)(2,1)S(1)}, u32[]{:S(2)}, u32[]{:S(2)}) collective-permute-start(bf16[12,256,128]{2,1,0:T(8,128)(2,1)S(1)} %shard_map.151), channel_id=1, source_target_pairs={{0,2},{1,3},{2,0},{3,1},{4,6},{5,7},{6,4},{7,5},{8,10},{9,11},{10,... | collective-permute-start | bytes 2359304 | tf_op jit(solution)/shard_map/ppermute | solution.py:359
  54.7 0.0 collective-permute-done.there
  54.7 0.0 collective-permute-done.1
  54.7 0.8 shard_map.149
  55.6 0.0 copy-start.8
  55.6 0.0 copy-start.9
  55.6 0.0 copy-start.6
  55.6 0.0 copy-start.7
  55.6 2.1 %collective-permute-start.4 = (bf16[112,128]{1,0:T(8,128)(2,1)S(1)}, bf16[112,128]{1,0:T(8,128)(2,1)S(1)}, u32[]{:S(2)}, u32[]{:S(2)}) collective-permute-start(bf16[112,128]{1,0:T(8,128)(2,1)S(1)} %get-tuple-element.20), channel_id=1, source_target_pairs={{0,4},{1,5},{2,6},{3,7},{4,12},{5,13},{6,14},{7,15},{8,20},{9,21},... | collective-permute-start | bytes 86024 | tf_op jit(solution)/shard_map/ppermute | solution.py:359
  57.7 0.7 collective-permute-start.3
  58.4 0.7 shard_map.150
  59.0 12.0 %collective-permute-done.4 = bf16[112,128]{1,0:T(8,128)(2,1)S(1)} collective-permute-done((bf16[112,128]{1,0:T(8,128)(2,1)S(1)}, bf16[112,128]{1,0:T(8,128)(2,1)S(1)}, u32[]{:S(2)}, u32[]{:S(2)}) %collective-permute-start.4) | collective-permute-done | bytes 28704 | tf_op jit(solution)/shard_map/ppermute | solution.py:359
  71.0 0.0 collective-permute-done.3
  71.0 3.5 %collective-permute-start.6 = (bf16[240,128]{1,0:T(8,128)(2,1)S(1)}, bf16[240,128]{1,0:T(8,128)(2,1)S(1)}, u32[]{:S(2)}, u32[]{:S(2)}) collective-permute-start(bf16[240,128]{1,0:T(8,128)(2,1)S(1)} %pad_maximum_fusion.near), channel_id=1, source_target_pairs={{0,2},{1,3},{2,0},{3,1},{4,6},{5,7},{6,4},{7,5},{8,10},{9,11},{10,... | collective-permute-start | bytes 184328 | tf_op jit(solution)/shard_map/ppermute | solution.py:359
  74.5 2.3 %collective-permute-start.2 = (bf16[224,128]{1,0:T(8,128)(2,1)S(1)}, bf16[224,128]{1,0:T(8,128)(2,1)S(1)}, u32[]{:S(2)}, u32[]{:S(2)}) collective-permute-start(bf16[224,128]{1,0:T(8,128)(2,1)S(1)} %get-tuple-element.23), channel_id=1, source_target_pairs={{0,2},{1,3},{2,0},{3,1},{4,6},{5,7},{6,4},{7,5},{8,10},{9,11},{10,... | collective-permute-start | bytes 172040 | tf_op jit(solution)/shard_map/ppermute | solution.py:359
  76.9 0.0 collective-permute-done.5
  76.9 0.2 collective-permute-done.6.far
  77.2 0.4 shard_map.152
  77.6 1.9 %collective-permute-start.7 = (bf16[4,32,224]{2,1,0:T(8,128)(2,1)S(1)}, bf16[4,32,224]{2,1,0:T(8,128)(2,1)S(1)}, u32[]{:S(2)}, u32[]{:S(2)}) collective-permute-start(bf16[4,32,224]{2,1,0:T(8,128)(2,1)S(1)} %get-tuple-element.28.own), channel_id=1, source_target_pairs={{0,1},{1,0},{2,3},{3,2},{4,5},{5,4},{6,7},{7,6},{8,9},{9,8},{10,11... | collective-permute-start | bytes 172040 | tf_op jit(solution)/shard_map/ppermute | solution.py:359
  79.5 1.1 collective-permute-done.2.other
  80.6 0.2 shard_map.153.query
  80.9 0.0 collective-permute-done.7.sibling
  80.9 0.5 shard_map.154
  81.4 33.4 %all-gather.1 = bf16[3584,128]{1,0:T(8,128)(2,1)S(1)} all-gather(bf16[224,128]{1,0:T(8,128)(2,1)S(1)} %shard_map.154), channel_id=3, replica_groups=mesh['section'=8,'z'=16,'y'=2,'core'=2] {'z'}, dimensions={0}, use_global_device_ids=true | all-gather | bytes 974848 | tf_op jit(solution)/shard_map/all_gather | solution.py:371
  114.8 1.9 %collective-permute-start.8 = (bf16[16,224,128]{2,1,0:T(8,128)(2,1)S(1)}, bf16[16,224,128]{2,1,0:T(8,128)(2,1)S(1)}, u32[]{:S(2)}, u32[]{:S(2)}) collective-permute-start(bf16[16,224,128]{2,1,0:T(8,128)(2,1)S(1)} %bitcast.17), channel_id=1, source_target_pairs={{0,1},{1,0},{2,3},{3,2},{4,5},{5,4},{6,7},{7,6},{8,9},{9,8},{10,11... | collective-permute-start | bytes 2752520 | tf_op jit(solution)/shard_map/ppermute | solution.py:359
  116.7 0.4 shard_map.155.acc
  117.2 2.0 %collective-permute-done.8.line = bf16[16,224,128]{2,1,0:T(8,128)(2,1)S(1)} collective-permute-done((bf16[16,224,128]{2,1,0:T(8,128)(2,1)S(1)}, bf16[16,224,128]{2,1,0:T(8,128)(2,1)S(1)}, u32[]{:S(2)}, u32[]{:S(2)}) %collective-permute-start.8) | collective-permute-done | bytes 917536 | tf_op jit(solution)/shard_map/ppermute | solution.py:359
  119.1 0.4 shard_map.157
  119.5 0.0 copy-start.3
  119.6 0.0 copy-start.5
  119.6 0.0 copy-start.10
  119.6 0.0 copy-start.4
  119.6 4.1 %collective-permute-start.9 = (bf16[224,128]{1,0:T(8,128)(2,1)S(1)}, bf16[224,128]{1,0:T(8,128)(2,1)S(1)}, u32[]{:S(2)}, u32[]{:S(2)}) collective-permute-start(bf16[224,128]{1,0:T(8,128)(2,1)S(1)} %shard_map.157), channel_id=1, source_target_pairs={{0,2},{1,3},{2,0},{3,1},{4,6},{5,7},{6,4},{7,5},{8,10},{9,11},{10,... | collective-permute-start | bytes 172040 | tf_op jit(solution)/shard_map/ppermute | solution.py:359
  123.7 0.4 shard_map.156.mine
  124.1 1.8 %collective-permute-done.9.other = bf16[224,128]{1,0:T(8,128)(2,1)S(1)} collective-permute-done((bf16[224,128]{1,0:T(8,128)(2,1)S(1)}, bf16[224,128]{1,0:T(8,128)(2,1)S(1)}, u32[]{:S(2)}, u32[]{:S(2)}) %collective-permute-start.9) | collective-permute-done | bytes 57376 | tf_op jit(solution)/shard_map/ppermute | solution.py:359
  125.9 0.0 copy-done.5
  125.9 0.6 shard_map.158.message
  126.5 5.3 %collective-permute-start.10 = (bf16[2,112,128]{2,1,0:T(8,128)(2,1)S(1)}, bf16[2,112,128]{2,1,0:T(8,128)(2,1)S(1)}, u32[]{:S(2)}, u32[]{:S(2)}) collective-permute-start(bf16[2,112,128]{2,1,0:T(8,128)(2,1)S(1)} %shard_map.158.message), channel_id=1, source_target_pairs={{0,64},{64,128},{128,192},{192,256},{256,320},{320,384},{384,448},... | collective-permute-start | bytes 172040 | tf_op jit(solution)/shard_map/ppermute | solution.py:467
  131.7 1.2 shard_map.160
  133.0 2.0 %collective-permute-done.10.arrived = bf16[2,112,128]{2,1,0:T(8,128)(2,1)S(1)} collective-permute-done((bf16[2,112,128]{2,1,0:T(8,128)(2,1)S(1)}, bf16[2,112,128]{2,1,0:T(8,128)(2,1)S(1)}, u32[]{:S(2)}, u32[]{:S(2)}) %collective-permute-start.10) | collective-permute-done | bytes 57376 | tf_op jit(solution)/shard_map/ppermute | solution.py:467
  135.0 1.3 shard_map.159
  (13 shorter events, 0.0 us)
Async XLA Ops:
  0.6 51.5 %copy-start = (bf16[1,8192,128]{2,1,0:T(8,128)(2,1)S(1)}, bf16[1,8192,128]{2,1,0:T(8,128)(2,1)}, u32[]{:S(2)}) copy-start(bf16[1,8192,128]{2,1,0:T(8,128)(2,1)} %weight.5) | copy-start | bytes 6291460
  4.4 50.3 %copy-start.2 = (bf16[1,8192,32]{1,2,0:T(8,128)(2,1)S(1)}, bf16[1,8192,32]{1,2,0:T(8,128)(2,1)}, u32[]{:S(2)}) copy-start(bf16[1,8192,32]{1,2,0:T(8,128)(2,1)} %param.20) | copy-start | bytes 1572868
  4.4 50.3 %collective-permute-start.1 = (bf16[24,256,128]{2,1,0:T(8,128)(2,1)}, bf16[24,256,128]{2,1,0:T(8,128)(2,1)S(1)}, u32[]{:S(2)}, u32[]{:S(2)}) collective-permute-start(bf16[24,256,128]{2,1,0:T(8,128)(2,1)} %get-tuple-element.19), channel_id=1, source_target_pairs={{0,2},{1,3},{2,0},{3,1},{4,6},{5,7},{6,4},{7,5},{8,10},{9,11},{10,... | collective-permute-start | bytes 4718600 | tf_op jit(solution)/shard_map/ppermute | solution.py:359
  50.2 4.5 %collective-permute-start = (bf16[16,240,128]{2,1,0:T(8,128)(2,1)S(1)}, bf16[16,240,128]{2,1,0:T(8,128)(2,1)S(1)}, u32[]{:S(2)}, u32[]{:S(2)}) collective-permute-start(bf16[16,240,128]{2,1,0:T(8,128)(2,1)S(1)} %bitcast.11), channel_id=1, source_target_pairs={{0,1},{1,0},{2,3},{3,2},{4,5},{5,4},{6,7},{7,6},{8,9},{9,8},{10,11... | collective-permute-start | bytes 2949128 | tf_op jit(solution)/shard_map/ppermute | solution.py:359
  52.2 6.2 %copy-start.1 = (bf16[1,8192,128]{2,1,0:T(8,128)(2,1)S(1)}, bf16[1,8192,128]{2,1,0:T(8,128)(2,1)}, u32[]{:S(2)}) copy-start(bf16[1,8192,128]{2,1,0:T(8,128)(2,1)} %weight.3) | copy-start | bytes 6291460
  52.2 24.7 %collective-permute-start.5 = (bf16[12,256,128]{2,1,0:T(8,128)(2,1)S(1)}, bf16[12,256,128]{2,1,0:T(8,128)(2,1)S(1)}, u32[]{:S(2)}, u32[]{:S(2)}) collective-permute-start(bf16[12,256,128]{2,1,0:T(8,128)(2,1)S(1)} %shard_map.151), channel_id=1, source_target_pairs={{0,2},{1,3},{2,0},{3,1},{4,6},{5,7},{6,4},{7,5},{8,10},{9,11},{10,... | collective-permute-start | bytes 2359304 | tf_op jit(solution)/shard_map/ppermute | solution.py:359
  55.6 21.6 %copy-start.8 = (f32[64,224]{1,0:T(8,128)S(1)}, f32[64,224]{1,0:T(8,128)}, u32[]{:S(2)}) copy-start(f32[64,224]{1,0:T(8,128)} %constant.8.clone.cos_t) | copy-start | bytes 172036
  55.6 21.6 %copy-start.9 = (f32[64,224]{1,0:T(8,128)S(1)}, f32[64,224]{1,0:T(8,128)}, u32[]{:S(2)}) copy-start(f32[64,224]{1,0:T(8,128)} %constant.9.clone.sin_t) | copy-start | bytes 172036
  55.6 25.0 %copy-start.6 = (f32[224,64]{1,0:T(8,128)S(1)}, f32[224,64]{1,0:T(8,128)}, u32[]{:S(2)}) copy-start(f32[224,64]{1,0:T(8,128)} %constant.10.clone.cos) | copy-start | bytes 172036
  55.6 25.0 %copy-start.7 = (f32[224,64]{1,0:T(8,128)S(1)}, f32[224,64]{1,0:T(8,128)}, u32[]{:S(2)}) copy-start(f32[224,64]{1,0:T(8,128)} %constant.11.clone.sin) | copy-start | bytes 172036
  55.6 15.4 %collective-permute-start.4 = (bf16[112,128]{1,0:T(8,128)(2,1)S(1)}, bf16[112,128]{1,0:T(8,128)(2,1)S(1)}, u32[]{:S(2)}, u32[]{:S(2)}) collective-permute-start(bf16[112,128]{1,0:T(8,128)(2,1)S(1)} %get-tuple-element.20), channel_id=1, source_target_pairs={{0,4},{1,5},{2,6},{3,7},{4,12},{5,13},{6,14},{7,15},{8,20},{9,21},... | collective-permute-start | bytes 86024 | tf_op jit(solution)/shard_map/ppermute | solution.py:359
  57.7 13.4 %collective-permute-start.3 = (bf16[112,128]{1,0:T(8,128)(2,1)S(1)}, bf16[112,128]{1,0:T(8,128)(2,1)S(1)}, u32[]{:S(2)}, u32[]{:S(2)}) collective-permute-start(bf16[112,128]{1,0:T(8,128)(2,1)S(1)} %get-tuple-element.20), channel_id=1, source_target_pairs={{0,0},{1,1},{2,2},{3,3},{4,8},{5,9},{6,10},{7,11},{8,16},{9,17},{1... | collective-permute-start | bytes 86024 | tf_op jit(solution)/shard_map/ppermute | solution.py:359
  71.0 6.1 %collective-permute-start.6 = (bf16[240,128]{1,0:T(8,128)(2,1)S(1)}, bf16[240,128]{1,0:T(8,128)(2,1)S(1)}, u32[]{:S(2)}, u32[]{:S(2)}) collective-permute-start(bf16[240,128]{1,0:T(8,128)(2,1)S(1)} %pad_maximum_fusion.near), channel_id=1, source_target_pairs={{0,2},{1,3},{2,0},{3,1},{4,6},{5,7},{6,4},{7,5},{8,10},{9,11},{10,... | collective-permute-start | bytes 184328 | tf_op jit(solution)/shard_map/ppermute | solution.py:359
  74.5 6.1 %collective-permute-start.2 = (bf16[224,128]{1,0:T(8,128)(2,1)S(1)}, bf16[224,128]{1,0:T(8,128)(2,1)S(1)}, u32[]{:S(2)}, u32[]{:S(2)}) collective-permute-start(bf16[224,128]{1,0:T(8,128)(2,1)S(1)} %get-tuple-element.23), channel_id=1, source_target_pairs={{0,2},{1,3},{2,0},{3,1},{4,6},{5,7},{6,4},{7,5},{8,10},{9,11},{10,... | collective-permute-start | bytes 172040 | tf_op jit(solution)/shard_map/ppermute | solution.py:359
  77.6 3.3 %collective-permute-start.7 = (bf16[4,32,224]{2,1,0:T(8,128)(2,1)S(1)}, bf16[4,32,224]{2,1,0:T(8,128)(2,1)S(1)}, u32[]{:S(2)}, u32[]{:S(2)}) collective-permute-start(bf16[4,32,224]{2,1,0:T(8,128)(2,1)S(1)} %get-tuple-element.28.own), channel_id=1, source_target_pairs={{0,1},{1,0},{2,3},{3,2},{4,5},{5,4},{6,7},{7,6},{8,9},{9,8},{10,11... | collective-permute-start | bytes 172040 | tf_op jit(solution)/shard_map/ppermute | solution.py:359
  114.8 4.4 %collective-permute-start.8 = (bf16[16,224,128]{2,1,0:T(8,128)(2,1)S(1)}, bf16[16,224,128]{2,1,0:T(8,128)(2,1)S(1)}, u32[]{:S(2)}, u32[]{:S(2)}) collective-permute-start(bf16[16,224,128]{2,1,0:T(8,128)(2,1)S(1)} %bitcast.17), channel_id=1, source_target_pairs={{0,1},{1,0},{2,3},{3,2},{4,5},{5,4},{6,7},{7,6},{8,9},{9,8},{10,11... | collective-permute-start | bytes 2752520 | tf_op jit(solution)/shard_map/ppermute | solution.py:359
  119.5 6.3 %copy-start.3 = (bf16[1,3,112,128]{3,2,1,0:T(8,128)(2,1)S(1)}, bf16[1,3,112,128]{3,2,1,0:T(8,128)(2,1)}, u32[]{:S(2)}) copy-start(bf16[1,3,112,128]{3,2,1,0:T(8,128)(2,1)} %buffer_out.3) | copy-start | bytes 258052
  119.6 6.3 %copy-start.5 = (bf16[2,112,128]{2,1,0:T(8,128)(2,1)S(1)}, bf16[2,112,128]{2,1,0:T(8,128)(2,1)}, u32[]{:S(2)}) copy-start(bf16[2,112,128]{2,1,0:T(8,128)(2,1)} %get-tuple-element.17.inputs) | copy-start | bytes 172036
  119.6 6.3 %copy-start.10 = (s32[8,2]{0,1:T(2,128)S(1)}, s32[8,2]{0,1:T(2,128)}, u32[]{:S(2)}) copy-start(s32[8,2]{0,1:T(2,128)} %param.15) | copy-start | bytes 196
  119.6 15.4 %copy-start.4 = (bf16[1,3,112,128]{3,2,1,0:T(8,128)(2,1)S(1)}, bf16[1,3,112,128]{3,2,1,0:T(8,128)(2,1)}, u32[]{:S(2)}) copy-start(bf16[1,3,112,128]{3,2,1,0:T(8,128)(2,1)} %buffer_in.3) | copy-start | bytes 258052
  119.6 6.3 %collective-permute-start.9 = (bf16[224,128]{1,0:T(8,128)(2,1)S(1)}, bf16[224,128]{1,0:T(8,128)(2,1)S(1)}, u32[]{:S(2)}, u32[]{:S(2)}) collective-permute-start(bf16[224,128]{1,0:T(8,128)(2,1)S(1)} %shard_map.157), channel_id=1, source_target_pairs={{0,2},{1,3},{2,0},{3,1},{4,6},{5,7},{6,4},{7,5},{8,10},{9,11},{10,... | collective-permute-start | bytes 172040 | tf_op jit(solution)/shard_map/ppermute | solution.py:359
  126.5 8.5 %collective-permute-start.10 = (bf16[2,112,128]{2,1,0:T(8,128)(2,1)S(1)}, bf16[2,112,128]{2,1,0:T(8,128)(2,1)S(1)}, u32[]{:S(2)}, u32[]{:S(2)}) collective-permute-start(bf16[2,112,128]{2,1,0:T(8,128)(2,1)S(1)} %shard_map.158.message), channel_id=1, source_target_pairs={{0,64},{64,128},{128,192},{192,256},{256,320},{320,384},{384,448},... | collective-permute-start | bytes 172040 | tf_op jit(solution)/shard_map/ppermute | solution.py:467

commit v10 on v9

--- a/solution.py
+++ b/solution.py
@@ -68,9 +68,6 @@
         pltpu.make_async_copy(buffer_in.at[0, ids[1, section]], stored_v.at[1], sems.at[4]),
         pltpu.make_async_copy(keyval, keyval_v, sems.at[5]),
     ]
-    for item in copies:
-        item.start()
-
     step = ZN // PIECES
     moves = [
         (query.at[pl.ds(i * step, step), far], half_v.at[i], packed.at[pl.ds(i * step, step)])
@@ -83,6 +80,11 @@
         loads.append(pltpu.make_async_copy(source, between, half_sems.at[0, i]))
         stores.append(pltpu.make_async_copy(between, target, half_sems.at[1, i]))
         loads[-1].start()
+    for item in copies:
+        item.start()
+    for load, store in zip(loads, stores):
+        load.wait()
+        store.start()
     for item in copies[:5]:
         item.wait()
     eye = lax.broadcasted_iota(jnp.int32, (LEN, LEN), 0) == lax.broadcasted_iota(
@@ -119,9 +121,6 @@
     stores.append(pltpu.make_async_copy(inputs_v, inputs_out, sems.at[8]))
     stores[-1].start()
 
-    for load, store in zip(loads, stores):
-        load.wait()
-        store.start()
     copies[5].wait()
     kv_width = keyval.shape[1]
     per_row = CN * HEAD // kv_width

time: 137 us -> 137 us (level)
  no operation moved by 1% of the time
where the time goes in v10:
time: 137 us; the launch traced here: 136 us
  blocking collectives  75.6 us (55%)
  starting transfers between devices  29.7 us (22%)
  waiting for transfers between devices  19.1 us (14%)
  Pallas kernels  10.5 us (8%)
    all_gather x2, blocking collectives, gather_z(): return lax.all_gather(x, 'z', axis=0)  75.6 us
    ppermute x10, starting transfers between devices, permute(): return lax.ppermute(x, LANES, pairs)  24.4 us
    ppermute x10, waiting for transfers between devices, permute(): return lax.ppermute(x, LANES, pairs)  17.1 us
    ppermute x1, starting transfers between devices, per_device(): lax.ppermute(message, 'section', [(i, i + 1) for i in range(sections - 1)])  5.28 us
    pallas_call x1, Pallas kernels, per_device(): pl.pallas_call(prepare, out_shape=(shape((ZN + ZN * kv_width // HEAD + EA...  3.5 us
  transfers between devices with their start and end apart: 11, of which 6 were waited for; matrix products, arithmetic and copies ran while one was open for 0% of the time, Pallas kernels for 3%

profile of v10, /device:TPU:6, one launch (start us, length us, event | category | flops | bytes accessed | tf_op | source)
XLA Modules:
  0.0 135.9 jit_solution(7845749761682629568)
XLA Ops:
  0.6 3.5 %shard_map.148 = (bf16[24,256,128]{2,1,0:T(8,128)(2,1)}, bf16[240,128]{1,0:T(8,128)(2,1)}, bf16[2,112,128]{2,1,0:T(8,128)(2,1)}) custom-call(s32[2,8]{1,0:T(2,128)} %bitcast.25, s32[1,2,112,128]{3,2,1,0:T(8,128)} %codes.1, s32[1,2,112]{2,1,0:T(2,128)} %exponents.1, bf16[1,3,112,128]{3,2,1,0:T(8,128)(2,1)} %buffer_in.3, bf16[1,128]{1,0:T(2,128)(2,1)} %gain.1, ...), custom_call_target="tpu_custom_call" | custom-call | flops 10000000 | bytes 4000000 | tf_op jit(solution)/shard_map/pallas_call | solution.py:387
  4.1 0.0 copy-start.2
  4.2 3.6 %collective-permute-start.1 = (bf16[24,256,128]{2,1,0:T(8,128)(2,1)}, bf16[24,256,128]{2,1,0:T(8,128)(2,1)S(1)}, u32[]{:S(2)}, u32[]{:S(2)}) collective-permute-start(bf16[24,256,128]{2,1,0:T(8,128)(2,1)} %get-tuple-element.19), channel_id=1, source_target_pairs={{0,2},{1,3},{2,0},{3,1},{4,6},{5,7},{6,4},{7,5},{8,10},{9,11},{10,... | collective-permute-start | bytes 4718600 | tf_op jit(solution)/shard_map/ppermute | solution.py:358
  7.8 42.1 %all-gather = bf16[3840,128]{1,0:T(8,128)(2,1)S(1)} all-gather(bf16[240,128]{1,0:T(8,128)(2,1)} %get-tuple-element.18), channel_id=2, replica_groups=mesh['section'=8,'z'=16,'y'=2,'core'=2] {'z'}, dimensions={0}, use_global_device_ids=true | all-gather | bytes 1044480 | tf_op jit(solution)/shard_map/all_gather | solution.py:370
  49.9 1.9 %collective-permute-start = (bf16[16,240,128]{2,1,0:T(8,128)(2,1)S(1)}, bf16[16,240,128]{2,1,0:T(8,128)(2,1)S(1)}, u32[]{:S(2)}, u32[]{:S(2)}) collective-permute-start(bf16[16,240,128]{2,1,0:T(8,128)(2,1)S(1)} %bitcast.11), channel_id=1, source_target_pairs={{0,1},{1,0},{2,3},{3,2},{4,5},{5,4},{6,7},{7,6},{8,9},{9,8},{10,11... | collective-permute-start | bytes 2949128 | tf_op jit(solution)/shard_map/ppermute | solution.py:358
  51.9 0.1 shard_map.151
  51.9 0.0 copy-start.1
  51.9 2.5 %collective-permute-start.5 = (bf16[12,256,128]{2,1,0:T(8,128)(2,1)S(1)}, bf16[12,256,128]{2,1,0:T(8,128)(2,1)S(1)}, u32[]{:S(2)}, u32[]{:S(2)}) collective-permute-start(bf16[12,256,128]{2,1,0:T(8,128)(2,1)S(1)} %shard_map.151), channel_id=1, source_target_pairs={{0,2},{1,3},{2,0},{3,1},{4,6},{5,7},{6,4},{7,5},{8,10},{9,11},{10,... | collective-permute-start | bytes 2359304 | tf_op jit(solution)/shard_map/ppermute | solution.py:358
  54.4 0.0 collective-permute-done.there
  54.4 0.0 collective-permute-done.1
  54.5 0.8 shard_map.149
  55.3 0.0 copy-start.8
  55.3 0.0 copy-start.9
  55.3 0.0 copy-start.6
  55.3 0.0 copy-start.7
  55.3 2.1 %collective-permute-start.4 = (bf16[112,128]{1,0:T(8,128)(2,1)S(1)}, bf16[112,128]{1,0:T(8,128)(2,1)S(1)}, u32[]{:S(2)}, u32[]{:S(2)}) collective-permute-start(bf16[112,128]{1,0:T(8,128)(2,1)S(1)} %get-tuple-element.20), channel_id=1, source_target_pairs={{0,4},{1,5},{2,6},{3,7},{4,12},{5,13},{6,14},{7,15},{8,20},{9,21},... | collective-permute-start | bytes 86024 | tf_op jit(solution)/shard_map/ppermute | solution.py:358
  57.4 0.7 collective-permute-start.3
  58.1 0.7 shard_map.150
  58.8 12.0 %collective-permute-done.4 = bf16[112,128]{1,0:T(8,128)(2,1)S(1)} collective-permute-done((bf16[112,128]{1,0:T(8,128)(2,1)S(1)}, bf16[112,128]{1,0:T(8,128)(2,1)S(1)}, u32[]{:S(2)}, u32[]{:S(2)}) %collective-permute-start.4) | collective-permute-done | bytes 28704 | tf_op jit(solution)/shard_map/ppermute | solution.py:358
  70.8 0.0 collective-permute-done.3
  70.8 3.5 %collective-permute-start.6 = (bf16[240,128]{1,0:T(8,128)(2,1)S(1)}, bf16[240,128]{1,0:T(8,128)(2,1)S(1)}, u32[]{:S(2)}, u32[]{:S(2)}) collective-permute-start(bf16[240,128]{1,0:T(8,128)(2,1)S(1)} %pad_maximum_fusion.near), channel_id=1, source_target_pairs={{0,2},{1,3},{2,0},{3,1},{4,6},{5,7},{6,4},{7,5},{8,10},{9,11},{10,... | collective-permute-start | bytes 184328 | tf_op jit(solution)/shard_map/ppermute | solution.py:358
  74.3 2.4 %collective-permute-start.2 = (bf16[224,128]{1,0:T(8,128)(2,1)S(1)}, bf16[224,128]{1,0:T(8,128)(2,1)S(1)}, u32[]{:S(2)}, u32[]{:S(2)}) collective-permute-start(bf16[224,128]{1,0:T(8,128)(2,1)S(1)} %get-tuple-element.23), channel_id=1, source_target_pairs={{0,2},{1,3},{2,0},{3,1},{4,6},{5,7},{6,4},{7,5},{8,10},{9,11},{10,... | collective-permute-start | bytes 172040 | tf_op jit(solution)/shard_map/ppermute | solution.py:358
  76.6 0.0 collective-permute-done.5
  76.6 0.2 collective-permute-done.6.far
  76.9 0.4 shard_map.152
  77.3 1.9 %collective-permute-start.7 = (bf16[4,32,224]{2,1,0:T(8,128)(2,1)S(1)}, bf16[4,32,224]{2,1,0:T(8,128)(2,1)S(1)}, u32[]{:S(2)}, u32[]{:S(2)}) collective-permute-start(bf16[4,32,224]{2,1,0:T(8,128)(2,1)S(1)} %get-tuple-element.28.own), channel_id=1, source_target_pairs={{0,1},{1,0},{2,3},{3,2},{4,5},{5,4},{6,7},{7,6},{8,9},{9,8},{10,11... | collective-permute-start | bytes 172040 | tf_op jit(solution)/shard_map/ppermute | solution.py:358
  79.2 1.1 collective-permute-done.2.other
  80.3 0.2 shard_map.153.query
  80.6 0.0 collective-permute-done.7.sibling
  80.6 0.5 shard_map.154
  81.1 33.5 %all-gather.1 = bf16[3584,128]{1,0:T(8,128)(2,1)S(1)} all-gather(bf16[224,128]{1,0:T(8,128)(2,1)S(1)} %shard_map.154), channel_id=3, replica_groups=mesh['section'=8,'z'=16,'y'=2,'core'=2] {'z'}, dimensions={0}, use_global_device_ids=true | all-gather | bytes 974848 | tf_op jit(solution)/shard_map/all_gather | solution.py:370
  114.5 1.9 %collective-permute-start.8 = (bf16[16,224,128]{2,1,0:T(8,128)(2,1)S(1)}, bf16[16,224,128]{2,1,0:T(8,128)(2,1)S(1)}, u32[]{:S(2)}, u32[]{:S(2)}) collective-permute-start(bf16[16,224,128]{2,1,0:T(8,128)(2,1)S(1)} %bitcast.17), channel_id=1, source_target_pairs={{0,1},{1,0},{2,3},{3,2},{4,5},{5,4},{6,7},{7,6},{8,9},{9,8},{10,11... | collective-permute-start | bytes 2752520 | tf_op jit(solution)/shard_map/ppermute | solution.py:358
  116.5 0.4 shard_map.155.acc
  116.9 2.0 %collective-permute-done.8.line = bf16[16,224,128]{2,1,0:T(8,128)(2,1)S(1)} collective-permute-done((bf16[16,224,128]{2,1,0:T(8,128)(2,1)S(1)}, bf16[16,224,128]{2,1,0:T(8,128)(2,1)S(1)}, u32[]{:S(2)}, u32[]{:S(2)}) %collective-permute-start.8) | collective-permute-done | bytes 917536 | tf_op jit(solution)/shard_map/ppermute | solution.py:358
  118.9 0.4 shard_map.157
  119.3 0.0 copy-start.3
  119.3 0.0 copy-start.5
  119.3 0.0 copy-start.10
  119.3 0.0 copy-start.4
  119.3 4.0 %collective-permute-start.9 = (bf16[224,128]{1,0:T(8,128)(2,1)S(1)}, bf16[224,128]{1,0:T(8,128)(2,1)S(1)}, u32[]{:S(2)}, u32[]{:S(2)}) collective-permute-start(bf16[224,128]{1,0:T(8,128)(2,1)S(1)} %shard_map.157), channel_id=1, source_target_pairs={{0,2},{1,3},{2,0},{3,1},{4,6},{5,7},{6,4},{7,5},{8,10},{9,11},{10,... | collective-permute-start | bytes 172040 | tf_op jit(solution)/shard_map/ppermute | solution.py:358
  123.4 0.4 shard_map.156.mine
  123.8 1.8 %collective-permute-done.9.other = bf16[224,128]{1,0:T(8,128)(2,1)S(1)} collective-permute-done((bf16[224,128]{1,0:T(8,128)(2,1)S(1)}, bf16[224,128]{1,0:T(8,128)(2,1)S(1)}, u32[]{:S(2)}, u32[]{:S(2)}) %collective-permute-start.9) | collective-permute-done | bytes 57376 | tf_op jit(solution)/shard_map/ppermute | solution.py:358
  125.6 0.0 copy-done.10
  125.6 0.6 shard_map.158.message
  126.2 5.3 %collective-permute-start.10 = (bf16[2,112,128]{2,1,0:T(8,128)(2,1)S(1)}, bf16[2,112,128]{2,1,0:T(8,128)(2,1)S(1)}, u32[]{:S(2)}, u32[]{:S(2)}) collective-permute-start(bf16[2,112,128]{2,1,0:T(8,128)(2,1)S(1)} %shard_map.158.message), channel_id=1, source_target_pairs={{0,64},{64,128},{128,192},{192,256},{256,320},{320,384},{384,448},... | collective-permute-start | bytes 172040 | tf_op jit(solution)/shard_map/ppermute | solution.py:466
  131.5 1.2 shard_map.160
  132.7 2.0 %collective-permute-done.10.arrived = bf16[2,112,128]{2,1,0:T(8,128)(2,1)S(1)} collective-permute-done((bf16[2,112,128]{2,1,0:T(8,128)(2,1)S(1)}, bf16[2,112,128]{2,1,0:T(8,128)(2,1)S(1)}, u32[]{:S(2)}, u32[]{:S(2)}) %collective-permute-start.10) | collective-permute-done | bytes 57376 | tf_op jit(solution)/shard_map/ppermute | solution.py:466
  134.7 1.3 shard_map.159
  (13 shorter events, 0.0 us)
Async XLA Ops:
  0.6 51.2 %copy-start = (bf16[1,8192,128]{2,1,0:T(8,128)(2,1)S(1)}, bf16[1,8192,128]{2,1,0:T(8,128)(2,1)}, u32[]{:S(2)}) copy-start(bf16[1,8192,128]{2,1,0:T(8,128)(2,1)} %weight.5) | copy-start | bytes 6291460
  4.1 50.3 %copy-start.2 = (bf16[1,8192,32]{1,2,0:T(8,128)(2,1)S(1)}, bf16[1,8192,32]{1,2,0:T(8,128)(2,1)}, u32[]{:S(2)}) copy-start(bf16[1,8192,32]{1,2,0:T(8,128)(2,1)} %param.20) | copy-start | bytes 1572868
  4.2 50.3 %collective-permute-start.1 = (bf16[24,256,128]{2,1,0:T(8,128)(2,1)}, bf16[24,256,128]{2,1,0:T(8,128)(2,1)S(1)}, u32[]{:S(2)}, u32[]{:S(2)}) collective-permute-start(bf16[24,256,128]{2,1,0:T(8,128)(2,1)} %get-tuple-element.19), channel_id=1, source_target_pairs={{0,2},{1,3},{2,0},{3,1},{4,6},{5,7},{6,4},{7,5},{8,10},{9,11},{10,... | collective-permute-start | bytes 4718600 | tf_op jit(solution)/shard_map/ppermute | solution.py:358
  49.9 4.5 %collective-permute-start = (bf16[16,240,128]{2,1,0:T(8,128)(2,1)S(1)}, bf16[16,240,128]{2,1,0:T(8,128)(2,1)S(1)}, u32[]{:S(2)}, u32[]{:S(2)}) collective-permute-start(bf16[16,240,128]{2,1,0:T(8,128)(2,1)S(1)} %bitcast.11), channel_id=1, source_target_pairs={{0,1},{1,0},{2,3},{3,2},{4,5},{5,4},{6,7},{7,6},{8,9},{9,8},{10,11... | collective-permute-start | bytes 2949128 | tf_op jit(solution)/shard_map/ppermute | solution.py:358
  51.9 6.2 %copy-start.1 = (bf16[1,8192,128]{2,1,0:T(8,128)(2,1)S(1)}, bf16[1,8192,128]{2,1,0:T(8,128)(2,1)}, u32[]{:S(2)}) copy-start(bf16[1,8192,128]{2,1,0:T(8,128)(2,1)} %weight.3) | copy-start | bytes 6291460
  51.9 24.7 %collective-permute-start.5 = (bf16[12,256,128]{2,1,0:T(8,128)(2,1)S(1)}, bf16[12,256,128]{2,1,0:T(8,128)(2,1)S(1)}, u32[]{:S(2)}, u32[]{:S(2)}) collective-permute-start(bf16[12,256,128]{2,1,0:T(8,128)(2,1)S(1)} %shard_map.151), channel_id=1, source_target_pairs={{0,2},{1,3},{2,0},{3,1},{4,6},{5,7},{6,4},{7,5},{8,10},{9,11},{10,... | collective-permute-start | bytes 2359304 | tf_op jit(solution)/shard_map/ppermute | solution.py:358
  55.3 21.6 %copy-start.8 = (f32[64,224]{1,0:T(8,128)S(1)}, f32[64,224]{1,0:T(8,128)}, u32[]{:S(2)}) copy-start(f32[64,224]{1,0:T(8,128)} %constant.8.clone.cos_t) | copy-start | bytes 172036
  55.3 21.6 %copy-start.9 = (f32[64,224]{1,0:T(8,128)S(1)}, f32[64,224]{1,0:T(8,128)}, u32[]{:S(2)}) copy-start(f32[64,224]{1,0:T(8,128)} %constant.9.clone.sin_t) | copy-start | bytes 172036
  55.3 25.0 %copy-start.6 = (f32[224,64]{1,0:T(8,128)S(1)}, f32[224,64]{1,0:T(8,128)}, u32[]{:S(2)}) copy-start(f32[224,64]{1,0:T(8,128)} %constant.10.clone.cos) | copy-start | bytes 172036
  55.3 25.0 %copy-start.7 = (f32[224,64]{1,0:T(8,128)S(1)}, f32[224,64]{1,0:T(8,128)}, u32[]{:S(2)}) copy-start(f32[224,64]{1,0:T(8,128)} %constant.11.clone.sin) | copy-start | bytes 172036
  55.3 15.4 %collective-permute-start.4 = (bf16[112,128]{1,0:T(8,128)(2,1)S(1)}, bf16[112,128]{1,0:T(8,128)(2,1)S(1)}, u32[]{:S(2)}, u32[]{:S(2)}) collective-permute-start(bf16[112,128]{1,0:T(8,128)(2,1)S(1)} %get-tuple-element.20), channel_id=1, source_target_pairs={{0,4},{1,5},{2,6},{3,7},{4,12},{5,13},{6,14},{7,15},{8,20},{9,21},... | collective-permute-start | bytes 86024 | tf_op jit(solution)/shard_map/ppermute | solution.py:358
  57.4 13.4 %collective-permute-start.3 = (bf16[112,128]{1,0:T(8,128)(2,1)S(1)}, bf16[112,128]{1,0:T(8,128)(2,1)S(1)}, u32[]{:S(2)}, u32[]{:S(2)}) collective-permute-start(bf16[112,128]{1,0:T(8,128)(2,1)S(1)} %get-tuple-element.20), channel_id=1, source_target_pairs={{0,0},{1,1},{2,2},{3,3},{4,8},{5,9},{6,10},{7,11},{8,16},{9,17},{1... | collective-permute-start | bytes 86024 | tf_op jit(solution)/shard_map/ppermute | solution.py:358
  70.8 6.1 %collective-permute-start.6 = (bf16[240,128]{1,0:T(8,128)(2,1)S(1)}, bf16[240,128]{1,0:T(8,128)(2,1)S(1)}, u32[]{:S(2)}, u32[]{:S(2)}) collective-permute-start(bf16[240,128]{1,0:T(8,128)(2,1)S(1)} %pad_maximum_fusion.near), channel_id=1, source_target_pairs={{0,2},{1,3},{2,0},{3,1},{4,6},{5,7},{6,4},{7,5},{8,10},{9,11},{10,... | collective-permute-start | bytes 184328 | tf_op jit(solution)/shard_map/ppermute | solution.py:358
  74.3 6.1 %collective-permute-start.2 = (bf16[224,128]{1,0:T(8,128)(2,1)S(1)}, bf16[224,128]{1,0:T(8,128)(2,1)S(1)}, u32[]{:S(2)}, u32[]{:S(2)}) collective-permute-start(bf16[224,128]{1,0:T(8,128)(2,1)S(1)} %get-tuple-element.23), channel_id=1, source_target_pairs={{0,2},{1,3},{2,0},{3,1},{4,6},{5,7},{6,4},{7,5},{8,10},{9,11},{10,... | collective-permute-start | bytes 172040 | tf_op jit(solution)/shard_map/ppermute | solution.py:358
  77.3 3.3 %collective-permute-start.7 = (bf16[4,32,224]{2,1,0:T(8,128)(2,1)S(1)}, bf16[4,32,224]{2,1,0:T(8,128)(2,1)S(1)}, u32[]{:S(2)}, u32[]{:S(2)}) collective-permute-start(bf16[4,32,224]{2,1,0:T(8,128)(2,1)S(1)} %get-tuple-element.28.own), channel_id=1, source_target_pairs={{0,1},{1,0},{2,3},{3,2},{4,5},{5,4},{6,7},{7,6},{8,9},{9,8},{10,11... | collective-permute-start | bytes 172040 | tf_op jit(solution)/shard_map/ppermute | solution.py:358
  114.5 4.4 %collective-permute-start.8 = (bf16[16,224,128]{2,1,0:T(8,128)(2,1)S(1)}, bf16[16,224,128]{2,1,0:T(8,128)(2,1)S(1)}, u32[]{:S(2)}, u32[]{:S(2)}) collective-permute-start(bf16[16,224,128]{2,1,0:T(8,128)(2,1)S(1)} %bitcast.17), channel_id=1, source_target_pairs={{0,1},{1,0},{2,3},{3,2},{4,5},{5,4},{6,7},{7,6},{8,9},{9,8},{10,11... | collective-permute-start | bytes 2752520 | tf_op jit(solution)/shard_map/ppermute | solution.py:358
  119.3 6.3 %copy-start.3 = (bf16[1,3,112,128]{3,2,1,0:T(8,128)(2,1)S(1)}, bf16[1,3,112,128]{3,2,1,0:T(8,128)(2,1)}, u32[]{:S(2)}) copy-start(bf16[1,3,112,128]{3,2,1,0:T(8,128)(2,1)} %buffer_out.3) | copy-start | bytes 258052
  119.3 6.3 %copy-start.5 = (bf16[2,112,128]{2,1,0:T(8,128)(2,1)S(1)}, bf16[2,112,128]{2,1,0:T(8,128)(2,1)}, u32[]{:S(2)}) copy-start(bf16[2,112,128]{2,1,0:T(8,128)(2,1)} %get-tuple-element.17.inputs) | copy-start | bytes 172036
  119.3 6.3 %copy-start.10 = (s32[8,2]{0,1:T(2,128)S(1)}, s32[8,2]{0,1:T(2,128)}, u32[]{:S(2)}) copy-start(s32[8,2]{0,1:T(2,128)} %param.15) | copy-start | bytes 196
  119.3 15.3 %copy-start.4 = (bf16[1,3,112,128]{3,2,1,0:T(8,128)(2,1)S(1)}, bf16[1,3,112,128]{3,2,1,0:T(8,128)(2,1)}, u32[]{:S(2)}) copy-start(bf16[1,3,112,128]{3,2,1,0:T(8,128)(2,1)} %buffer_in.3) | copy-start | bytes 258052
  119.3 6.3 %collective-permute-start.9 = (bf16[224,128]{1,0:T(8,128)(2,1)S(1)}, bf16[224,128]{1,0:T(8,128)(2,1)S(1)}, u32[]{:S(2)}, u32[]{:S(2)}) collective-permute-start(bf16[224,128]{1,0:T(8,128)(2,1)S(1)} %shard_map.157), channel_id=1, source_target_pairs={{0,2},{1,3},{2,0},{3,1},{4,6},{5,7},{6,4},{7,5},{8,10},{9,11},{10,... | collective-permute-start | bytes 172040 | tf_op jit(solution)/shard_map/ppermute | solution.py:358
  126.2 8.5 %collective-permute-start.10 = (bf16[2,112,128]{2,1,0:T(8,128)(2,1)S(1)}, bf16[2,112,128]{2,1,0:T(8,128)(2,1)S(1)}, u32[]{:S(2)}, u32[]{:S(2)}) collective-permute-start(bf16[2,112,128]{2,1,0:T(8,128)(2,1)S(1)} %shard_map.158.message), channel_id=1, source_target_pairs={{0,64},{64,128},{128,192},{192,256},{256,320},{320,384},{384,448},... | collective-permute-start | bytes 172040 | tf_op jit(solution)/shard_map/ppermute | solution.py:466
